TPU v7x, 32 devices: a whole 2x2x4 slice. The times are simulated.
32 devices in a mesh: video: 2 (over y), space: 4 (over z), tm: 4 (over x, core).
Axes of the slice: x: 2, y: 2, z: 4, core: 2. Of those that a mesh axis runs over, the one named last changes fastest.
Arguments:
- spatial_q: bfloat16 [16, 16, 16, 1152], P(('video', 'tm'), 'space'), parts along dimension 0, may hold values from -17 to 17
- spatial_k: bfloat16 [16, 16, 16, 1152], P(('video', 'tm'), 'space'), parts along dimension 0, may hold values from -17 to 17
- spatial_v: bfloat16 [16, 16, 16, 1152], P(('video', 'tm'), 'space'), parts along dimension 0, may hold values from -6 to 6
- temporal_q: bfloat16 [16, 16, 16, 1152], P(('video', 'tm'), 'space'), parts along dimension 0, may hold values from -17 to 17
- temporal_k: bfloat16 [16, 16, 16, 1152], P(('video', 'tm'), 'space'), parts along dimension 0, may hold values from -17 to 17
- temporal_v: bfloat16 [16, 16, 16, 1152], P(('video', 'tm'), 'space'), parts along dimension 0, may hold values from -6 to 6
- key_lists: int32 [16, 8], replicated, may hold values from -1 to 15, as said below
Outputs:
- spatial_out: bfloat16 [16, 16, 16, 1152], P(('video', 'tm'), 'space'), parts along dimension 0
- temporal_out: bfloat16 [16, 16, 16, 1152], P(('video', 'tm'), 'space'), parts along dimension 0
There are 2 independent parts, one for each index of `video`. A program takes and returns all parts, laid end to end along the dimension named above; an argument that names none is the same for every part. Nothing has to cross between parts.
Inputs may be any that keep to these rules, and one draw needn't show every extreme that they name: key_lists[r] names distinct tile rows within 4 rows of r, r itself first; the named entries come first and the rest are -1.
All inputs are finite; a program needn't handle non-finite values.
Results may differ from a plain program's by a relative error of at most 0.0037.
Values may be sent and summed in bfloat16 or wider, within the bound.
No kernel may reach another device: no remote copies, remote signals or barrier semaphores. Data moves between devices by JAX's collectives and lax.ppermute only.
A program may use at most 64 MiB of HBM per device.

v0:
```python
import jax
import jax.numpy as jnp
from jax import lax
from jax.sharding import PartitionSpec as P

HEADS = 16
HEAD_DIM = 72


big_negative = -1e30


def passed_along(value, axis, by):
    length = lax.axis_size(axis)
    pairs = [(i, i + by) for i in range(length) if 0 <= i + by < length]
    return lax.ppermute(value, axis, pairs)


def temporal_attend(operands):
    queries, keyset, values = operands
    outer = queries.shape
    frames = outer[0]
    channels = outer[-1]
    groups = channels // HEAD_DIM
    queries = queries.reshape(frames, -1, groups, HEAD_DIM)
    keyset = keyset.reshape(frames, -1, groups, HEAD_DIM)
    values = values.reshape(frames, -1, groups, HEAD_DIM)
    scores = jnp.einsum(
        "fnhd,enhd->nhfe", queries, keyset, preferred_element_type=jnp.float32
    ) * HEAD_DIM ** (-0.5)
    highest = jnp.max(scores, axis=-1, keepdims=True)
    weights = jnp.exp(scores - highest)
    totals = jnp.sum(weights, axis=-1)
    blended = jnp.einsum(
        "nhfe,enhd->fnhd", weights.astype(jnp.bfloat16), values, preferred_element_type=jnp.float32
    )
    blended = blended / jnp.transpose(totals, (2, 0, 1))[:, :, :, None]
    return blended.astype(jnp.bfloat16).reshape(outer)


def on_device(spatial_q, spatial_k, spatial_v, temporal_q, temporal_k, temporal_v, key_lists):
    frames, rows_dev, columns, channels = spatial_q.shape
    space_count = lax.axis_size("space")
    reach = min(5, (space_count - 1) // 2)
    radius = reach * rows_dev
    scale = HEAD_DIM ** (-0.5)
    row_start = lax.axis_index("space") * rows_dev
    own_lists = lax.dynamic_slice_in_dim(key_lists, row_start, rows_dev, 0)
    stacked = jnp.stack([spatial_k, spatial_v])
    below_list = []
    above_list = []
    for distance in range(1, reach + 1):
        below_list.append(passed_along(stacked, "space", distance))
        above_list.append(passed_along(stacked, "space", -distance))
    window = jnp.concatenate(below_list[::-1] + [stacked] + above_list, axis=2)
    extent = window.shape[2]
    window_rows = row_start - radius + jnp.arange(extent, dtype=jnp.int32)
    member = (
        jnp.any(own_lists[:, :, None] == window_rows[None, None, :], axis=1)
        & (window_rows >= 0)[None, :]
    )
    allowed = jnp.repeat(member, columns, axis=1)[:, None, None, :]

    def frame_window(frame_index):
        queries = spatial_q[frame_index].reshape(rows_dev, columns, HEADS, HEAD_DIM)
        keyset = window[0, frame_index].reshape(extent * columns, HEADS, HEAD_DIM)
        values = window[1, frame_index].reshape(extent * columns, HEADS, HEAD_DIM)
        scores = (
            jnp.einsum("rchd,khd->rhck", queries, keyset, preferred_element_type=jnp.float32)
            * scale
        )
        highest = jnp.max(jnp.where(allowed, scores, big_negative), axis=-1, keepdims=True)
        weights = jnp.where(allowed, jnp.exp(scores - highest), 0.0)
        totals = jnp.sum(weights, axis=-1)
        blended = jnp.einsum(
            "rhck,khd->rchd",
            weights.astype(jnp.bfloat16),
            values,
            preferred_element_type=jnp.float32,
        )
        blended = blended / jnp.transpose(totals, (0, 2, 1))[:, :, :, None]
        return blended.reshape(rows_dev, columns, channels).astype(jnp.bfloat16)

    spatial_out = lax.map(frame_window, jnp.arange(frames, dtype=jnp.int32))
    tm_count = lax.axis_size("tm")
    share = rows_dev * columns // tm_count
    grid_q = temporal_q.reshape(frames, tm_count, share, channels)
    grid_k = temporal_k.reshape(frames, tm_count, share, channels)
    grid_v = temporal_v.reshape(frames, tm_count, share, channels)
    attended = temporal_attend(
        (
            lax.all_to_all(grid_q, "tm", split_axis=1, concat_axis=0, tiled=True),
            lax.all_to_all(grid_k, "tm", split_axis=1, concat_axis=0, tiled=True),
            lax.all_to_all(grid_v, "tm", split_axis=1, concat_axis=0, tiled=True),
        )
    )
    temporal_out = lax.all_to_all(attended, "tm", split_axis=0, concat_axis=1, tiled=True)
    temporal_out = temporal_out.reshape(frames, rows_dev, columns, channels)
    return (spatial_out, temporal_out)


def solution(mesh):
    placed = (
        P(("video", "tm"), "space", None, None),
        P(("video", "tm"), "space", None, None),
        P(("video", "tm"), "space", None, None),
        P(("video", "tm"), "space", None, None),
        P(("video", "tm"), "space", None, None),
        P(("video", "tm"), "space", None, None),
        P(),
    )
    return jax.shard_map(
        on_device,
        mesh=mesh,
        in_specs=placed,
        out_specs=(
            P(("video", "tm"), "space", None, None),
            P(("video", "tm"), "space", None, None),
        ),
        check_vma=False,
    )
```

profile of v0, /device:TPU:0, one launch (start us, length us, event | category | flops | bytes accessed | tf_op | source)
XLA Modules:
  0.0 75.9 jit_solution(447818133705378317)
XLA Ops:
  0.7 2.0 %pad_maximum_fusion.1 = bf16[2,2,4,16,1152]{4,3,2,1,0:T(8,128)(2,1)} fusion(bf16[1,2,4,16,1152]{4,3,2,1,0:T(8,128)(2,1)} %bitcast.94, bf16[1,2,4,16,1152]{4,3,2,1,0:T(8,128)(2,1)} %bitcast.96), kind=kLoop, calls=%fused_computation.37 | loop fusion | flops 294912 | bytes 1179648 | tf_op jit(solution)/shard_map/stack | solution.py:49
  2.7 5.0 %collective-permute-start = (bf16[2,2,4,16,1152]{4,3,2,1,0:T(8,128)(2,1)}, bf16[2,2,4,16,1152]{4,3,2,1,0:T(8,128)(2,1)S(1)}, u32[]{:S(2)}, u32[]{:S(2)}) collective-permute-start(bf16[2,2,4,16,1152]{4,3,2,1,0:T(8,128)(2,1)} %pad_maximum_fusion.1), channel_id=1, source_target_pairs={{0,4},{4,8},{8,12},{1,5},{5,9},{9,13},{2,6},{6,10},{10,14},{3,7},{... | collective-permute-start | bytes 1769480 | tf_op jit(solution)/shard_map/ppermute | solution.py:16
  7.6 1.3 %collective-permute-start.1 = (bf16[2,2,4,16,1152]{4,3,2,1,0:T(8,128)(2,1)}, bf16[2,2,4,16,1152]{4,3,2,1,0:T(8,128)(2,1)}, u32[]{:S(2)}, u32[]{:S(2)}) collective-permute-start(bf16[2,2,4,16,1152]{4,3,2,1,0:T(8,128)(2,1)} %pad_maximum_fusion.1), channel_id=1, source_target_pairs={{4,0},{8,4},{12,8},{5,1},{9,5},{13,9},{6,2},{10,6},{14,10},{7,3},{... | collective-permute-start | bytes 1769480 | tf_op jit(solution)/shard_map/ppermute | solution.py:16
  8.9 1.7 %copy.47 = bf16[2,4,16,1152]{3,2,0,1:T(8,128)(2,1)} copy(bf16[2,4,16,1152]{3,2,1,0:T(8,128)(2,1)} %param.12) | data formatting | bytes 589824 | tf_op args[3]
  10.6 3.5 %all-to-all-start = ((bf16[2,4,16,1152]{3,2,0,1:T(8,128)(2,1)}), bf16[2,4,16,1152]{3,2,0,1:T(8,128)(2,1)S(1)}, u32[]{:S(2)}, u32[]{:S(2)}) async-start(bf16[2,4,16,1152]{3,2,0,1:T(8,128)(2,1)} %copy.47), calls=%async_computation | async-start | bytes 589824 | tf_op jit(solution)/shard_map/all_to_all | solution.py:92
  14.3 0.7 copy.48
  15.0 0.7 copy.51
  15.7 4.7 %all-to-all-done = bf16[2,4,16,1152]{3,2,0,1:T(8,128)(2,1)S(1)} async-done(((bf16[2,4,16,1152]{3,2,0,1:T(8,128)(2,1)}), bf16[2,4,16,1152]{3,2,0,1:T(8,128)(2,1)S(1)}, u32[]{:S(2)}, u32[]{:S(2)}) %all-to-all-start) | async-done | bytes 294944 | tf_op jit(solution)/shard_map/all_to_all | solution.py:92
  20.4 3.5 %all-to-all-start.1 = ((bf16[2,4,16,1152]{3,2,0,1:T(8,128)(2,1)}), bf16[2,4,16,1152]{3,2,0,1:T(8,128)(2,1)S(1)}, u32[]{:S(2)}, u32[]{:S(2)}) async-start(bf16[2,4,16,1152]{3,2,0,1:T(8,128)(2,1)} %copy.48), calls=%async_computation.1 | async-start | bytes 589824 | tf_op jit(solution)/shard_map/all_to_all | solution.py:93
  23.9 0.1 compare_reduce_fusion
  24.0 0.9 %reshape.45 = bf16[8,16,16,72]{3,2,1,0:T(8,128)(2,1)S(1)} reshape(bf16[4,2,1,16,1152]{4,3,1,0,2:T(8,128)(2,1)S(1)} %bitcast.98) | data formatting | bytes 589824 | tf_op jit(solution)/shard_map/reshape | solution.py:25
  24.9 5.3 %all-to-all-done.1 = bf16[2,4,16,1152]{3,2,0,1:T(8,128)(2,1)S(1)} async-done(((bf16[2,4,16,1152]{3,2,0,1:T(8,128)(2,1)}), bf16[2,4,16,1152]{3,2,0,1:T(8,128)(2,1)S(1)}, u32[]{:S(2)}, u32[]{:S(2)}) %all-to-all-start.1) | async-done | bytes 294944 | tf_op jit(solution)/shard_map/all_to_all | solution.py:93
  30.2 3.5 %all-to-all-start.2 = ((bf16[2,4,16,1152]{3,2,0,1:T(8,128)(2,1)}), bf16[2,4,16,1152]{3,2,0,1:T(8,128)(2,1)S(1)}, u32[]{:S(2)}, u32[]{:S(2)}) async-start(bf16[2,4,16,1152]{3,2,0,1:T(8,128)(2,1)} %copy.51), calls=%async_computation.2 | async-start | bytes 589824 | tf_op jit(solution)/shard_map/all_to_all | solution.py:94
  33.7 0.9 %reshape.46 = bf16[8,16,16,72]{3,2,1,0:T(8,128)(2,1)S(1)} reshape(bf16[4,2,1,16,1152]{4,3,1,0,2:T(8,128)(2,1)S(1)} %bitcast.99) | data formatting | bytes 589824 | tf_op jit(solution)/shard_map/reshape | solution.py:26
  34.6 0.9 %fusion.44 = (f32[16,16,8]{2,1,0:T(8,128)S(1)}, f32[16,16,8,8]{2,3,1,0:T(8,128)S(1)}) fusion(bf16[8,16,16,72]{3,2,1,0:T(8,128)(2,1)S(1)} %reshape.46, bf16[8,16,16,72]{3,2,1,0:T(8,128)(2,1)S(1)} %reshape.45), kind=kOutput, calls=%fused_computation.48 | convolution fusion | flops 2390016 | bytes 663552 | tf_op jit(solution)/shard_map/fnhd,enhd->nhfe/dot_general | solution.py:28
  35.5 0.4 fusion.36
  35.9 4.1 %all-to-all-done.2 = bf16[2,4,16,1152]{3,2,0,1:T(8,128)(2,1)S(1)} async-done(((bf16[2,4,16,1152]{3,2,0,1:T(8,128)(2,1)}), bf16[2,4,16,1152]{3,2,0,1:T(8,128)(2,1)S(1)}, u32[]{:S(2)}, u32[]{:S(2)}) %all-to-all-start.2) | async-done | bytes 294944 | tf_op jit(solution)/shard_map/all_to_all | solution.py:94
  40.1 0.9 %reshape.47 = bf16[8,16,16,72]{3,2,1,0:T(8,128)(2,1)S(1)} reshape(bf16[4,2,1,16,1152]{4,3,1,0,2:T(8,128)(2,1)S(1)} %bitcast.100) | data formatting | bytes 589824 | tf_op jit(solution)/shard_map/reshape | solution.py:27
  41.0 0.7 fusion.35
  41.8 1.3 %reshape.48 = bf16[8,1,16,1152]{3,2,0,1:T(8,128)(2,1)} reshape(bf16[8,16,16,72]{3,2,1,0:T(8,128)(2,1)S(1)} %copy.54) | data formatting | bytes 589824 | tf_op jit(solution)/shard_map/reshape | solution.py:38
  43.1 3.5 %all-to-all-start.3 = ((bf16[8,1,16,1152]{3,2,1,0:T(8,128)(2,1)}), bf16[8,1,16,1152]{3,2,1,0:T(8,128)(2,1)S(1)}, u32[]{:S(2)}, u32[]{:S(2)}) async-start(bf16[8,1,16,1152]{3,2,1,0:T(8,128)(2,1)} %bitcast.10), calls=%async_computation.3 | async-start | bytes 589824 | tf_op jit(solution)/shard_map/all_to_all | solution.py:97
  46.5 6.3 %all-to-all-done.3 = bf16[8,1,16,1152]{3,2,1,0:T(8,128)(2,1)S(1)} async-done(((bf16[8,1,16,1152]{3,2,1,0:T(8,128)(2,1)}), bf16[8,1,16,1152]{3,2,1,0:T(8,128)(2,1)S(1)}, u32[]{:S(2)}, u32[]{:S(2)}) %all-to-all-start.3) | async-done | bytes 294944 | tf_op jit(solution)/shard_map/all_to_all | solution.py:97
  52.9 0.7 copy.56
  53.6 2.6 %pad_maximum_fusion = bf16[2,2,12,16,1152]{4,3,2,1,0:T(8,128)(2,1)} fusion(bf16[2,2,4,16,1152]{4,3,2,1,0:T(8,128)(2,1)} %collective-permute-done.1, bf16[1,2,4,16,1152]{4,3,2,1,0:T(8,128)(2,1)S(1)} %bitcast.95, bf16[1,2,4,16,1152]{4,3,2,1,0:T(8,128)(2,1)S(1)} %bitcast.97, bf16[2,2,4,16,1152]{4,3,2,1,0:T(8,128)(2,1)S(1)} %collective-permute-done), kind=kLoop, calls=%fused_computation.29 | loop fusion | flops 2654208 | bytes 3538944 | tf_op jit(solution)/shard_map/concatenate | solution.py:55
  56.3 19.0 %while.11 = (s32[]{:T(128)}, bf16[2,4,16,1152]{3,2,1,0:T(8,128)(2,1)S(1)}, s32[2]{0:T(128)S(1)}, bf16[2,2,12,16,1152]{4,3,2,1,0:T(8,128)(2,1)}, bf16[2,4,16,1152...) while((s32[]{:T(128)}, ...), condition=%wide.region_4.5_spmd.clone, body=%wide.region_1.4_spmd.clone.sunk | while | flops 59131268 | bytes 8859591 | solution.py:84
  56.3 0.6 dynamic_slice.30
  58.8 1.2 %constant_dynamic-slice_fusion.6 = (bf16[1,1,12,16,1152]{4,3,2,1,0:T(8,128)(2,1)S(1)}, bf16[1,1,12,16,1152]{4,3,2,1,0:T(8,128)(2,1)S(1)}) fusion(bf16[2,2,12,16,1152]{4,3,2,1,0:T(8,128)(2,1)} %get-tuple-element.134, s32[]{:T(128)S(6)} %select_n.44), kind=kLoop, calls=%fused_computation.21.clone.1 | loop fusion | bytes 1769476 | tf_op jit(solution)/shard_map/while/body/eval_jaxpr/dynamic_slice | solution.py:66
  60.0 1.4 %squeeze.22 = bf16[192,16,72]{2,1,0:T(8,128)(2,1)S(1)} reshape(bf16[1,1,12,16,1152]{4,3,2,1,0:T(8,128)(2,1)S(1)} %get-tuple-element.112) | data formatting | bytes 884736 | tf_op jit(solution)/shard_map/while/body/eval_jaxpr/reshape;while/body/eval_jaxpr/squeeze | solution.py:66
  61.4 0.5 squeeze.21
  62.0 0.6 fusion.59
  62.7 0.1 broadcast_in_dim.85
  62.8 0.5 fusion.60
  63.3 1.4 %squeeze.20 = bf16[192,16,72]{2,1,0:T(8,128)(2,1)S(1)} reshape(bf16[1,1,12,16,1152]{4,3,2,1,0:T(8,128)(2,1)S(1)} %get-tuple-element.111) | data formatting | bytes 884736 | tf_op jit(solution)/shard_map/while/body/eval_jaxpr/reshape;while/body/eval_jaxpr/squeeze | solution.py:67
  64.6 0.6 fusion.61
  65.2 0.2 copy.82
  65.4 0.3 convert_element_type.38
  65.7 0.6 dynamic_slice.30
  68.3 1.2 %constant_dynamic-slice_fusion.6 = (bf16[1,1,12,16,1152]{4,3,2,1,0:T(8,128)(2,1)S(1)}, bf16[1,1,12,16,1152]{4,3,2,1,0:T(8,128)(2,1)S(1)}) fusion(bf16[2,2,12,16,1152]{4,3,2,1,0:T(8,128)(2,1)} %get-tuple-element.134, s32[]{:T(128)S(6)} %select_n.44), kind=kLoop, calls=%fused_computation.21.clone.1 | loop fusion | bytes 1769476 | tf_op jit(solution)/shard_map/while/body/eval_jaxpr/dynamic_slice | solution.py:66
  69.5 1.4 %squeeze.22 = bf16[192,16,72]{2,1,0:T(8,128)(2,1)S(1)} reshape(bf16[1,1,12,16,1152]{4,3,2,1,0:T(8,128)(2,1)S(1)} %get-tuple-element.112) | data formatting | bytes 884736 | tf_op jit(solution)/shard_map/while/body/eval_jaxpr/reshape;while/body/eval_jaxpr/squeeze | solution.py:66
  70.9 0.5 squeeze.21
  71.4 0.6 fusion.59
  72.1 0.1 broadcast_in_dim.85
  72.2 0.5 fusion.60
  72.7 1.4 %squeeze.20 = bf16[192,16,72]{2,1,0:T(8,128)(2,1)S(1)} reshape(bf16[1,1,12,16,1152]{4,3,2,1,0:T(8,128)(2,1)S(1)} %get-tuple-element.111) | data formatting | bytes 884736 | tf_op jit(solution)/shard_map/while/body/eval_jaxpr/reshape;while/body/eval_jaxpr/squeeze | solution.py:67
  74.1 0.6 fusion.61
  74.7 0.2 copy.82
  74.9 0.3 convert_element_type.38
  75.2 0.7 copy-done.7
  (33 shorter events, 0.7 us)
Async XLA Ops:
  0.6 13.5 %copy-start = (s32[16,8]{0,1:T(8,128)S(1)}, s32[16,8]{0,1:T(8,128)}, u32[]{:S(2)}) copy-start(s32[16,8]{0,1:T(8,128)} %param.15) | copy-start | bytes 1540
  0.6 13.6 %copy-start.4 = (bf16[2,4,16,1152]{3,2,1,0:T(8,128)(2,1)S(1)}, bf16[2,4,16,1152]{3,2,1,0:T(8,128)(2,1)}, u32[]{:S(2)}) copy-start(bf16[2,4,16,1152]{3,2,1,0:T(8,128)(2,1)} %param.13) | copy-start | bytes 884740
  0.7 14.3 %copy-start.5 = (bf16[2,4,16,1152]{3,2,1,0:T(8,128)(2,1)S(1)}, bf16[2,4,16,1152]{3,2,1,0:T(8,128)(2,1)}, u32[]{:S(2)}) copy-start(bf16[2,4,16,1152]{3,2,1,0:T(8,128)(2,1)} %param.14) | copy-start | bytes 884740
  2.7 51.0 %collective-permute-start = (bf16[2,2,4,16,1152]{4,3,2,1,0:T(8,128)(2,1)}, bf16[2,2,4,16,1152]{4,3,2,1,0:T(8,128)(2,1)S(1)}, u32[]{:S(2)}, u32[]{:S(2)}) collective-permute-start(bf16[2,2,4,16,1152]{4,3,2,1,0:T(8,128)(2,1)} %pad_maximum_fusion.1), channel_id=1, source_target_pairs={{0,4},{4,8},{8,12},{1,5},{5,9},{9,13},{2,6},{6,10},{10,14},{3,7},{... | collective-permute-start | bytes 1769480 | tf_op jit(solution)/shard_map/ppermute | solution.py:16
  7.6 46.0 %collective-permute-start.1 = (bf16[2,2,4,16,1152]{4,3,2,1,0:T(8,128)(2,1)}, bf16[2,2,4,16,1152]{4,3,2,1,0:T(8,128)(2,1)}, u32[]{:S(2)}, u32[]{:S(2)}) collective-permute-start(bf16[2,2,4,16,1152]{4,3,2,1,0:T(8,128)(2,1)} %pad_maximum_fusion.1), channel_id=1, source_target_pairs={{4,0},{8,4},{12,8},{5,1},{9,5},{13,9},{6,2},{10,6},{14,10},{7,3},{... | collective-permute-start | bytes 1769480 | tf_op jit(solution)/shard_map/ppermute | solution.py:16
  10.6 9.8 %all-to-all-start = ((bf16[2,4,16,1152]{3,2,0,1:T(8,128)(2,1)}), bf16[2,4,16,1152]{3,2,0,1:T(8,128)(2,1)S(1)}, u32[]{:S(2)}, u32[]{:S(2)}) async-start(bf16[2,4,16,1152]{3,2,0,1:T(8,128)(2,1)} %copy.47), calls=%async_computation | async-start | bytes 589824 | tf_op jit(solution)/shard_map/all_to_all | solution.py:92
  20.4 9.8 %all-to-all-start.1 = ((bf16[2,4,16,1152]{3,2,0,1:T(8,128)(2,1)}), bf16[2,4,16,1152]{3,2,0,1:T(8,128)(2,1)S(1)}, u32[]{:S(2)}, u32[]{:S(2)}) async-start(bf16[2,4,16,1152]{3,2,0,1:T(8,128)(2,1)} %copy.48), calls=%async_computation.1 | async-start | bytes 589824 | tf_op jit(solution)/shard_map/all_to_all | solution.py:93
  30.2 9.8 %all-to-all-start.2 = ((bf16[2,4,16,1152]{3,2,0,1:T(8,128)(2,1)}), bf16[2,4,16,1152]{3,2,0,1:T(8,128)(2,1)S(1)}, u32[]{:S(2)}, u32[]{:S(2)}) async-start(bf16[2,4,16,1152]{3,2,0,1:T(8,128)(2,1)} %copy.51), calls=%async_computation.2 | async-start | bytes 589824 | tf_op jit(solution)/shard_map/all_to_all | solution.py:94
  41.7 11.9 %copy-start.2 = (bf16[2,4,16,1152]{3,2,1,0:T(8,128)(2,1)S(1)}, bf16[2,4,16,1152]{3,2,1,0:T(8,128)(2,1)}, u32[]{:S(2)}) copy-start(bf16[2,4,16,1152]{3,2,1,0:T(8,128)(2,1)} %param.11) | copy-start | bytes 884740
  41.7 11.9 %copy-start.3 = (bf16[2,4,16,1152]{3,2,1,0:T(8,128)(2,1)S(1)}, bf16[2,4,16,1152]{3,2,1,0:T(8,128)(2,1)}, u32[]{:S(2)}) copy-start(bf16[2,4,16,1152]{3,2,1,0:T(8,128)(2,1)} %param.10) | copy-start | bytes 884740
  43.1 9.8 %all-to-all-start.3 = ((bf16[8,1,16,1152]{3,2,1,0:T(8,128)(2,1)}), bf16[8,1,16,1152]{3,2,1,0:T(8,128)(2,1)S(1)}, u32[]{:S(2)}, u32[]{:S(2)}) async-start(bf16[8,1,16,1152]{3,2,1,0:T(8,128)(2,1)} %bitcast.10), calls=%async_computation.3 | async-start | bytes 589824 | tf_op jit(solution)/shard_map/all_to_all | solution.py:97
  53.6 2.6 %copy-start.1 = (bf16[2,4,16,1152]{3,2,1,0:T(8,128)(2,1)S(1)}, bf16[2,4,16,1152]{3,2,1,0:T(8,128)(2,1)}, u32[]{:S(2)}) copy-start(bf16[2,4,16,1152]{3,2,1,0:T(8,128)(2,1)} %param.9) | copy-start | bytes 884740
  53.6 2.6 %copy-start.6 = (bf16[2,4,16,1152]{3,2,1,0:T(8,128)(2,1)S(1)}, bf16[2,4,16,1152]{3,2,1,0:T(8,128)(2,1)}, u32[]{:S(2)}) copy-start(bf16[2,4,16,1152]{3,2,1,0:T(8,128)(2,1)} %custom-call) | copy-start | bytes 884740
  75.2 0.7 copy-start.7
where the time goes:
time: 77 us; the launch traced here: 75.9 us
  local copies, waits for them, and re-layouts  20.4 us (26%)
  waiting for transfers between devices  20.4 us (26%)
  starting transfers between devices  20 us (26%)
  other arithmetic  6.11 us (8%)
  loops' own time  4.04 us (5%)
  matrix products  4 us (5%)
  between operations  0.85 us (1%)
    all_to_all x1, waiting for transfers between devices, on_device(): lax.all_to_all(attended, 'tm', split_axis=0, concat_axis=1, tiled=True)  6.34 us
    ppermute x2, starting transfers between devices, passed_along(): return lax.ppermute(value, axis, pairs)  6.24 us
    all_to_all x1, waiting for transfers between devices, on_device(): lax.all_to_all(grid_k, 'tm', split_axis=1, concat_axis=0, tiled=True)  5.3 us
    all_to_all x1, waiting for transfers between devices, on_device(): lax.all_to_all(grid_q, 'tm', split_axis=1, concat_axis=0, tiled=True)  4.69 us
    unnamed x20, local copies, waits for them, and re-layouts  4.65 us
    all_to_all x1, waiting for transfers between devices, on_device(): lax.all_to_all(grid_v, 'tm', split_axis=1, concat_axis=0, tiled=True)  4.12 us
    another operation x1, loops' own time, on_device(): spatial_out = lax.map(frame_window, jnp.arange(frames, dtype=jnp.int32))  4.04 us
    all_to_all x1, starting transfers between devices, on_device(): lax.all_to_all(grid_k, 'tm', split_axis=1, concat_axis=0, tiled=True)  3.45 us
  transfers between devices with their start and end apart: 6, of which 4 were waited for; matrix products, arithmetic and copies ran while one was open for 14% of the time, Pallas kernels for 0%

commit v1 on v0

v1 whole, which is shorter than its diff:
```python
import functools
import math

import jax
import jax.numpy as jnp
from jax import lax
from jax.experimental import pallas as pl
from jax.experimental.pallas import tpu as pltpu
from jax.sharding import PartitionSpec as P

HEAD_DIM = 72
PAIR = 2 * HEAD_DIM
LANES = 128
WINDOW = 2 * LANES
SCALE = HEAD_DIM ** (-0.5) * math.log2(math.e)
big_negative = -1e30


def shifted(value, axis, by):
    length = lax.axis_size(axis)
    pairs = [(i, i + by) for i in range(length) if 0 <= i + by < length]
    return lax.ppermute(value, axis, pairs)


def gathered(values, axis):
    length = lax.axis_size(axis)
    held = [[value] for value in values]
    step = length // 2
    while step:
        pairs = [(i, i ^ step) for i in range(length)]
        for parts in held:
            parts.extend([lax.ppermute(part, axis, pairs) for part in parts])
        step //= 2
    return held


def head_masks(pair, rows):
    lane = lax.broadcasted_iota(jnp.int32, (rows, WINDOW), 1)
    first = (PAIR - LANES) * pair
    return [
        (lane >= first + head * HEAD_DIM) & (lane < first + (head + 1) * HEAD_DIM)
        for head in range(2)
    ]


def attend_pair(pair, queries, keyset, values, bias):
    rows = queries.shape[0]
    masks = head_masks(pair, rows)
    stacked = jnp.concatenate(
        [jnp.where(mask, queries, jnp.zeros_like(queries)) for mask in masks], axis=0
    )
    scores = lax.dot_general(
        stacked, keyset, (((1,), (1,)), ((), ())), preferred_element_type=jnp.float32
    )
    scores = scores * SCALE + bias
    highest = jnp.max(scores, axis=-1, keepdims=True)
    weights = jnp.exp2(scores - highest)
    totals = jnp.sum(weights, axis=-1, keepdims=True)
    blended = jnp.dot(
        weights.astype(jnp.bfloat16), values, preferred_element_type=jnp.float32
    )
    blended = blended / totals
    zeros = jnp.zeros((rows, WINDOW), jnp.float32)
    return jnp.where(masks[0], blended[:rows], jnp.where(masks[1], blended[rows:], zeros))


def attend(channels, read_queries, read_keys, read_values, bias, write):
    carry = None
    pairs = channels // PAIR
    for pair in range(pairs):
        lanes = slice(pair * LANES, pair * LANES + WINDOW)
        both = attend_pair(
            pair, read_queries(lanes), read_keys(lanes), read_values(lanes), bias
        )
        low = both[:, :LANES]
        if carry is not None:
            low = low + carry
        write(slice(pair * LANES, (pair + 1) * LANES), low.astype(jnp.bfloat16))
        carry = both[:, LANES:]
    write(slice(pairs * LANES, (pairs + 1) * LANES), carry.astype(jnp.bfloat16))


def spatial_kernel(blocks, row_start_ref, lists_ref, q_ref, *refs):
    k_refs, v_refs, out_ref = refs[:blocks], refs[blocks : 2 * blocks], refs[2 * blocks]
    frames, rows, columns, channels = q_ref.shape
    entries = lists_ref.shape[1]
    row_start = row_start_ref[0]
    extent = blocks * rows
    key_rows = lax.broadcasted_iota(jnp.int32, (columns, extent * columns), 1) // columns
    key_rows = key_rows + (row_start - (blocks // 2) * rows)
    bias = []
    for row in range(rows):
        member = key_rows == row_start + row
        for entry in range(entries):
            member = member | (key_rows == lists_ref[row_start + row, entry])
        bias.append(jnp.where(member & (key_rows >= 0), 0.0, big_negative))
    bias = jnp.concatenate(bias + bias, axis=0)
    tokens = rows * columns
    for frame in range(frames):

        def read(chosen, lanes):
            return jnp.concatenate(
                [ref[frame, :, :, lanes].reshape(tokens, WINDOW) for ref in chosen], axis=0
            )

        def write(lanes, value):
            out_ref[frame, :, :, lanes] = value.reshape(rows, columns, LANES)

        attend(
            channels,
            lambda lanes: read([q_ref], lanes),
            lambda lanes: read(k_refs, lanes),
            lambda lanes: read(v_refs, lanes),
            bias,
            write,
        )


def temporal_kernel(blocks, q_ref, *refs):
    k_refs, v_refs, out_ref = refs[:blocks], refs[blocks : 2 * blocks], refs[2 * blocks]
    frames, rows, columns, channels = q_ref.shape
    queries = frames * columns
    shape = (2 * queries, blocks * queries)
    own = lax.broadcasted_iota(jnp.int32, shape, 0) % columns
    other = lax.broadcasted_iota(jnp.int32, shape, 1) % columns
    bias = jnp.where(own == other, 0.0, big_negative)
    for row in range(rows):

        def read(chosen, lanes):
            return jnp.concatenate(
                [ref[:, row, :, lanes].reshape(queries, WINDOW) for ref in chosen], axis=0
            )

        def write(lanes, value):
            out_ref[:, row, :, lanes] = value.reshape(frames, columns, LANES)

        attend(
            channels,
            lambda lanes: read([q_ref], lanes),
            lambda lanes: read(k_refs, lanes),
            lambda lanes: read(v_refs, lanes),
            bias,
            write,
        )


def in_vmem():
    return pl.BlockSpec(memory_space=pltpu.VMEM)


def in_smem():
    return pl.BlockSpec(memory_space=pltpu.SMEM)


def on_device(spatial_q, spatial_k, spatial_v, temporal_q, temporal_k, temporal_v, key_lists):
    frames, rows, columns, channels = spatial_q.shape
    reach = -(-(key_lists.shape[1] // 2) // rows)
    row_start = lax.axis_index("space") * rows
    hops = [by for distance in range(1, reach + 1) for by in (distance, -distance)]
    hops.sort(reverse=True)
    hops.insert(reach, 0)
    temporal_keys, temporal_values = gathered([temporal_k, temporal_v], "tm")
    spatial_keys = [shifted(spatial_k, "space", by) if by else spatial_k for by in hops]
    spatial_values = [shifted(spatial_v, "space", by) if by else spatial_v for by in hops]

    params = pltpu.CompilerParams(vmem_limit_bytes=40 * 1024 * 1024)
    out_shape = jax.ShapeDtypeStruct(spatial_q.shape, jnp.bfloat16)
    blocks = len(hops)
    tokens = frames * rows * columns
    spatial_out = pl.pallas_call(
        functools.partial(spatial_kernel, blocks),
        out_shape=out_shape,
        in_specs=[in_smem(), in_smem()] + [in_vmem()] * (1 + 2 * blocks),
        out_specs=in_vmem(),
        compiler_params=params,
        cost_estimate=pl.CostEstimate(
            flops=4 * tokens * blocks * rows * columns * channels,
            bytes_accessed=(2 + 2 * blocks) * spatial_q.size * 2,
            transcendentals=0,
        ),
        name="spatial",
    )(row_start.reshape(1), key_lists, spatial_q, *spatial_keys, *spatial_values)
    blocks = len(temporal_keys)
    temporal_out = pl.pallas_call(
        functools.partial(temporal_kernel, blocks),
        out_shape=out_shape,
        in_specs=[in_vmem()] * (1 + 2 * blocks),
        out_specs=in_vmem(),
        compiler_params=params,
        cost_estimate=pl.CostEstimate(
            flops=4 * tokens * blocks * frames * columns * channels,
            bytes_accessed=(2 + 2 * blocks) * spatial_q.size * 2,
            transcendentals=0,
        ),
        name="temporal",
    )(temporal_q, *temporal_keys, *temporal_values)
    return (spatial_out, temporal_out)


def solution(mesh):
    placed = P(("video", "tm"), "space", None, None)
    return jax.shard_map(
        on_device,
        mesh=mesh,
        in_specs=(placed,) * 6 + (P(),),
        out_specs=(placed, placed),
        check_vma=False,
    )
```

time: 77 us -> 41.1 us (0.53)
  local copies, waits for them, and re-layouts: 20.4 us -> 3.65 us
  Pallas kernels: 0 us -> 13.8 us
  waiting for transfers between devices: 20.4 us -> 7.88 us
  other arithmetic: 6.11 us -> 0 us
  starting transfers between devices: 20 us -> 14.7 us
  loops' own time: 4.04 us -> 0 us
  matrix products: 4 us -> 0 us
    all_to_all x4 -> x0, waiting for transfers between devices: 20.4 us -> none  [the longest x1 6.34 us: on_device(): lax.all_to_all(attended, 'tm', split_axis=0, concat_axis=1, tiled=True)]
    all_to_all x4 -> x0, starting transfers between devices: 13.8 us -> none  [the longest x1 3.45 us: on_device(): lax.all_to_all(grid_k, 'tm', split_axis=1, concat_axis=0, tiled=True)]
    pallas_call x0 -> x2, Pallas kernels: none -> 13.8 us  [the longest x1 8.36 us: on_device(): pl.pallas_call(functools.partial(temporal_kernel, blocks), out_shape=out_...]
    ppermute x2 -> x10, starting transfers between devices: 6.24 us -> 14.7 us  [the longest x4 11.1 us: shifted(): return lax.ppermute(value, axis, pairs)]
    ppermute x2 -> x10, waiting for transfers between devices: 0.01 us -> 7.88 us  [the longest x4 5.55 us: shifted(): return lax.ppermute(value, axis, pairs)]
    squeeze x8 -> x0, local copies, waits for them, and re-layouts: 6.51 us -> none  [the longest x2 2.73 us: frame_window(): values = window[1, frame_index].reshape(extent * columns, HEADS, HEAD_DIM)]
    reshape x4 -> x0, local copies, waits for them, and re-layouts: 4.08 us -> none  [the longest x1 1.26 us: temporal_attend(): return blended.astype(jnp.bfloat16).reshape(outer)]
    another operation x1 -> x0, loops' own time: 4.04 us -> none  [on_device(): spatial_out = lax.map(frame_window, jnp.arange(frames, dtype=jnp.int32))]
  transfers between devices with their start and end apart: 6 -> 10, of which waited for: 4 -> 4; matrix products, arithmetic and copies ran while one was open for 14% -> 2% of each run, Pallas kernels for 0% -> 13%
where the time goes in v1:
time: 41.1 us; the launch traced here: 40.7 us
  starting transfers between devices  14.7 us (36%)
  Pallas kernels  13.8 us (34%)
  waiting for transfers between devices  7.88 us (19%)
  local copies, waits for them, and re-layouts  3.65 us (9%)
  between operations  0.72 us (2%)
    ppermute x4, starting transfers between devices, shifted(): return lax.ppermute(value, axis, pairs)  11.1 us
    pallas_call x1, Pallas kernels, on_device(): pl.pallas_call(functools.partial(temporal_kernel, blocks), out_shape=out_...  8.36 us
    ppermute x4, waiting for transfers between devices, shifted(): return lax.ppermute(value, axis, pairs)  5.55 us
    pallas_call x1, Pallas kernels, on_device(): pl.pallas_call(functools.partial(spatial_kernel, blocks), out_shape=out_s...  5.44 us
    unnamed x13, local copies, waits for them, and re-layouts  3.65 us
    ppermute x6, starting transfers between devices, gathered(): parts.extend([lax.ppermute(part, axis, pairs) for part in parts])  3.6 us
    ppermute x6, waiting for transfers between devices, gathered(): parts.extend([lax.ppermute(part, axis, pairs) for part in parts])  2.33 us
  transfers between devices with their start and end apart: 10, of which 4 were waited for; matrix products, arithmetic and copies ran while one was open for 2% of the time, Pallas kernels for 13%

profile of v1, /device:TPU:0, one launch (start us, length us, event | category | flops | bytes accessed | tf_op | source)
XLA Modules:
  0.0 40.7 jit_solution(2268441123533741092)
XLA Ops:
  0.6 3.0 %collective-permute-start.4 = (bf16[2,4,16,1152]{3,2,1,0:T(8,128)(2,1)}, bf16[2,4,16,1152]{3,2,1,0:T(8,128)(2,1)S(1)}, u32[]{:S(2)}, u32[]{:S(2)}) collective-permute-start(bf16[2,4,16,1152]{3,2,1,0:T(8,128)(2,1)} %refs_0_.1), channel_id=1, source_target_pairs={{0,2},{1,3},{2,0},{3,1},{4,6},{5,7},{6,4},{7,5},{8,10},{9,11},{10,... | collective-permute-start | bytes 884744 | tf_op jit(solution)/shard_map/ppermute | solution.py:32
  3.6 0.1 collective-permute-start.7
  3.7 3.9 %collective-permute-start = (bf16[2,4,16,1152]{3,2,1,0:T(8,128)(2,1)}, bf16[2,4,16,1152]{3,2,1,0:T(8,128)(2,1)S(1)}, u32[]{:S(2)}, u32[]{:S(2)}) collective-permute-start(bf16[2,4,16,1152]{3,2,1,0:T(8,128)(2,1)} %refs_1_.1), channel_id=1, source_target_pairs={{0,4},{4,8},{8,12},{1,5},{5,9},{9,13},{2,6},{6,10},{10,14},{3,7},{... | collective-permute-start | bytes 884744 | tf_op jit(solution)/shard_map/ppermute | solution.py:22
  7.7 1.3 %collective-permute-start.1 = (bf16[2,4,16,1152]{3,2,1,0:T(8,128)(2,1)}, bf16[2,4,16,1152]{3,2,1,0:T(8,128)(2,1)S(1)}, u32[]{:S(2)}, u32[]{:S(2)}) collective-permute-start(bf16[2,4,16,1152]{3,2,1,0:T(8,128)(2,1)} %refs_1_.1), channel_id=1, source_target_pairs={{4,0},{8,4},{12,8},{5,1},{9,5},{13,9},{6,2},{10,6},{14,10},{7,3},{... | collective-permute-start | bytes 884744 | tf_op jit(solution)/shard_map/ppermute | solution.py:22
  9.0 4.6 %collective-permute-start.2 = (bf16[2,4,16,1152]{3,2,1,0:T(8,128)(2,1)}, bf16[2,4,16,1152]{3,2,1,0:T(8,128)(2,1)S(1)}, u32[]{:S(2)}, u32[]{:S(2)}) collective-permute-start(bf16[2,4,16,1152]{3,2,1,0:T(8,128)(2,1)} %refs_4_.2), channel_id=1, source_target_pairs={{0,4},{4,8},{8,12},{1,5},{5,9},{9,13},{2,6},{6,10},{10,14},{3,7},{... | collective-permute-start | bytes 884744 | tf_op jit(solution)/shard_map/ppermute | solution.py:22
  13.5 0.0 collective-permute-done.4.refs_1_
  13.6 1.3 %collective-permute-start.3 = (bf16[2,4,16,1152]{3,2,1,0:T(8,128)(2,1)}, bf16[2,4,16,1152]{3,2,1,0:T(8,128)(2,1)S(1)}, u32[]{:S(2)}, u32[]{:S(2)}) collective-permute-start(bf16[2,4,16,1152]{3,2,1,0:T(8,128)(2,1)} %refs_4_.2), channel_id=1, source_target_pairs={{4,0},{8,4},{12,8},{5,1},{9,5},{13,9},{6,2},{10,6},{14,10},{7,3},{... | collective-permute-start | bytes 884744 | tf_op jit(solution)/shard_map/ppermute | solution.py:22
  14.9 2.3 %collective-permute-done.7.refs_5_ = bf16[2,4,16,1152]{3,2,1,0:T(8,128)(2,1)S(1)} collective-permute-done((bf16[2,4,16,1152]{3,2,1,0:T(8,128)(2,1)}, bf16[2,4,16,1152]{3,2,1,0:T(8,128)(2,1)S(1)}, u32[]{:S(2)}, u32[]{:S(2)}) %collective-permute-start.7) | collective-permute-done | bytes 294944 | tf_op jit(solution)/shard_map/ppermute | solution.py:32
  17.2 0.0 collective-permute-start.5
  17.2 0.0 collective-permute-done.refs_0_
  17.2 0.5 %collective-permute-start.8 = (bf16[2,4,16,1152]{3,2,1,0:T(8,128)(2,1)}, bf16[2,4,16,1152]{3,2,1,0:T(8,128)(2,1)S(1)}, u32[]{:S(2)}, u32[]{:S(2)}) collective-permute-start(bf16[2,4,16,1152]{3,2,1,0:T(8,128)(2,1)} %refs_4_.3), channel_id=1, source_target_pairs={{0,1},{1,0},{2,3},{3,2},{4,5},{5,4},{6,7},{7,6},{8,9},{9,8},{10,11... | collective-permute-start | bytes 884744 | tf_op jit(solution)/shard_map/ppermute | solution.py:32
  17.7 0.9 %collective-permute-done.1.refs_2_ = bf16[2,4,16,1152]{3,2,1,0:T(8,128)(2,1)S(1)} collective-permute-done((bf16[2,4,16,1152]{3,2,1,0:T(8,128)(2,1)}, bf16[2,4,16,1152]{3,2,1,0:T(8,128)(2,1)S(1)}, u32[]{:S(2)}, u32[]{:S(2)}) %collective-permute-start.1) | collective-permute-done | bytes 294944 | tf_op jit(solution)/shard_map/ppermute | solution.py:22
  18.6 0.0 collective-permute-start.6
  18.6 1.4 %collective-permute-done.2.refs_3_ = bf16[2,4,16,1152]{3,2,1,0:T(8,128)(2,1)S(1)} collective-permute-done((bf16[2,4,16,1152]{3,2,1,0:T(8,128)(2,1)}, bf16[2,4,16,1152]{3,2,1,0:T(8,128)(2,1)S(1)}, u32[]{:S(2)}, u32[]{:S(2)}) %collective-permute-start.2) | collective-permute-done | bytes 294944 | tf_op jit(solution)/shard_map/ppermute | solution.py:22
  20.0 0.0 collective-permute-start.9
  20.0 0.8 %copy.9.lists_ref = s32[16,8]{1,0:T(8,128)S(1)} copy(s32[16,8]{0,1:T(8,128)} %param.13) | data formatting | bytes 1024 | tf_op args[6]
  20.7 3.3 %collective-permute-done.3.refs_5_ = bf16[2,4,16,1152]{3,2,1,0:T(8,128)(2,1)S(1)} collective-permute-done((bf16[2,4,16,1152]{3,2,1,0:T(8,128)(2,1)}, bf16[2,4,16,1152]{3,2,1,0:T(8,128)(2,1)S(1)}, u32[]{:S(2)}, u32[]{:S(2)}) %collective-permute-start.3) | collective-permute-done | bytes 294944 | tf_op jit(solution)/shard_map/ppermute | solution.py:22
  24.0 0.0 copy-start.3
  24.0 1.0 %copy-done.3 = bf16[2,4,16,1152]{3,2,1,0:T(8,128)(2,1)S(1)} copy-done((bf16[2,4,16,1152]{3,2,1,0:T(8,128)(2,1)S(1)}, bf16[2,4,16,1152]{3,2,1,0:T(8,128)(2,1)}, u32[]{:S(2)}) %copy-start.3) | copy-done | bytes 294936
  25.0 0.0 copy-start.4
  25.0 1.0 %copy-done.4 = bf16[2,4,16,1152]{3,2,1,0:T(8,128)(2,1)S(1)} copy-done((bf16[2,4,16,1152]{3,2,1,0:T(8,128)(2,1)S(1)}, bf16[2,4,16,1152]{3,2,1,0:T(8,128)(2,1)}, u32[]{:S(2)}) %copy-start.4) | copy-done | bytes 294936
  25.9 0.0 copy-start.5
  25.9 1.0 %copy-done.5 = bf16[2,4,16,1152]{3,2,1,0:T(8,128)(2,1)S(1)} copy-done((bf16[2,4,16,1152]{3,2,1,0:T(8,128)(2,1)S(1)}, bf16[2,4,16,1152]{3,2,1,0:T(8,128)(2,1)}, u32[]{:S(2)}) %copy-start.5) | copy-done | bytes 294936
  26.9 0.0 copy-start
  26.9 0.0 copy-start.1
  26.9 0.0 copy-start.2
  26.9 5.4 %spatial.1 = bf16[2,4,16,1152]{3,2,1,0:T(8,128)(2,1)} custom-call(s32[1]{0:T(128)} %bitcast.row_start_ref, s32[16,8]{1,0:T(8,128)S(1)} %copy.9.lists_ref, bf16[2,4,16,1152]{3,2,1,0:T(8,128)(2,1)S(1)} %copy-done.3, bf16[2,4,16,1152]{3,2,1,0:T(8,128)(2,1)S(1)} %collective-permute-done.refs_0_, bf16[2,4,16,1152]{3,2,1,0:T(8,128)(2,1)S(1)} %copy-done.4, ...), custom_call_target="tpu_custom_call" | custom-call | flops 113246208 | bytes 2359296 | tf_op jit(solution)/shard_map/spatial/pallas_call | solution.py:170
  32.3 0.0 collective-permute-done.5.refs_2_
  32.3 0.0 collective-permute-done.8.refs_6_
  32.3 0.0 collective-permute-done.6.refs_3_
  32.3 0.0 collective-permute-done.9.refs_7_
  32.4 0.0 copy-done
  32.4 0.0 copy-done.1
  32.4 0.0 copy-done.2
  32.4 8.4 %temporal.1 = bf16[2,4,16,1152]{3,2,1,0:T(8,128)(2,1)} custom-call(bf16[2,4,16,1152]{3,2,1,0:T(8,128)(2,1)S(1)} %copy-done, bf16[2,4,16,1152]{3,2,1,0:T(8,128)(2,1)S(1)} %copy-done.1, bf16[2,4,16,1152]{3,2,1,0:T(8,128)(2,1)S(1)} %collective-permute-done.4.refs_1_, bf16[2,4,16,1152]{3,2,1,0:T(8,128)(2,1)S(1)} %collective-permute-done.5.refs_2_, ...), custom_call_target="tpu_custom_call" | custom-call | flops 75497472 | bytes 2949120 | tf_op jit(solution)/shard_map/temporal/pallas_call | solution.py:184
Async XLA Ops:
  0.6 12.9 %collective-permute-start.4 = (bf16[2,4,16,1152]{3,2,1,0:T(8,128)(2,1)}, bf16[2,4,16,1152]{3,2,1,0:T(8,128)(2,1)S(1)}, u32[]{:S(2)}, u32[]{:S(2)}) collective-permute-start(bf16[2,4,16,1152]{3,2,1,0:T(8,128)(2,1)} %refs_0_.1), channel_id=1, source_target_pairs={{0,2},{1,3},{2,0},{3,1},{4,6},{5,7},{6,4},{7,5},{8,10},{9,11},{10,... | collective-permute-start | bytes 884744 | tf_op jit(solution)/shard_map/ppermute | solution.py:32
  3.6 13.5 %collective-permute-start.7 = (bf16[2,4,16,1152]{3,2,1,0:T(8,128)(2,1)}, bf16[2,4,16,1152]{3,2,1,0:T(8,128)(2,1)S(1)}, u32[]{:S(2)}, u32[]{:S(2)}) collective-permute-start(bf16[2,4,16,1152]{3,2,1,0:T(8,128)(2,1)} %refs_4_.3), channel_id=1, source_target_pairs={{0,2},{1,3},{2,0},{3,1},{4,6},{5,7},{6,4},{7,5},{8,10},{9,11},{10,... | collective-permute-start | bytes 884744 | tf_op jit(solution)/shard_map/ppermute | solution.py:32
  3.7 13.5 %collective-permute-start = (bf16[2,4,16,1152]{3,2,1,0:T(8,128)(2,1)}, bf16[2,4,16,1152]{3,2,1,0:T(8,128)(2,1)S(1)}, u32[]{:S(2)}, u32[]{:S(2)}) collective-permute-start(bf16[2,4,16,1152]{3,2,1,0:T(8,128)(2,1)} %refs_1_.1), channel_id=1, source_target_pairs={{0,4},{4,8},{8,12},{1,5},{5,9},{9,13},{2,6},{6,10},{10,14},{3,7},{... | collective-permute-start | bytes 884744 | tf_op jit(solution)/shard_map/ppermute | solution.py:22
  7.7 10.9 %collective-permute-start.1 = (bf16[2,4,16,1152]{3,2,1,0:T(8,128)(2,1)}, bf16[2,4,16,1152]{3,2,1,0:T(8,128)(2,1)S(1)}, u32[]{:S(2)}, u32[]{:S(2)}) collective-permute-start(bf16[2,4,16,1152]{3,2,1,0:T(8,128)(2,1)} %refs_1_.1), channel_id=1, source_target_pairs={{4,0},{8,4},{12,8},{5,1},{9,5},{13,9},{6,2},{10,6},{14,10},{7,3},{... | collective-permute-start | bytes 884744 | tf_op jit(solution)/shard_map/ppermute | solution.py:22
  9.0 11.0 %collective-permute-start.2 = (bf16[2,4,16,1152]{3,2,1,0:T(8,128)(2,1)}, bf16[2,4,16,1152]{3,2,1,0:T(8,128)(2,1)S(1)}, u32[]{:S(2)}, u32[]{:S(2)}) collective-permute-start(bf16[2,4,16,1152]{3,2,1,0:T(8,128)(2,1)} %refs_4_.2), channel_id=1, source_target_pairs={{0,4},{4,8},{8,12},{1,5},{5,9},{9,13},{2,6},{6,10},{10,14},{3,7},{... | collective-permute-start | bytes 884744 | tf_op jit(solution)/shard_map/ppermute | solution.py:22
  13.6 10.4 %collective-permute-start.3 = (bf16[2,4,16,1152]{3,2,1,0:T(8,128)(2,1)}, bf16[2,4,16,1152]{3,2,1,0:T(8,128)(2,1)S(1)}, u32[]{:S(2)}, u32[]{:S(2)}) collective-permute-start(bf16[2,4,16,1152]{3,2,1,0:T(8,128)(2,1)} %refs_4_.2), channel_id=1, source_target_pairs={{4,0},{8,4},{12,8},{5,1},{9,5},{13,9},{6,2},{10,6},{14,10},{7,3},{... | collective-permute-start | bytes 884744 | tf_op jit(solution)/shard_map/ppermute | solution.py:22
  17.2 15.2 %collective-permute-start.5 = (bf16[2,4,16,1152]{3,2,1,0:T(8,128)(2,1)}, bf16[2,4,16,1152]{3,2,1,0:T(8,128)(2,1)S(1)}, u32[]{:S(2)}, u32[]{:S(2)}) collective-permute-start(bf16[2,4,16,1152]{3,2,1,0:T(8,128)(2,1)} %refs_0_.1), channel_id=1, source_target_pairs={{0,1},{1,0},{2,3},{3,2},{4,5},{5,4},{6,7},{7,6},{8,9},{9,8},{10,11... | collective-permute-start | bytes 884744 | tf_op jit(solution)/shard_map/ppermute | solution.py:32
  17.2 15.2 %collective-permute-start.8 = (bf16[2,4,16,1152]{3,2,1,0:T(8,128)(2,1)}, bf16[2,4,16,1152]{3,2,1,0:T(8,128)(2,1)S(1)}, u32[]{:S(2)}, u32[]{:S(2)}) collective-permute-start(bf16[2,4,16,1152]{3,2,1,0:T(8,128)(2,1)} %refs_4_.3), channel_id=1, source_target_pairs={{0,1},{1,0},{2,3},{3,2},{4,5},{5,4},{6,7},{7,6},{8,9},{9,8},{10,11... | collective-permute-start | bytes 884744 | tf_op jit(solution)/shard_map/ppermute | solution.py:32
  18.6 13.7 %collective-permute-start.6 = (bf16[2,4,16,1152]{3,2,1,0:T(8,128)(2,1)S(1)}, bf16[2,4,16,1152]{3,2,1,0:T(8,128)(2,1)S(1)}, u32[]{:S(2)}, u32[]{:S(2)}) collective-permute-start(bf16[2,4,16,1152]{3,2,1,0:T(8,128)(2,1)S(1)} %collective-permute-done.4.refs_1_), channel_id=1, source_target_pairs={{0,1},{1,0},{2,3},{3,2},{4,5},{5,4},{6,7},{7,6},{8,9},{9,8},{10,11... | collective-permute-start | bytes 884744 | tf_op jit(solution)/shard_map/ppermute | solution.py:32
  20.0 12.4 %collective-permute-start.9 = (bf16[2,4,16,1152]{3,2,1,0:T(8,128)(2,1)S(1)}, bf16[2,4,16,1152]{3,2,1,0:T(8,128)(2,1)S(1)}, u32[]{:S(2)}, u32[]{:S(2)}) collective-permute-start(bf16[2,4,16,1152]{3,2,1,0:T(8,128)(2,1)S(1)} %collective-permute-done.7.refs_5_), channel_id=1, source_target_pairs={{0,1},{1,0},{2,3},{3,2},{4,5},{5,4},{6,7},{7,6},{8,9},{9,8},{10,11... | collective-permute-start | bytes 884744 | tf_op jit(solution)/shard_map/ppermute | solution.py:32
  24.0 1.0 %copy-start.3 = (bf16[2,4,16,1152]{3,2,1,0:T(8,128)(2,1)S(1)}, bf16[2,4,16,1152]{3,2,1,0:T(8,128)(2,1)}, u32[]{:S(2)}) copy-start(bf16[2,4,16,1152]{3,2,1,0:T(8,128)(2,1)} %q_ref.2) | copy-start | bytes 884740
  25.0 1.0 %copy-start.4 = (bf16[2,4,16,1152]{3,2,1,0:T(8,128)(2,1)S(1)}, bf16[2,4,16,1152]{3,2,1,0:T(8,128)(2,1)}, u32[]{:S(2)}) copy-start(bf16[2,4,16,1152]{3,2,1,0:T(8,128)(2,1)} %refs_1_.1) | copy-start | bytes 884740
  25.9 1.0 %copy-start.5 = (bf16[2,4,16,1152]{3,2,1,0:T(8,128)(2,1)S(1)}, bf16[2,4,16,1152]{3,2,1,0:T(8,128)(2,1)}, u32[]{:S(2)}) copy-start(bf16[2,4,16,1152]{3,2,1,0:T(8,128)(2,1)} %refs_4_.2) | copy-start | bytes 884740
  26.9 5.5 %copy-start = (bf16[2,4,16,1152]{3,2,1,0:T(8,128)(2,1)S(1)}, bf16[2,4,16,1152]{3,2,1,0:T(8,128)(2,1)}, u32[]{:S(2)}) copy-start(bf16[2,4,16,1152]{3,2,1,0:T(8,128)(2,1)} %q_ref.3) | copy-start | bytes 884740
  26.9 5.5 %copy-start.1 = (bf16[2,4,16,1152]{3,2,1,0:T(8,128)(2,1)S(1)}, bf16[2,4,16,1152]{3,2,1,0:T(8,128)(2,1)}, u32[]{:S(2)}) copy-start(bf16[2,4,16,1152]{3,2,1,0:T(8,128)(2,1)} %refs_0_.1) | copy-start | bytes 884740
  26.9 5.5 %copy-start.2 = (bf16[2,4,16,1152]{3,2,1,0:T(8,128)(2,1)S(1)}, bf16[2,4,16,1152]{3,2,1,0:T(8,128)(2,1)}, u32[]{:S(2)}) copy-start(bf16[2,4,16,1152]{3,2,1,0:T(8,128)(2,1)} %refs_4_.3) | copy-start | bytes 884740

commit v2 on v1

v2 whole, which is shorter than its diff:
```python
import functools
import math

import jax
import jax.numpy as jnp
from jax import lax
from jax.experimental import pallas as pl
from jax.experimental.pallas import tpu as pltpu
from jax.sharding import PartitionSpec as P

HEAD_DIM = 72
PAIR = 2 * HEAD_DIM
LANES = 128
WINDOW = 2 * LANES
SCALE = HEAD_DIM ** (-0.5) * math.log2(math.e)
big_negative = -1e30


def partner_of(index, distance, parity):
    upward = (index // distance) % 2 == parity
    if isinstance(index, int):
        return index + distance if upward else index - distance
    return jnp.where(upward, index + distance, index - distance)


def exchanged(value, axis, distance, parity):
    length = lax.axis_size(axis)
    pairs = []
    for index in range(length):
        partner = partner_of(index, distance, parity)
        pairs.append((index, partner if 0 <= partner < length else index))
    return lax.ppermute(value, axis, pairs)


def gathered(value, axis):
    length = lax.axis_size(axis)
    held = [value]
    step = length // 2
    while step:
        pairs = [(i, i ^ step) for i in range(length)]
        held.extend([lax.ppermute(part, axis, pairs) for part in held])
        step //= 2
    return held


def head_masks(pair, rows):
    lane = lax.broadcasted_iota(jnp.int32, (rows, WINDOW), 1)
    first = (PAIR - LANES) * pair
    return [
        (lane >= first + head * HEAD_DIM) & (lane < first + (head + 1) * HEAD_DIM)
        for head in range(2)
    ]


def window_of(pair):
    return slice(pair * LANES, pair * LANES + WINDOW)


def weigh_pair(pair, queries, keyset, bias):
    rows = queries.shape[0]
    masks = head_masks(pair, rows)
    stacked = jnp.concatenate(
        [queries * mask.astype(jnp.bfloat16) for mask in masks], axis=0
    )
    scores = lax.dot_general(
        stacked, keyset, (((1,), (1,)), ((), ())), preferred_element_type=jnp.float32
    )
    scores = scores * SCALE + bias
    highest = jnp.max(scores, axis=-1, keepdims=True)
    weights = jnp.exp2(scores - highest)
    inverse = 1.0 / jnp.sum(weights, axis=-1, keepdims=True)
    inverse = jnp.where(masks[0], inverse[:rows], jnp.where(masks[1], inverse[rows:], 0.0))
    return weights.astype(jnp.bfloat16), inverse


def blend_pairs(pairs, read_weights, read_inverse, read_values, write):
    carry = None
    for pair in range(pairs):
        inverse = read_inverse(pair)
        rows = inverse.shape[0]
        blended = jnp.dot(
            read_weights(pair), read_values(window_of(pair)), preferred_element_type=jnp.float32
        )
        mask = head_masks(pair, rows)[0]
        both = jnp.where(mask, blended[:rows], blended[rows:]) * inverse
        low = both[:, :LANES]
        if carry is not None:
            low = low + carry
        write(slice(pair * LANES, (pair + 1) * LANES), low.astype(jnp.bfloat16))
        carry = both[:, LANES:]
    write(slice(pairs * LANES, (pairs + 1) * LANES), carry.astype(jnp.bfloat16))


def read_tokens(refs, frame, lanes):
    return jnp.concatenate(
        [ref[frame, :, :, lanes].reshape(-1, WINDOW) for ref in refs], axis=0
    )


def read_row(refs, row, lanes):
    return jnp.concatenate([ref[:, row, :, lanes].reshape(-1, WINDOW) for ref in refs], axis=0)


def spatial_weigh_kernel(blocks, space, index_ref, lists_ref, q_ref, *refs):
    k_refs, weights_ref, inverse_ref = refs[:blocks], refs[blocks], refs[blocks + 1]
    frames, rows, columns, channels = q_ref.shape
    index = index_ref[0]
    key_rows = []
    for distance in range(blocks // 2 + 1):
        for parity in range(2 if distance else 1):
            owner = partner_of(index, distance, parity) if distance else index
            first = jnp.where((owner >= 0) & (owner < space), owner * rows, -(2**20))
            row = lax.broadcasted_iota(jnp.int32, (columns, rows * columns), 1) // columns
            key_rows.append(row + first)
    key_rows = jnp.concatenate(key_rows, axis=1)
    bias = []
    for row in range(rows):
        query_row = index * rows + row
        member = key_rows == query_row
        for entry in range(lists_ref.shape[0]):
            member = member | (key_rows == lists_ref[entry, query_row])
        bias.append(jnp.where(member & (key_rows >= 0), 0.0, big_negative))
    bias = jnp.concatenate(bias + bias, axis=0)
    for frame in range(frames):
        for pair in range(channels // PAIR):
            lanes = window_of(pair)
            weights_ref[frame, pair], inverse_ref[frame, pair] = weigh_pair(
                pair, read_tokens([q_ref], frame, lanes), read_tokens(k_refs, frame, lanes), bias
            )


def spatial_blend_kernel(blocks, weights_ref, inverse_ref, *refs):
    v_refs, out_ref = refs[:blocks], refs[blocks]
    frames, rows, columns, channels = out_ref.shape
    for frame in range(frames):

        def write(lanes, value):
            out_ref[frame, :, :, lanes] = value.reshape(rows, columns, LANES)

        blend_pairs(
            channels // PAIR,
            lambda pair: weights_ref[frame, pair],
            lambda pair: inverse_ref[frame, pair],
            lambda lanes: read_tokens(v_refs, frame, lanes),
            write,
        )


def temporal_weigh_kernel(blocks, q_ref, *refs):
    k_refs, weights_ref, inverse_ref = refs[:blocks], refs[blocks], refs[blocks + 1]
    frames, rows, columns, channels = q_ref.shape
    shape = (2 * frames * columns, blocks * frames * columns)
    own = lax.broadcasted_iota(jnp.int32, shape, 0) % columns
    other = lax.broadcasted_iota(jnp.int32, shape, 1) % columns
    bias = jnp.where(own == other, 0.0, big_negative)
    for row in range(rows):
        for pair in range(channels // PAIR):
            lanes = window_of(pair)
            weights_ref[row, pair], inverse_ref[row, pair] = weigh_pair(
                pair, read_row([q_ref], row, lanes), read_row(k_refs, row, lanes), bias
            )


def temporal_blend_kernel(blocks, weights_ref, inverse_ref, *refs):
    v_refs, out_ref = refs[:blocks], refs[blocks]
    frames, rows, columns, channels = out_ref.shape
    for row in range(rows):

        def write(lanes, value):
            out_ref[:, row, :, lanes] = value.reshape(frames, columns, LANES)

        blend_pairs(
            channels // PAIR,
            lambda pair: weights_ref[row, pair],
            lambda pair: inverse_ref[row, pair],
            lambda lanes: read_row(v_refs, row, lanes),
            write,
        )


def call(kernel, name, out_shape, scalars, arrays, flops):
    in_vmem = pl.BlockSpec(memory_space=pltpu.VMEM)
    in_smem = pl.BlockSpec(memory_space=pltpu.SMEM)
    return pl.pallas_call(
        kernel,
        out_shape=out_shape,
        in_specs=[in_smem] * len(scalars) + [in_vmem] * len(arrays),
        out_specs=jax.tree.map(lambda _: in_vmem, out_shape),
        compiler_params=pltpu.CompilerParams(vmem_limit_bytes=40 * 1024 * 1024),
        cost_estimate=pl.CostEstimate(
            flops=flops, bytes_accessed=sum(2 * a.size for a in arrays), transcendentals=0
        ),
        name=name,
    )(*scalars, *arrays)


def weigh_shapes(groups, channels, queries, keys):
    pairs = channels // PAIR
    return (
        jax.ShapeDtypeStruct((groups, pairs, 2 * queries, keys), jnp.bfloat16),
        jax.ShapeDtypeStruct((groups, pairs, queries, WINDOW), jnp.float32),
    )


def on_device(spatial_q, spatial_k, spatial_v, temporal_q, temporal_k, temporal_v, key_lists):
    frames, rows, columns, channels = spatial_q.shape
    space = lax.axis_size("space")
    reach = -(-(key_lists.shape[1] // 2) // rows)
    index = lax.axis_index("space").reshape(1)
    out_shape = jax.ShapeDtypeStruct(spatial_q.shape, jnp.bfloat16)
    tokens = frames * rows * columns

    def halo(value):
        return [value] + [
            exchanged(value, "space", distance, parity)
            for distance in range(1, reach + 1)
            for parity in range(2)
        ]

    temporal_keys = gathered(temporal_k, "tm")
    spatial_keys = halo(spatial_k)
    temporal_values = gathered(temporal_v, "tm")
    spatial_values = halo(spatial_v)

    blocks = len(spatial_keys)
    keys = blocks * rows * columns
    flops = 2 * tokens * keys * channels
    weights, inverse = call(
        functools.partial(spatial_weigh_kernel, blocks, space),
        "spatial_weigh",
        weigh_shapes(frames, channels, rows * columns, keys),
        [index, key_lists.T],
        [spatial_q, *spatial_keys],
        flops,
    )
    spatial_out = call(
        functools.partial(spatial_blend_kernel, blocks),
        "spatial_blend",
        out_shape,
        [],
        [weights, inverse, *spatial_values],
        flops,
    )
    blocks = len(temporal_keys)
    keys = blocks * frames * columns
    flops = 2 * tokens * keys * channels
    weights, inverse = call(
        functools.partial(temporal_weigh_kernel, blocks),
        "temporal_weigh",
        weigh_shapes(rows, channels, frames * columns, keys),
        [],
        [temporal_q, *temporal_keys],
        flops,
    )
    temporal_out = call(
        functools.partial(temporal_blend_kernel, blocks),
        "temporal_blend",
        out_shape,
        [],
        [weights, inverse, *temporal_values],
        flops,
    )
    return (spatial_out, temporal_out)


def solution(mesh):
    placed = P(("video", "tm"), "space", None, None)
    return jax.shard_map(
        on_device,
        mesh=mesh,
        in_specs=(placed,) * 6 + (P(),),
        out_specs=(placed, placed),
        check_vma=False,
    )
```

time: 41.1 us -> 29.3 us (0.71)
  the two profiles are of different devices: /device:TPU:0 before, /device:TPU:9 now
where the time goes in v2:
time: 29.3 us; the launch traced here: 29 us
  starting transfers between devices  16.1 us (55%)
  Pallas kernels  5.06 us (17%)
  waiting for transfers between devices  4.46 us (15%)
  local copies, waits for them, and re-layouts  2.63 us (9%)
  between operations  0.76 us (3%)
    ppermute x6, starting transfers between devices, gathered(): held.extend([lax.ppermute(part, axis, pairs) for part in held])  8.35 us
    ppermute x4, starting transfers between devices, exchanged(): return lax.ppermute(value, axis, pairs)  7.74 us
    pallas_call x4, Pallas kernels, call(): pl.pallas_call(kernel, out_shape=out_shape, in_specs=[in_smem] * len(scal...  5.06 us
    unnamed x14, local copies, waits for them, and re-layouts  2.63 us
    ppermute x6, waiting for transfers between devices, gathered(): held.extend([lax.ppermute(part, axis, pairs) for part in held])  2.4 us
    ppermute x4, waiting for transfers between devices, exchanged(): return lax.ppermute(value, axis, pairs)  2.06 us
  transfers between devices with their start and end apart: 10, of which 2 were waited for; matrix products, arithmetic and copies ran while one was open for 0% of the time, Pallas kernels for 13%

profile of v2, /device:TPU:9, one launch (start us, length us, event | category | flops | bytes accessed | tf_op | source)
XLA Modules:
  0.0 29.0 jit_solution(1879898435252397747)
XLA Ops:
  0.6 0.1 collective-permute-start
  0.7 4.5 %collective-permute-start.1 = (bf16[2,4,16,1152]{3,2,1,0:T(8,128)(2,1)}, bf16[2,4,16,1152]{3,2,1,0:T(8,128)(2,1)S(1)}, u32[]{:S(2)}, u32[]{:S(2)}) collective-permute-start(bf16[2,4,16,1152]{3,2,1,0:T(8,128)(2,1)} %refs_0_.4), channel_id=1, source_target_pairs={{0,0},{4,8},{8,4},{12,12},{1,1},{5,9},{9,5},{13,13},{2,2},{6,10},{... | collective-permute-start | bytes 884744 | tf_op jit(solution)/shard_map/ppermute | solution.py:32
  5.2 1.3 %collective-permute-start.4 = (bf16[2,4,16,1152]{3,2,1,0:T(8,128)(2,1)}, bf16[2,4,16,1152]{3,2,1,0:T(8,128)(2,1)S(1)}, u32[]{:S(2)}, u32[]{:S(2)}) collective-permute-start(bf16[2,4,16,1152]{3,2,1,0:T(8,128)(2,1)} %refs_0_.6), channel_id=1, source_target_pairs={{0,2},{1,3},{2,0},{3,1},{4,6},{5,7},{6,4},{7,5},{8,10},{9,11},{10,... | collective-permute-start | bytes 884744 | tf_op jit(solution)/shard_map/ppermute | solution.py:41
  6.5 0.0 collective-permute-start.2
  6.5 0.3 collective-permute-start.7
  6.7 2.1 %collective-permute-done.refs_1_ = bf16[2,4,16,1152]{3,2,1,0:T(8,128)(2,1)S(1)} collective-permute-done((bf16[2,4,16,1152]{3,2,1,0:T(8,128)(2,1)}, bf16[2,4,16,1152]{3,2,1,0:T(8,128)(2,1)S(1)}, u32[]{:S(2)}, u32[]{:S(2)}) %collective-permute-start) | collective-permute-done | bytes 294944 | tf_op jit(solution)/shard_map/ppermute | solution.py:32
  8.8 3.2 %collective-permute-start.3 = (bf16[2,4,16,1152]{3,2,1,0:T(8,128)(2,1)}, bf16[2,4,16,1152]{3,2,1,0:T(8,128)(2,1)S(1)}, u32[]{:S(2)}, u32[]{:S(2)}) collective-permute-start(bf16[2,4,16,1152]{3,2,1,0:T(8,128)(2,1)} %refs_0_.5), channel_id=1, source_target_pairs={{0,0},{4,8},{8,4},{12,12},{1,1},{5,9},{9,5},{13,13},{2,2},{6,10},{... | collective-permute-start | bytes 884744 | tf_op jit(solution)/shard_map/ppermute | solution.py:32
  12.0 0.0 collective-permute-done.1.refs_2_
  12.0 3.0 %collective-permute-start.5 = (bf16[2,4,16,1152]{3,2,1,0:T(8,128)(2,1)}, bf16[2,4,16,1152]{3,2,1,0:T(8,128)(2,1)S(1)}, u32[]{:S(2)}, u32[]{:S(2)}) collective-permute-start(bf16[2,4,16,1152]{3,2,1,0:T(8,128)(2,1)} %refs_0_.6), channel_id=1, source_target_pairs={{0,1},{1,0},{2,3},{3,2},{4,5},{5,4},{6,7},{7,6},{8,9},{9,8},{10,11... | collective-permute-start | bytes 884744 | tf_op jit(solution)/shard_map/ppermute | solution.py:41
  15.0 0.0 collective-permute-done.4.refs_1_
  15.0 1.6 %collective-permute-start.6 = (bf16[2,4,16,1152]{3,2,1,0:T(8,128)(2,1)S(1)}, bf16[2,4,16,1152]{3,2,1,0:T(8,128)(2,1)S(1)}, u32[]{:S(2)}, u32[]{:S(2)}) collective-permute-start(bf16[2,4,16,1152]{3,2,1,0:T(8,128)(2,1)S(1)} %collective-permute-done.4.refs_1_), channel_id=1, source_target_pairs={{0,1},{1,0},{2,3},{3,2},{4,5},{5,4},{6,7},{7,6},{8,9},{9,8},{10,11... | collective-permute-start | bytes 884744 | tf_op jit(solution)/shard_map/ppermute | solution.py:41
  16.7 0.0 collective-permute-done.2.refs_1_
  16.7 0.0 collective-permute-start.8
  16.7 2.4 %collective-permute-done.7.refs_1_ = bf16[2,4,16,1152]{3,2,1,0:T(8,128)(2,1)S(1)} collective-permute-done((bf16[2,4,16,1152]{3,2,1,0:T(8,128)(2,1)}, bf16[2,4,16,1152]{3,2,1,0:T(8,128)(2,1)S(1)}, u32[]{:S(2)}, u32[]{:S(2)}) %collective-permute-start.7) | collective-permute-done | bytes 294944 | tf_op jit(solution)/shard_map/ppermute | solution.py:41
  19.1 2.2 %collective-permute-start.9 = (bf16[2,4,16,1152]{3,2,1,0:T(8,128)(2,1)S(1)}, bf16[2,4,16,1152]{3,2,1,0:T(8,128)(2,1)S(1)}, u32[]{:S(2)}, u32[]{:S(2)}) collective-permute-start(bf16[2,4,16,1152]{3,2,1,0:T(8,128)(2,1)S(1)} %collective-permute-done.7.refs_1_), channel_id=1, source_target_pairs={{0,1},{1,0},{2,3},{3,2},{4,5},{5,4},{6,7},{7,6},{8,9},{9,8},{10,11... | collective-permute-start | bytes 884744 | tf_op jit(solution)/shard_map/ppermute | solution.py:41
  21.2 0.0 copy-start.6
  21.2 0.7 %copy-done.6 = s32[16,8]{0,1:T(8,128)S(1)} copy-done((s32[16,8]{0,1:T(8,128)S(1)}, s32[16,8]{0,1:T(8,128)}, u32[]{:S(2)}) %copy-start.6) | copy-done | bytes 536
  21.9 0.0 copy-start.2
  21.9 1.0 %copy-done.2 = bf16[2,4,16,1152]{3,2,1,0:T(8,128)(2,1)S(1)} copy-done((bf16[2,4,16,1152]{3,2,1,0:T(8,128)(2,1)S(1)}, bf16[2,4,16,1152]{3,2,1,0:T(8,128)(2,1)}, u32[]{:S(2)}) %copy-start.2) | copy-done | bytes 294936
  22.9 0.0 copy-start.3
  22.9 1.0 %copy-done.3 = bf16[2,4,16,1152]{3,2,1,0:T(8,128)(2,1)S(1)} copy-done((bf16[2,4,16,1152]{3,2,1,0:T(8,128)(2,1)S(1)}, bf16[2,4,16,1152]{3,2,1,0:T(8,128)(2,1)}, u32[]{:S(2)}) %copy-start.3) | copy-done | bytes 294936
  23.8 0.0 copy-start
  23.8 1.7 %spatial_weigh.1 = (bf16[2,8,128,192]{3,2,1,0:T(8,128)(2,1)S(1)}, f32[2,8,64,256]{3,2,1,0:T(8,128)S(1)}) custom-call(s32[1]{0:T(128)} %bitcast.index_ref, s32[8,16]{1,0:T(8,128)S(1)} %bitcast.2, bf16[2,4,16,1152]{3,2,1,0:T(8,128)(2,1)S(1)} %copy-done.2, bf16[2,4,16,1152]{3,2,1,0:T(8,128)(2,1)S(1)} %copy-done.3, ...), custom_call_target="tpu_custom_call" | custom-call | flops 56623104 | bytes 1179648 | tf_op jit(solution)/shard_map/spatial_weigh/pallas_call | solution.py:184
  25.5 0.0 collective-permute-done.3.refs_2_
  25.5 0.0 copy-done
  25.5 0.0 copy-start.4
  25.6 0.0 copy-start.5
  25.6 1.2 %spatial_blend.1 = bf16[2,4,16,1152]{3,2,1,0:T(8,128)(2,1)} custom-call(bf16[2,8,128,192]{3,2,1,0:T(8,128)(2,1)S(1)} %get-tuple-element.6.weights_ref, f32[2,8,64,256]{3,2,1,0:T(8,128)S(1)} %get-tuple-element.7.inverse_ref, bf16[2,4,16,1152]{3,2,1,0:T(8,128)(2,1)S(1)} %copy-done, bf16[2,4,16,1152]{3,2,1,0:T(8,128)(2,1)S(1)} %collective-permute-done.2.refs_1_, ...), custom_call_target="tpu_custom_call" | custom-call | flops 56623104 | bytes 2195456 | tf_op jit(solution)/shard_map/spatial_blend/pallas_call | solution.py:184
  26.8 0.0 copy-start.1
  26.8 0.0 collective-permute-done.5.refs_2_
  26.8 0.0 collective-permute-done.6.refs_3_
  26.8 0.0 copy-done.4
  26.8 0.0 copy-done.5
  26.8 1.0 %temporal_weigh.1 = (bf16[4,8,64,128]{3,2,1,0:T(8,128)(2,1)S(1)}, f32[4,8,32,256]{3,2,1,0:T(8,128)S(1)}) custom-call(bf16[2,4,16,1152]{3,2,1,0:T(8,128)(2,1)S(1)} %copy-done.4, bf16[2,4,16,1152]{3,2,1,0:T(8,128)(2,1)S(1)} %copy-done.5, bf16[2,4,16,1152]{3,2,1,0:T(8,128)(2,1)S(1)} %collective-permute-done.4.refs_1_, ...), custom_call_target="tpu_custom_call" | custom-call | flops 37748736 | bytes 1474560 | tf_op jit(solution)/shard_map/temporal_weigh/pallas_call | solution.py:184
  27.8 0.0 collective-permute-done.8.refs_2_
  27.8 0.0 collective-permute-done.9.refs_3_
  27.8 0.0 copy-done.1
  27.9 1.2 %temporal_blend.1 = bf16[2,4,16,1152]{3,2,1,0:T(8,128)(2,1)} custom-call(bf16[4,8,64,128]{3,2,1,0:T(8,128)(2,1)S(1)} %get-tuple-element.8.weights_ref, f32[4,8,32,256]{3,2,1,0:T(8,128)S(1)} %get-tuple-element.9.inverse_ref, bf16[2,4,16,1152]{3,2,1,0:T(8,128)(2,1)S(1)} %copy-done.1, bf16[2,4,16,1152]{3,2,1,0:T(8,128)(2,1)S(1)} %collective-permute-done.7.refs_1_, ...), custom_call_target="tpu_custom_call" | custom-call | flops 37748736 | bytes 2228224 | tf_op jit(solution)/shard_map/temporal_blend/pallas_call | solution.py:184
Async XLA Ops:
  0.6 8.2 %collective-permute-start = (bf16[2,4,16,1152]{3,2,1,0:T(8,128)(2,1)}, bf16[2,4,16,1152]{3,2,1,0:T(8,128)(2,1)S(1)}, u32[]{:S(2)}, u32[]{:S(2)}) collective-permute-start(bf16[2,4,16,1152]{3,2,1,0:T(8,128)(2,1)} %refs_0_.4), channel_id=1, source_target_pairs={{0,4},{4,0},{8,12},{12,8},{1,5},{5,1},{9,13},{13,9},{2,6},{6,2},{1... | collective-permute-start | bytes 884744 | tf_op jit(solution)/shard_map/ppermute | solution.py:32
  0.7 11.3 %collective-permute-start.1 = (bf16[2,4,16,1152]{3,2,1,0:T(8,128)(2,1)}, bf16[2,4,16,1152]{3,2,1,0:T(8,128)(2,1)S(1)}, u32[]{:S(2)}, u32[]{:S(2)}) collective-permute-start(bf16[2,4,16,1152]{3,2,1,0:T(8,128)(2,1)} %refs_0_.4), channel_id=1, source_target_pairs={{0,0},{4,8},{8,4},{12,12},{1,1},{5,9},{9,5},{13,13},{2,2},{6,10},{... | collective-permute-start | bytes 884744 | tf_op jit(solution)/shard_map/ppermute | solution.py:32
  5.2 9.8 %collective-permute-start.4 = (bf16[2,4,16,1152]{3,2,1,0:T(8,128)(2,1)}, bf16[2,4,16,1152]{3,2,1,0:T(8,128)(2,1)S(1)}, u32[]{:S(2)}, u32[]{:S(2)}) collective-permute-start(bf16[2,4,16,1152]{3,2,1,0:T(8,128)(2,1)} %refs_0_.6), channel_id=1, source_target_pairs={{0,2},{1,3},{2,0},{3,1},{4,6},{5,7},{6,4},{7,5},{8,10},{9,11},{10,... | collective-permute-start | bytes 884744 | tf_op jit(solution)/shard_map/ppermute | solution.py:41
  6.5 10.2 %collective-permute-start.2 = (bf16[2,4,16,1152]{3,2,1,0:T(8,128)(2,1)}, bf16[2,4,16,1152]{3,2,1,0:T(8,128)(2,1)S(1)}, u32[]{:S(2)}, u32[]{:S(2)}) collective-permute-start(bf16[2,4,16,1152]{3,2,1,0:T(8,128)(2,1)} %refs_0_.5), channel_id=1, source_target_pairs={{0,4},{4,0},{8,12},{12,8},{1,5},{5,1},{9,13},{13,9},{2,6},{6,2},{1... | collective-permute-start | bytes 884744 | tf_op jit(solution)/shard_map/ppermute | solution.py:32
  6.5 12.6 %collective-permute-start.7 = (bf16[2,4,16,1152]{3,2,1,0:T(8,128)(2,1)}, bf16[2,4,16,1152]{3,2,1,0:T(8,128)(2,1)S(1)}, u32[]{:S(2)}, u32[]{:S(2)}) collective-permute-start(bf16[2,4,16,1152]{3,2,1,0:T(8,128)(2,1)} %refs_0_.7), channel_id=1, source_target_pairs={{0,2},{1,3},{2,0},{3,1},{4,6},{5,7},{6,4},{7,5},{8,10},{9,11},{10,... | collective-permute-start | bytes 884744 | tf_op jit(solution)/shard_map/ppermute | solution.py:41
  8.8 16.7 %collective-permute-start.3 = (bf16[2,4,16,1152]{3,2,1,0:T(8,128)(2,1)}, bf16[2,4,16,1152]{3,2,1,0:T(8,128)(2,1)S(1)}, u32[]{:S(2)}, u32[]{:S(2)}) collective-permute-start(bf16[2,4,16,1152]{3,2,1,0:T(8,128)(2,1)} %refs_0_.5), channel_id=1, source_target_pairs={{0,0},{4,8},{8,4},{12,12},{1,1},{5,9},{9,5},{13,13},{2,2},{6,10},{... | collective-permute-start | bytes 884744 | tf_op jit(solution)/shard_map/ppermute | solution.py:32
  12.0 14.8 %collective-permute-start.5 = (bf16[2,4,16,1152]{3,2,1,0:T(8,128)(2,1)}, bf16[2,4,16,1152]{3,2,1,0:T(8,128)(2,1)S(1)}, u32[]{:S(2)}, u32[]{:S(2)}) collective-permute-start(bf16[2,4,16,1152]{3,2,1,0:T(8,128)(2,1)} %refs_0_.6), channel_id=1, source_target_pairs={{0,1},{1,0},{2,3},{3,2},{4,5},{5,4},{6,7},{7,6},{8,9},{9,8},{10,11... | collective-permute-start | bytes 884744 | tf_op jit(solution)/shard_map/ppermute | solution.py:41
  15.0 11.7 %collective-permute-start.6 = (bf16[2,4,16,1152]{3,2,1,0:T(8,128)(2,1)S(1)}, bf16[2,4,16,1152]{3,2,1,0:T(8,128)(2,1)S(1)}, u32[]{:S(2)}, u32[]{:S(2)}) collective-permute-start(bf16[2,4,16,1152]{3,2,1,0:T(8,128)(2,1)S(1)} %collective-permute-done.4.refs_1_), channel_id=1, source_target_pairs={{0,1},{1,0},{2,3},{3,2},{4,5},{5,4},{6,7},{7,6},{8,9},{9,8},{10,11... | collective-permute-start | bytes 884744 | tf_op jit(solution)/shard_map/ppermute | solution.py:41
  16.7 11.2 %collective-permute-start.8 = (bf16[2,4,16,1152]{3,2,1,0:T(8,128)(2,1)}, bf16[2,4,16,1152]{3,2,1,0:T(8,128)(2,1)S(1)}, u32[]{:S(2)}, u32[]{:S(2)}) collective-permute-start(bf16[2,4,16,1152]{3,2,1,0:T(8,128)(2,1)} %refs_0_.7), channel_id=1, source_target_pairs={{0,1},{1,0},{2,3},{3,2},{4,5},{5,4},{6,7},{7,6},{8,9},{9,8},{10,11... | collective-permute-start | bytes 884744 | tf_op jit(solution)/shard_map/ppermute | solution.py:41
  19.1 8.8 %collective-permute-start.9 = (bf16[2,4,16,1152]{3,2,1,0:T(8,128)(2,1)S(1)}, bf16[2,4,16,1152]{3,2,1,0:T(8,128)(2,1)S(1)}, u32[]{:S(2)}, u32[]{:S(2)}) collective-permute-start(bf16[2,4,16,1152]{3,2,1,0:T(8,128)(2,1)S(1)} %collective-permute-done.7.refs_1_), channel_id=1, source_target_pairs={{0,1},{1,0},{2,3},{3,2},{4,5},{5,4},{6,7},{7,6},{8,9},{9,8},{10,11... | collective-permute-start | bytes 884744 | tf_op jit(solution)/shard_map/ppermute | solution.py:41
  21.2 0.7 %copy-start.6 = (s32[16,8]{0,1:T(8,128)S(1)}, s32[16,8]{0,1:T(8,128)}, u32[]{:S(2)}) copy-start(s32[16,8]{0,1:T(8,128)} %param.13) | copy-start | bytes 1540
  21.9 1.0 %copy-start.2 = (bf16[2,4,16,1152]{3,2,1,0:T(8,128)(2,1)S(1)}, bf16[2,4,16,1152]{3,2,1,0:T(8,128)(2,1)}, u32[]{:S(2)}) copy-start(bf16[2,4,16,1152]{3,2,1,0:T(8,128)(2,1)} %q_ref.2) | copy-start | bytes 884740
  22.9 1.0 %copy-start.3 = (bf16[2,4,16,1152]{3,2,1,0:T(8,128)(2,1)S(1)}, bf16[2,4,16,1152]{3,2,1,0:T(8,128)(2,1)}, u32[]{:S(2)}) copy-start(bf16[2,4,16,1152]{3,2,1,0:T(8,128)(2,1)} %refs_0_.4) | copy-start | bytes 884740
  23.8 1.7 %copy-start = (bf16[2,4,16,1152]{3,2,1,0:T(8,128)(2,1)S(1)}, bf16[2,4,16,1152]{3,2,1,0:T(8,128)(2,1)}, u32[]{:S(2)}) copy-start(bf16[2,4,16,1152]{3,2,1,0:T(8,128)(2,1)} %refs_0_.5) | copy-start | bytes 884740
  25.5 1.2 %copy-start.4 = (bf16[2,4,16,1152]{3,2,1,0:T(8,128)(2,1)S(1)}, bf16[2,4,16,1152]{3,2,1,0:T(8,128)(2,1)}, u32[]{:S(2)}) copy-start(bf16[2,4,16,1152]{3,2,1,0:T(8,128)(2,1)} %q_ref.3) | copy-start | bytes 884740
  25.6 1.2 %copy-start.5 = (bf16[2,4,16,1152]{3,2,1,0:T(8,128)(2,1)S(1)}, bf16[2,4,16,1152]{3,2,1,0:T(8,128)(2,1)}, u32[]{:S(2)}) copy-start(bf16[2,4,16,1152]{3,2,1,0:T(8,128)(2,1)} %refs_0_.6) | copy-start | bytes 884740
  26.8 1.1 %copy-start.1 = (bf16[2,4,16,1152]{3,2,1,0:T(8,128)(2,1)S(1)}, bf16[2,4,16,1152]{3,2,1,0:T(8,128)(2,1)}, u32[]{:S(2)}) copy-start(bf16[2,4,16,1152]{3,2,1,0:T(8,128)(2,1)} %refs_0_.7) | copy-start | bytes 884740

commit v3 on v2

--- a/solution.py
+++ b/solution.py
@@ -33,14 +33,7 @@
 
 
 def gathered(value, axis):
-    length = lax.axis_size(axis)
-    held = [value]
-    step = length // 2
-    while step:
-        pairs = [(i, i ^ step) for i in range(length)]
-        held.extend([lax.ppermute(part, axis, pairs) for part in held])
-        step //= 2
-    return held
+    return [lax.all_gather(value, axis, axis=0, tiled=True)]
 
 
 def head_masks(pair, rows):
@@ -149,7 +142,7 @@
 def temporal_weigh_kernel(blocks, q_ref, *refs):
     k_refs, weights_ref, inverse_ref = refs[:blocks], refs[blocks], refs[blocks + 1]
     frames, rows, columns, channels = q_ref.shape
-    shape = (2 * frames * columns, blocks * frames * columns)
+    shape = (2 * frames * columns, blocks * k_refs[0].shape[0] * columns)
     own = lax.broadcasted_iota(jnp.int32, shape, 0) % columns
     other = lax.broadcasted_iota(jnp.int32, shape, 1) % columns
     bias = jnp.where(own == other, 0.0, big_negative)
@@ -242,7 +235,7 @@
         flops,
     )
     blocks = len(temporal_keys)
-    keys = blocks * frames * columns
+    keys = temporal_keys[0].shape[0] * columns
     flops = 2 * tokens * keys * channels
     weights, inverse = call(
         functools.partial(temporal_weigh_kernel, blocks),

time: 29.3 us -> 58.4 us (1.99)
  the two profiles are of different devices: /device:TPU:9 before, /device:TPU:0 now
where the time goes in v3:
time: 58.4 us; the launch traced here: 58.1 us
  waiting for transfers between devices  23.9 us (41%)
  between operations  14.1 us (24%)
  starting transfers between devices  9.9 us (17%)
  local copies, waits for them, and re-layouts  5.16 us (9%)
  Pallas kernels  5.05 us (9%)
    all_gather x2, waiting for transfers between devices, gathered(): return [lax.all_gather(value, axis, axis=0, tiled=True)]  20 us
    ppermute x4, starting transfers between devices, exchanged(): return lax.ppermute(value, axis, pairs)  9.83 us
    unnamed x14, local copies, waits for them, and re-layouts  5.16 us
    pallas_call x4, Pallas kernels, call(): pl.pallas_call(kernel, out_shape=out_shape, in_specs=[in_smem] * len(scal...  5.05 us
    ppermute x4, waiting for transfers between devices, exchanged(): return lax.ppermute(value, axis, pairs)  2.5 us
    unnamed x2, waiting for transfers between devices  1.38 us
  transfers between devices with their start and end apart: 6, of which 4 were waited for; matrix products, arithmetic and copies ran while one was open for 0% of the time, Pallas kernels for 7%

profile of v3, /device:TPU:0, one launch (start us, length us, event | category | flops | bytes accessed | tf_op | source)
XLA Modules:
  0.0 58.1 jit_solution(9206197762521656833)
XLA Ops:
  7.2 0.0 copy-start.2
  7.2 0.0 all-gather.3.cloned.1.call-start
  7.2 0.7 %all-gather.3.cloned.1.call-update = ((bf16[2,4,16,1152]{3,2,1,0:T(8,128)(2,1)}), bf16[8,4,16,1152]{3,2,1,0:T(8,128)(2,1)}) async-update(((), (), s32[]{:S(2)}) %all-gather.3.cloned.1.call-start, bf16[2,4,16,1152]{3,2,1,0:T(8,128)(2,1)} %param.11) | async-update | bytes 1769496
  7.9 0.0 all-gather.5.cloned.1.call-start
  8.0 0.7 %all-gather.5.cloned.1.call-update = ((bf16[2,4,16,1152]{3,2,1,0:T(8,128)(2,1)}), bf16[8,4,16,1152]{3,2,1,0:T(8,128)(2,1)}) async-update(((), (), s32[]{:S(2)}) %all-gather.5.cloned.1.call-start, bf16[2,4,16,1152]{3,2,1,0:T(8,128)(2,1)} %param.12) | async-update | bytes 1769496
  8.7 3.1 %collective-permute-start = (bf16[2,4,16,1152]{3,2,1,0:T(8,128)(2,1)}, bf16[2,4,16,1152]{3,2,1,0:T(8,128)(2,1)S(1)}, u32[]{:S(2)}, u32[]{:S(2)}) collective-permute-start(bf16[2,4,16,1152]{3,2,1,0:T(8,128)(2,1)} %refs_0_.2), channel_id=1, source_target_pairs={{0,4},{4,0},{8,12},{12,8},{1,5},{5,1},{9,13},{13,9},{2,6},{6,2},{1... | collective-permute-start | bytes 884744 | tf_op jit(solution)/shard_map/ppermute | solution.py:32
  11.7 1.6 %collective-permute-start.1 = (bf16[2,4,16,1152]{3,2,1,0:T(8,128)(2,1)}, bf16[2,4,16,1152]{3,2,1,0:T(8,128)(2,1)S(1)}, u32[]{:S(2)}, u32[]{:S(2)}) collective-permute-start(bf16[2,4,16,1152]{3,2,1,0:T(8,128)(2,1)} %refs_0_.2), channel_id=1, source_target_pairs={{0,0},{4,8},{8,4},{12,12},{1,1},{5,9},{9,5},{13,13},{2,2},{6,10},{... | collective-permute-start | bytes 884744 | tf_op jit(solution)/shard_map/ppermute | solution.py:32
  13.4 3.5 %collective-permute-start.2 = (bf16[2,4,16,1152]{3,2,1,0:T(8,128)(2,1)}, bf16[2,4,16,1152]{3,2,1,0:T(8,128)(2,1)S(1)}, u32[]{:S(2)}, u32[]{:S(2)}) collective-permute-start(bf16[2,4,16,1152]{3,2,1,0:T(8,128)(2,1)} %refs_0_.3), channel_id=1, source_target_pairs={{0,4},{4,0},{8,12},{12,8},{1,5},{5,1},{9,13},{13,9},{2,6},{6,2},{1... | collective-permute-start | bytes 884744 | tf_op jit(solution)/shard_map/ppermute | solution.py:32
  16.9 1.6 %collective-permute-start.3 = (bf16[2,4,16,1152]{3,2,1,0:T(8,128)(2,1)}, bf16[2,4,16,1152]{3,2,1,0:T(8,128)(2,1)S(1)}, u32[]{:S(2)}, u32[]{:S(2)}) collective-permute-start(bf16[2,4,16,1152]{3,2,1,0:T(8,128)(2,1)} %refs_0_.3), channel_id=1, source_target_pairs={{0,0},{4,8},{8,4},{12,12},{1,1},{5,9},{9,5},{13,13},{2,2},{6,10},{... | collective-permute-start | bytes 884744 | tf_op jit(solution)/shard_map/ppermute | solution.py:32
  18.5 1.3 %collective-permute-done.refs_1_ = bf16[2,4,16,1152]{3,2,1,0:T(8,128)(2,1)S(1)} collective-permute-done((bf16[2,4,16,1152]{3,2,1,0:T(8,128)(2,1)}, bf16[2,4,16,1152]{3,2,1,0:T(8,128)(2,1)S(1)}, u32[]{:S(2)}, u32[]{:S(2)}) %collective-permute-start) | collective-permute-done | bytes 294944 | tf_op jit(solution)/shard_map/ppermute | solution.py:32
  19.8 0.0 collective-permute-done.1.refs_2_
  19.8 0.0 copy-start.3
  19.8 1.0 %copy-done.3 = bf16[2,4,16,1152]{3,2,1,0:T(8,128)(2,1)S(1)} copy-done((bf16[2,4,16,1152]{3,2,1,0:T(8,128)(2,1)S(1)}, bf16[2,4,16,1152]{3,2,1,0:T(8,128)(2,1)}, u32[]{:S(2)}) %copy-start.3) | copy-done | bytes 294936
  20.8 0.0 copy-start.4
  20.8 1.0 %copy-done.4 = bf16[2,4,16,1152]{3,2,1,0:T(8,128)(2,1)S(1)} copy-done((bf16[2,4,16,1152]{3,2,1,0:T(8,128)(2,1)S(1)}, bf16[2,4,16,1152]{3,2,1,0:T(8,128)(2,1)}, u32[]{:S(2)}) %copy-start.4) | copy-done | bytes 294936
  21.7 0.0 copy-start.6
  21.7 0.7 %copy-done.6 = s32[16,8]{0,1:T(8,128)S(1)} copy-done((s32[16,8]{0,1:T(8,128)S(1)}, s32[16,8]{0,1:T(8,128)}, u32[]{:S(2)}) %copy-start.6) | copy-done | bytes 536
  22.4 1.7 %spatial_weigh.1 = (bf16[2,8,128,192]{3,2,1,0:T(8,128)(2,1)S(1)}, f32[2,8,64,256]{3,2,1,0:T(8,128)S(1)}) custom-call(s32[1]{0:T(128)} %bitcast.index_ref, s32[8,16]{1,0:T(8,128)S(1)} %bitcast.2, bf16[2,4,16,1152]{3,2,1,0:T(8,128)(2,1)S(1)} %copy-done.3, bf16[2,4,16,1152]{3,2,1,0:T(8,128)(2,1)S(1)} %copy-done.4, ...), custom_call_target="tpu_custom_call" | custom-call | flops 56623104 | bytes 1179648 | tf_op jit(solution)/shard_map/spatial_weigh/pallas_call | solution.py:177
  24.1 1.2 %collective-permute-done.2.refs_1_ = bf16[2,4,16,1152]{3,2,1,0:T(8,128)(2,1)S(1)} collective-permute-done((bf16[2,4,16,1152]{3,2,1,0:T(8,128)(2,1)}, bf16[2,4,16,1152]{3,2,1,0:T(8,128)(2,1)S(1)}, u32[]{:S(2)}, u32[]{:S(2)}) %collective-permute-start.2) | collective-permute-done | bytes 294944 | tf_op jit(solution)/shard_map/ppermute | solution.py:32
  25.3 0.0 collective-permute-done.3.refs_2_
  25.3 0.0 copy-done.2
  25.3 0.0 copy-start.5
  25.3 1.2 %spatial_blend.1 = bf16[2,4,16,1152]{3,2,1,0:T(8,128)(2,1)} custom-call(bf16[2,8,128,192]{3,2,1,0:T(8,128)(2,1)S(1)} %get-tuple-element.6.weights_ref, f32[2,8,64,256]{3,2,1,0:T(8,128)S(1)} %get-tuple-element.7.inverse_ref, bf16[2,4,16,1152]{3,2,1,0:T(8,128)(2,1)S(1)} %copy-done.2, bf16[2,4,16,1152]{3,2,1,0:T(8,128)(2,1)S(1)} %collective-permute-done.2.refs_1_, ...), custom_call_target="tpu_custom_call" | custom-call | flops 56623104 | bytes 2195456 | tf_op jit(solution)/shard_map/spatial_blend/pallas_call | solution.py:177
  26.5 3.3 %all-gather.3.cloned.1.call-done.refs_0_ = bf16[8,4,16,1152]{3,2,1,0:T(8,128)(2,1)} async-done(((bf16[2,4,16,1152]{3,2,1,0:T(8,128)(2,1)}), bf16[8,4,16,1152]{3,2,1,0:T(8,128)(2,1)}) %all-gather.3.cloned.1.call-update) | async-done | bytes 1179664 | tf_op jit(solution)/shard_map/all_gather | solution.py:36
  29.8 0.0 copy-done.5
  29.8 0.0 copy-start
  29.8 1.3 %copy-done = bf16[8,4,16,1152]{3,2,1,0:T(8,128)(2,1)S(1)} copy-done((bf16[8,4,16,1152]{3,2,1,0:T(8,128)(2,1)S(1)}, bf16[8,4,16,1152]{3,2,1,0:T(8,128)(2,1)}, u32[]{:S(2)}) %copy-start) | copy-done | bytes 1179672
  31.0 1.0 %temporal_weigh.1 = (bf16[4,8,64,128]{3,2,1,0:T(8,128)(2,1)S(1)}, f32[4,8,32,256]{3,2,1,0:T(8,128)S(1)}) custom-call(bf16[2,4,16,1152]{3,2,1,0:T(8,128)(2,1)S(1)} %copy-done.5, bf16[8,4,16,1152]{3,2,1,0:T(8,128)(2,1)S(1)} %copy-done), custom_call_target="tpu_custom_call" | custom-call | flops 37748736 | bytes 1474560 | tf_op jit(solution)/shard_map/temporal_weigh/pallas_call | solution.py:177
  32.1 16.7 %all-gather.5.cloned.1.call-done.refs_0_ = bf16[8,4,16,1152]{3,2,1,0:T(8,128)(2,1)} async-done(((bf16[2,4,16,1152]{3,2,1,0:T(8,128)(2,1)}), bf16[8,4,16,1152]{3,2,1,0:T(8,128)(2,1)}) %all-gather.5.cloned.1.call-update) | async-done | bytes 1179664 | tf_op jit(solution)/shard_map/all_gather | solution.py:36
  48.8 0.0 copy-start.1
  48.8 1.3 %copy-done.1 = bf16[8,4,16,1152]{3,2,1,0:T(8,128)(2,1)S(1)} copy-done((bf16[8,4,16,1152]{3,2,1,0:T(8,128)(2,1)S(1)}, bf16[8,4,16,1152]{3,2,1,0:T(8,128)(2,1)}, u32[]{:S(2)}) %copy-start.1) | copy-done | bytes 1179672
  50.1 1.1 %temporal_blend.1 = bf16[2,4,16,1152]{3,2,1,0:T(8,128)(2,1)} custom-call(bf16[4,8,64,128]{3,2,1,0:T(8,128)(2,1)S(1)} %get-tuple-element.8.weights_ref, f32[4,8,32,256]{3,2,1,0:T(8,128)S(1)} %get-tuple-element.9.inverse_ref, bf16[8,4,16,1152]{3,2,1,0:T(8,128)(2,1)S(1)} %copy-done.1), custom_call_target="tpu_custom_call" | custom-call | flops 37748736 | bytes 2228224 | tf_op jit(solution)/shard_map/temporal_blend/pallas_call | solution.py:177
Async XLA Ops:
  7.2 18.1 %copy-start.2 = (bf16[2,4,16,1152]{3,2,1,0:T(8,128)(2,1)S(1)}, bf16[2,4,16,1152]{3,2,1,0:T(8,128)(2,1)}, u32[]{:S(2)}) copy-start(bf16[2,4,16,1152]{3,2,1,0:T(8,128)(2,1)} %refs_0_.3) | copy-start | bytes 884740
  7.2 22.6 %all-gather.3.cloned.1.call-start = ((), (), s32[]{:S(2)}) async-start(), calls=%async_computation | async-start | bytes 1474560 | tf_op jit(solution)/shard_map/all_gather | solution.py:36
  7.9 40.9 %all-gather.5.cloned.1.call-start = ((), (), s32[]{:S(2)}) async-start(), calls=%async_computation.1 | async-start | bytes 1474560 | tf_op jit(solution)/shard_map/all_gather | solution.py:36
  8.7 11.1 %collective-permute-start = (bf16[2,4,16,1152]{3,2,1,0:T(8,128)(2,1)}, bf16[2,4,16,1152]{3,2,1,0:T(8,128)(2,1)S(1)}, u32[]{:S(2)}, u32[]{:S(2)}) collective-permute-start(bf16[2,4,16,1152]{3,2,1,0:T(8,128)(2,1)} %refs_0_.2), channel_id=1, source_target_pairs={{0,4},{4,0},{8,12},{12,8},{1,5},{5,1},{9,13},{13,9},{2,6},{6,2},{1... | collective-permute-start | bytes 884744 | tf_op jit(solution)/shard_map/ppermute | solution.py:32
  11.7 8.0 %collective-permute-start.1 = (bf16[2,4,16,1152]{3,2,1,0:T(8,128)(2,1)}, bf16[2,4,16,1152]{3,2,1,0:T(8,128)(2,1)S(1)}, u32[]{:S(2)}, u32[]{:S(2)}) collective-permute-start(bf16[2,4,16,1152]{3,2,1,0:T(8,128)(2,1)} %refs_0_.2), channel_id=1, source_target_pairs={{0,0},{4,8},{8,4},{12,12},{1,1},{5,9},{9,5},{13,13},{2,2},{6,10},{... | collective-permute-start | bytes 884744 | tf_op jit(solution)/shard_map/ppermute | solution.py:32
  13.4 11.9 %collective-permute-start.2 = (bf16[2,4,16,1152]{3,2,1,0:T(8,128)(2,1)}, bf16[2,4,16,1152]{3,2,1,0:T(8,128)(2,1)S(1)}, u32[]{:S(2)}, u32[]{:S(2)}) collective-permute-start(bf16[2,4,16,1152]{3,2,1,0:T(8,128)(2,1)} %refs_0_.3), channel_id=1, source_target_pairs={{0,4},{4,0},{8,12},{12,8},{1,5},{5,1},{9,13},{13,9},{2,6},{6,2},{1... | collective-permute-start | bytes 884744 | tf_op jit(solution)/shard_map/ppermute | solution.py:32
  16.9 8.4 %collective-permute-start.3 = (bf16[2,4,16,1152]{3,2,1,0:T(8,128)(2,1)}, bf16[2,4,16,1152]{3,2,1,0:T(8,128)(2,1)S(1)}, u32[]{:S(2)}, u32[]{:S(2)}) collective-permute-start(bf16[2,4,16,1152]{3,2,1,0:T(8,128)(2,1)} %refs_0_.3), channel_id=1, source_target_pairs={{0,0},{4,8},{8,4},{12,12},{1,1},{5,9},{9,5},{13,13},{2,2},{6,10},{... | collective-permute-start | bytes 884744 | tf_op jit(solution)/shard_map/ppermute | solution.py:32
  19.8 1.0 %copy-start.3 = (bf16[2,4,16,1152]{3,2,1,0:T(8,128)(2,1)S(1)}, bf16[2,4,16,1152]{3,2,1,0:T(8,128)(2,1)}, u32[]{:S(2)}) copy-start(bf16[2,4,16,1152]{3,2,1,0:T(8,128)(2,1)} %q_ref.2) | copy-start | bytes 884740
  20.8 1.0 %copy-start.4 = (bf16[2,4,16,1152]{3,2,1,0:T(8,128)(2,1)S(1)}, bf16[2,4,16,1152]{3,2,1,0:T(8,128)(2,1)}, u32[]{:S(2)}) copy-start(bf16[2,4,16,1152]{3,2,1,0:T(8,128)(2,1)} %refs_0_.2) | copy-start | bytes 884740
  21.7 0.7 %copy-start.6 = (s32[16,8]{0,1:T(8,128)S(1)}, s32[16,8]{0,1:T(8,128)}, u32[]{:S(2)}) copy-start(s32[16,8]{0,1:T(8,128)} %param.13) | copy-start | bytes 1540
  25.3 4.5 %copy-start.5 = (bf16[2,4,16,1152]{3,2,1,0:T(8,128)(2,1)S(1)}, bf16[2,4,16,1152]{3,2,1,0:T(8,128)(2,1)}, u32[]{:S(2)}) copy-start(bf16[2,4,16,1152]{3,2,1,0:T(8,128)(2,1)} %q_ref.3) | copy-start | bytes 884740
  29.8 1.3 %copy-start = (bf16[8,4,16,1152]{3,2,1,0:T(8,128)(2,1)S(1)}, bf16[8,4,16,1152]{3,2,1,0:T(8,128)(2,1)}, u32[]{:S(2)}) copy-start(bf16[8,4,16,1152]{3,2,1,0:T(8,128)(2,1)} %all-gather.3.cloned.1.call-done.refs_0_) | copy-start | bytes 3538948
  48.8 1.3 %copy-start.1 = (bf16[8,4,16,1152]{3,2,1,0:T(8,128)(2,1)S(1)}, bf16[8,4,16,1152]{3,2,1,0:T(8,128)(2,1)}, u32[]{:S(2)}) copy-start(bf16[8,4,16,1152]{3,2,1,0:T(8,128)(2,1)} %all-gather.5.cloned.1.call-done.refs_0_) | copy-start | bytes 3538948
Sparse Core Ops, SparseCore 0:
  9.6 20.1 all-gather.2
  31.3 17.4 all-gather.4

commit v4 on v3

--- a/solution.py
+++ b/solution.py
@@ -32,8 +32,8 @@
     return lax.ppermute(value, axis, pairs)
 
 
-def gathered(value, axis):
-    return [lax.all_gather(value, axis, axis=0, tiled=True)]
+def swapped(value, axis, step):
+    return lax.ppermute(value, axis, [(i, i ^ step) for i in range(lax.axis_size(axis))])
 
 
 def head_masks(pair, rows):
@@ -95,7 +95,7 @@
 
 
 def spatial_weigh_kernel(blocks, space, index_ref, lists_ref, q_ref, *refs):
-    k_refs, weights_ref, inverse_ref = refs[:blocks], refs[blocks], refs[blocks + 1]
+    k_refs, weights_ref, inverse_ref = refs[:blocks], *refs[-2:]
     frames, rows, columns, channels = q_ref.shape
     index = index_ref[0]
     key_rows = []
@@ -140,9 +140,9 @@
 
 
 def temporal_weigh_kernel(blocks, q_ref, *refs):
-    k_refs, weights_ref, inverse_ref = refs[:blocks], refs[blocks], refs[blocks + 1]
+    k_refs, weights_ref, inverse_ref = refs[:blocks], *refs[-2:]
     frames, rows, columns, channels = q_ref.shape
-    shape = (2 * frames * columns, blocks * k_refs[0].shape[0] * columns)
+    shape = (2 * frames * columns, sum(ref.shape[0] for ref in k_refs) * columns)
     own = lax.broadcasted_iota(jnp.int32, shape, 0) % columns
     other = lax.broadcasted_iota(jnp.int32, shape, 1) % columns
     bias = jnp.where(own == other, 0.0, big_negative)
@@ -171,20 +171,42 @@
         )
 
 
-def call(kernel, name, out_shape, scalars, arrays, flops):
+def call(kernel, name, out_shape, scalars, arrays, flops, others=()):
     in_vmem = pl.BlockSpec(memory_space=pltpu.VMEM)
     in_smem = pl.BlockSpec(memory_space=pltpu.SMEM)
+    anywhere = pl.BlockSpec(memory_space=pl.ANY)
     return pl.pallas_call(
         kernel,
         out_shape=out_shape,
-        in_specs=[in_smem] * len(scalars) + [in_vmem] * len(arrays),
+        in_specs=[in_smem] * len(scalars) + [in_vmem] * len(arrays) + [anywhere] * len(others),
         out_specs=jax.tree.map(lambda _: in_vmem, out_shape),
         compiler_params=pltpu.CompilerParams(vmem_limit_bytes=40 * 1024 * 1024),
         cost_estimate=pl.CostEstimate(
-            flops=flops, bytes_accessed=sum(2 * a.size for a in arrays), transcendentals=0
+            flops=flops, bytes_accessed=1, transcendentals=0
         ),
         name=name,
-    )(*scalars, *arrays)
+    )(*scalars, *arrays, *others)
+
+
+def join_kernel(count, *refs):
+    out_ref = refs[-1]
+    first = 0
+    for ref in refs[:count]:
+        out_ref[first : first + ref.shape[0]] = ref[...]
+        first += ref.shape[0]
+
+
+def joined(arrays, others):
+    shape = (sum(a.shape[0] for a in arrays),) + arrays[0].shape[1:]
+    return call(
+        functools.partial(join_kernel, len(arrays)),
+        "join",
+        jax.ShapeDtypeStruct(shape, arrays[0].dtype),
+        [],
+        arrays,
+        1,
+        others,
+    )
 
 
 def weigh_shapes(groups, channels, queries, keys):
@@ -202,6 +224,7 @@
     index = lax.axis_index("space").reshape(1)
     out_shape = jax.ShapeDtypeStruct(spatial_q.shape, jnp.bfloat16)
     tokens = frames * rows * columns
+    first_step = lax.axis_size("tm") // 2
 
     def halo(value):
         return [value] + [
@@ -210,48 +233,58 @@
             for parity in range(2)
         ]
 
-    temporal_keys = gathered(temporal_k, "tm")
+    def gathered(own, received, others):
+        held, step = [own, received], first_step // 2
+        while step:
+            held = [joined(held, others)]
+            held.append(swapped(held[0], "tm", step))
+            step //= 2
+        return held
+
+    received_keys = swapped(temporal_k, "tm", first_step)
+    received_values = swapped(temporal_v, "tm", first_step)
     spatial_keys = halo(spatial_k)
-    temporal_values = gathered(temporal_v, "tm")
     spatial_values = halo(spatial_v)
 
     blocks = len(spatial_keys)
     keys = blocks * rows * columns
     flops = 2 * tokens * keys * channels
-    weights, inverse = call(
+    spatial_weights, spatial_inverse = call(
         functools.partial(spatial_weigh_kernel, blocks, space),
         "spatial_weigh",
         weigh_shapes(frames, channels, rows * columns, keys),
         [index, key_lists.T],
         [spatial_q, *spatial_keys],
-        flops,
-    )
-    spatial_out = call(
-        functools.partial(spatial_blend_kernel, blocks),
-        "spatial_blend",
-        out_shape,
-        [],
-        [weights, inverse, *spatial_values],
-        flops,
-    )
+        1,
+        [],
+    )
+    temporal_keys = gathered(temporal_k, received_keys, [spatial_weights])
     blocks = len(temporal_keys)
-    keys = temporal_keys[0].shape[0] * columns
-    flops = 2 * tokens * keys * channels
-    weights, inverse = call(
+    keys = sum(k.shape[0] for k in temporal_keys) * columns
+    temporal_weights, temporal_inverse = call(
         functools.partial(temporal_weigh_kernel, blocks),
         "temporal_weigh",
         weigh_shapes(rows, channels, frames * columns, keys),
         [],
         [temporal_q, *temporal_keys],
-        flops,
+        1,
+    )
+    temporal_values = gathered(temporal_v, received_values, [spatial_weights, *spatial_values[1:]])
+    spatial_out = call(
+        functools.partial(spatial_blend_kernel, len(spatial_values)),
+        "spatial_blend",
+        out_shape,
+        [],
+        [spatial_weights, spatial_inverse, *spatial_values],
+        1,
     )
     temporal_out = call(
         functools.partial(temporal_blend_kernel, blocks),
         "temporal_blend",
         out_shape,
         [],
-        [weights, inverse, *temporal_values],
-        flops,
+        [temporal_weights, temporal_inverse, *temporal_values],
+        1,
     )
     return (spatial_out, temporal_out)
 

time: 58.4 us -> 25.1 us (0.43)
  the two profiles are of different devices: /device:TPU:0 before, /device:TPU:13 now
where the time goes in v4:
time: 25.1 us; the launch traced here: 24.8 us
  starting transfers between devices  14.2 us (57%)
  Pallas kernels  5.2 us (21%)
  local copies, waits for them, and re-layouts  2.61 us (10%)
  waiting for transfers between devices  2.07 us (8%)
  between operations  0.76 us (3%)
    ppermute x4, starting transfers between devices, exchanged(): return lax.ppermute(value, axis, pairs)  7.75 us
    ppermute x4, starting transfers between devices, swapped(): lax.ppermute(value, axis, [(i, i ^ step) for i in range(lax.axis_size(axi...  6.41 us
    pallas_call x6, Pallas kernels, call(): pl.pallas_call(kernel, out_shape=out_shape, in_specs=[in_smem] * len(scal...  5.2 us
    unnamed x14, local copies, waits for them, and re-layouts  2.61 us
    ppermute x4, waiting for transfers between devices, exchanged(): return lax.ppermute(value, axis, pairs)  2.06 us
  transfers between devices with their start and end apart: 8, of which 1 were waited for; matrix products, arithmetic and copies ran while one was open for 0% of the time, Pallas kernels for 16%

profile of v4, /device:TPU:13, one launch (start us, length us, event | category | flops | bytes accessed | tf_op | source)
XLA Modules:
  0.0 24.8 jit_solution(17228240753802998432)
XLA Ops:
  0.6 0.2 collective-permute-start
  0.9 4.3 %collective-permute-start.1 = (bf16[2,4,16,1152]{3,2,1,0:T(8,128)(2,1)}, bf16[2,4,16,1152]{3,2,1,0:T(8,128)(2,1)S(1)}, u32[]{:S(2)}, u32[]{:S(2)}) collective-permute-start(bf16[2,4,16,1152]{3,2,1,0:T(8,128)(2,1)} %refs_0_.4), channel_id=1, source_target_pairs={{0,0},{4,8},{8,4},{12,12},{1,1},{5,9},{9,5},{13,13},{2,2},{6,10},{... | collective-permute-start | bytes 884744 | tf_op jit(solution)/shard_map/ppermute | solution.py:32
  5.2 1.3 %collective-permute-start.4 = (bf16[2,4,16,1152]{3,2,1,0:T(8,128)(2,1)}, bf16[2,4,16,1152]{3,2,1,0:T(8,128)(2,1)S(1)}, u32[]{:S(2)}, u32[]{:S(2)}) collective-permute-start(bf16[2,4,16,1152]{3,2,1,0:T(8,128)(2,1)} %refs_0_.6), channel_id=1, source_target_pairs={{0,2},{1,3},{2,0},{3,1},{4,6},{5,7},{6,4},{7,5},{8,10},{9,11},{10,... | collective-permute-start | bytes 884744 | tf_op jit(solution)/shard_map/ppermute | solution.py:36
  6.5 0.3 %collective-permute-start.6 = (bf16[2,4,16,1152]{3,2,1,0:T(8,128)(2,1)}, bf16[2,4,16,1152]{3,2,1,0:T(8,128)(2,1)S(1)}, u32[]{:S(2)}, u32[]{:S(2)}) collective-permute-start(bf16[2,4,16,1152]{3,2,1,0:T(8,128)(2,1)} %refs_0_.7), channel_id=1, source_target_pairs={{0,2},{1,3},{2,0},{3,1},{4,6},{5,7},{6,4},{7,5},{8,10},{9,11},{10,... | collective-permute-start | bytes 884744 | tf_op jit(solution)/shard_map/ppermute | solution.py:36
  6.7 0.0 collective-permute-start.2
  6.7 2.1 %collective-permute-done.refs_1_ = bf16[2,4,16,1152]{3,2,1,0:T(8,128)(2,1)S(1)} collective-permute-done((bf16[2,4,16,1152]{3,2,1,0:T(8,128)(2,1)}, bf16[2,4,16,1152]{3,2,1,0:T(8,128)(2,1)S(1)}, u32[]{:S(2)}, u32[]{:S(2)}) %collective-permute-start) | collective-permute-done | bytes 294944 | tf_op jit(solution)/shard_map/ppermute | solution.py:32
  8.8 3.2 %collective-permute-start.3 = (bf16[2,4,16,1152]{3,2,1,0:T(8,128)(2,1)}, bf16[2,4,16,1152]{3,2,1,0:T(8,128)(2,1)S(1)}, u32[]{:S(2)}, u32[]{:S(2)}) collective-permute-start(bf16[2,4,16,1152]{3,2,1,0:T(8,128)(2,1)} %refs_0_.5), channel_id=1, source_target_pairs={{0,0},{4,8},{8,4},{12,12},{1,1},{5,9},{9,5},{13,13},{2,2},{6,10},{... | collective-permute-start | bytes 884744 | tf_op jit(solution)/shard_map/ppermute | solution.py:32
  12.0 0.0 copy-start.6
  12.0 0.0 collective-permute-done.1.refs_2_
  12.0 0.7 %copy-done.6 = s32[16,8]{0,1:T(8,128)S(1)} copy-done((s32[16,8]{0,1:T(8,128)S(1)}, s32[16,8]{0,1:T(8,128)}, u32[]{:S(2)}) %copy-start.6) | copy-done | bytes 536
  12.7 0.0 copy-start.2
  12.7 1.0 %copy-done.2 = bf16[2,4,16,1152]{3,2,1,0:T(8,128)(2,1)S(1)} copy-done((bf16[2,4,16,1152]{3,2,1,0:T(8,128)(2,1)S(1)}, bf16[2,4,16,1152]{3,2,1,0:T(8,128)(2,1)}, u32[]{:S(2)}) %copy-start.2) | copy-done | bytes 294936
  13.6 0.0 copy-start.3
  13.6 1.0 %copy-done.3 = bf16[2,4,16,1152]{3,2,1,0:T(8,128)(2,1)S(1)} copy-done((bf16[2,4,16,1152]{3,2,1,0:T(8,128)(2,1)S(1)}, bf16[2,4,16,1152]{3,2,1,0:T(8,128)(2,1)}, u32[]{:S(2)}) %copy-start.3) | copy-done | bytes 294936
  14.6 0.0 copy-start
  14.6 1.7 %spatial_weigh.1 = (bf16[2,8,128,192]{3,2,1,0:T(8,128)(2,1)S(1)}, f32[2,8,64,256]{3,2,1,0:T(8,128)S(1)}) custom-call(s32[1]{0:T(128)} %bitcast.index_ref, s32[8,16]{1,0:T(8,128)S(1)} %bitcast.2, bf16[2,4,16,1152]{3,2,1,0:T(8,128)(2,1)S(1)} %copy-done.2, bf16[2,4,16,1152]{3,2,1,0:T(8,128)(2,1)S(1)} %copy-done.3, ...), custom_call_target="tpu_custom_call" | custom-call | flops 1 | bytes 1 | tf_op jit(solution)/shard_map/spatial_weigh/pallas_call | solution.py:178
  16.3 0.0 collective-permute-done.4.refs_1_
  16.3 0.0 copy-done
  16.3 0.0 copy-start.4
  16.4 0.0 copy-start.1
  16.4 3.0 %collective-permute-start.5 = (bf16[4,4,16,1152]{3,2,1,0:T(8,128)(2,1)S(1)}, bf16[4,4,16,1152]{3,2,1,0:T(8,128)(2,1)S(1)}, u32[]{:S(2)}, u32[]{:S(2)}) collective-permute-start(bf16[4,4,16,1152]{3,2,1,0:T(8,128)(2,1)S(1)} %join.2.refs_0_), channel_id=1, source_target_pairs={{0,1},{1,0},{2,3},{3,2},{4,5},{5,4},{6,7},{7,6},{8,9},{9,8},{10,11... | collective-permute-start | bytes 1769480 | tf_op jit(solution)/shard_map/ppermute | solution.py:36
  19.4 0.0 collective-permute-done.6.refs_1_
  19.4 0.0 collective-permute-done.2.refs_1_.refs_3_
  19.4 0.0 collective-permute-done.3.refs_2_.refs_4_
  19.4 0.0 copy-done.4
  19.5 1.8 %collective-permute-start.7 = (bf16[4,4,16,1152]{3,2,1,0:T(8,128)(2,1)S(1)}, bf16[4,4,16,1152]{3,2,1,0:T(8,128)(2,1)S(1)}, u32[]{:S(2)}, u32[]{:S(2)}) collective-permute-start(bf16[4,4,16,1152]{3,2,1,0:T(8,128)(2,1)S(1)} %join.3.refs_0_), channel_id=1, source_target_pairs={{0,1},{1,0},{2,3},{3,2},{4,5},{5,4},{6,7},{7,6},{8,9},{9,8},{10,11... | collective-permute-start | bytes 1769480 | tf_op jit(solution)/shard_map/ppermute | solution.py:36
  21.3 0.0 copy-done.1
  21.3 0.0 copy-start.5
  21.3 1.2 %spatial_blend.1 = bf16[2,4,16,1152]{3,2,1,0:T(8,128)(2,1)} custom-call(bf16[2,8,128,192]{3,2,1,0:T(8,128)(2,1)S(1)} %get-tuple-element.6.weights_ref.refs_2_, f32[2,8,64,256]{3,2,1,0:T(8,128)S(1)} %get-tuple-element.7.inverse_ref, bf16[2,4,16,1152]{3,2,1,0:T(8,128)(2,1)S(1)} %copy-done.1, ...), custom_call_target="tpu_custom_call" | custom-call | flops 1 | bytes 1 | tf_op jit(solution)/shard_map/spatial_blend/pallas_call | solution.py:178
  22.5 0.0 collective-permute-done.5.refs_1_
  22.5 0.0 copy-done.5
  22.6 1.0 %temporal_weigh.1 = (bf16[4,8,64,128]{3,2,1,0:T(8,128)(2,1)S(1)}, f32[4,8,32,256]{3,2,1,0:T(8,128)S(1)}) custom-call(bf16[2,4,16,1152]{3,2,1,0:T(8,128)(2,1)S(1)} %copy-done.5, bf16[4,4,16,1152]{3,2,1,0:T(8,128)(2,1)S(1)} %join.2.refs_0_, bf16[4,4,16,1152]{3,2,1,0:T(8,128)(2,1)S(1)} %collective-permute-done.5.refs_1_), custom_call_target="tpu_custom_call" | custom-call | flops 1 | bytes 1 | tf_op jit(solution)/shard_map/temporal_weigh/pallas_call | solution.py:178
  23.6 0.0 collective-permute-done.7.refs_1_
  23.6 1.2 %temporal_blend.1 = bf16[2,4,16,1152]{3,2,1,0:T(8,128)(2,1)} custom-call(bf16[4,8,64,128]{3,2,1,0:T(8,128)(2,1)S(1)} %get-tuple-element.8.weights_ref, f32[4,8,32,256]{3,2,1,0:T(8,128)S(1)} %get-tuple-element.9.inverse_ref, bf16[4,4,16,1152]{3,2,1,0:T(8,128)(2,1)S(1)} %join.3.refs_0_, bf16[4,4,16,1152]{3,2,1,0:T(8,128)(2,1)S(1)} %collective-permute-done.7.refs_1_), custom_call_target="tpu_custom_call" | custom-call | flops 1 | bytes 1 | tf_op jit(solution)/shard_map/temporal_blend/pallas_call | solution.py:178
  (2 shorter events, 0.1 us)
Async XLA Ops:
  0.6 8.2 %collective-permute-start = (bf16[2,4,16,1152]{3,2,1,0:T(8,128)(2,1)}, bf16[2,4,16,1152]{3,2,1,0:T(8,128)(2,1)S(1)}, u32[]{:S(2)}, u32[]{:S(2)}) collective-permute-start(bf16[2,4,16,1152]{3,2,1,0:T(8,128)(2,1)} %refs_0_.4), channel_id=1, source_target_pairs={{0,4},{4,0},{8,12},{12,8},{1,5},{5,1},{9,13},{13,9},{2,6},{6,2},{1... | collective-permute-start | bytes 884744 | tf_op jit(solution)/shard_map/ppermute | solution.py:32
  0.9 11.1 %collective-permute-start.1 = (bf16[2,4,16,1152]{3,2,1,0:T(8,128)(2,1)}, bf16[2,4,16,1152]{3,2,1,0:T(8,128)(2,1)S(1)}, u32[]{:S(2)}, u32[]{:S(2)}) collective-permute-start(bf16[2,4,16,1152]{3,2,1,0:T(8,128)(2,1)} %refs_0_.4), channel_id=1, source_target_pairs={{0,0},{4,8},{8,4},{12,12},{1,1},{5,9},{9,5},{13,13},{2,2},{6,10},{... | collective-permute-start | bytes 884744 | tf_op jit(solution)/shard_map/ppermute | solution.py:32
  5.2 11.1 %collective-permute-start.4 = (bf16[2,4,16,1152]{3,2,1,0:T(8,128)(2,1)}, bf16[2,4,16,1152]{3,2,1,0:T(8,128)(2,1)S(1)}, u32[]{:S(2)}, u32[]{:S(2)}) collective-permute-start(bf16[2,4,16,1152]{3,2,1,0:T(8,128)(2,1)} %refs_0_.6), channel_id=1, source_target_pairs={{0,2},{1,3},{2,0},{3,1},{4,6},{5,7},{6,4},{7,5},{8,10},{9,11},{10,... | collective-permute-start | bytes 884744 | tf_op jit(solution)/shard_map/ppermute | solution.py:36
  6.5 13.0 %collective-permute-start.6 = (bf16[2,4,16,1152]{3,2,1,0:T(8,128)(2,1)}, bf16[2,4,16,1152]{3,2,1,0:T(8,128)(2,1)S(1)}, u32[]{:S(2)}, u32[]{:S(2)}) collective-permute-start(bf16[2,4,16,1152]{3,2,1,0:T(8,128)(2,1)} %refs_0_.7), channel_id=1, source_target_pairs={{0,2},{1,3},{2,0},{3,1},{4,6},{5,7},{6,4},{7,5},{8,10},{9,11},{10,... | collective-permute-start | bytes 884744 | tf_op jit(solution)/shard_map/ppermute | solution.py:36
  6.7 12.7 %collective-permute-start.2 = (bf16[2,4,16,1152]{3,2,1,0:T(8,128)(2,1)}, bf16[2,4,16,1152]{3,2,1,0:T(8,128)(2,1)S(1)}, u32[]{:S(2)}, u32[]{:S(2)}) collective-permute-start(bf16[2,4,16,1152]{3,2,1,0:T(8,128)(2,1)} %refs_0_.5), channel_id=1, source_target_pairs={{0,4},{4,0},{8,12},{12,8},{1,5},{5,1},{9,13},{13,9},{2,6},{6,2},{1... | collective-permute-start | bytes 884744 | tf_op jit(solution)/shard_map/ppermute | solution.py:32
  8.8 10.7 %collective-permute-start.3 = (bf16[2,4,16,1152]{3,2,1,0:T(8,128)(2,1)}, bf16[2,4,16,1152]{3,2,1,0:T(8,128)(2,1)S(1)}, u32[]{:S(2)}, u32[]{:S(2)}) collective-permute-start(bf16[2,4,16,1152]{3,2,1,0:T(8,128)(2,1)} %refs_0_.5), channel_id=1, source_target_pairs={{0,0},{4,8},{8,4},{12,12},{1,1},{5,9},{9,5},{13,13},{2,2},{6,10},{... | collective-permute-start | bytes 884744 | tf_op jit(solution)/shard_map/ppermute | solution.py:32
  12.0 0.7 %copy-start.6 = (s32[16,8]{0,1:T(8,128)S(1)}, s32[16,8]{0,1:T(8,128)}, u32[]{:S(2)}) copy-start(s32[16,8]{0,1:T(8,128)} %param.13) | copy-start | bytes 1540
  12.7 1.0 %copy-start.2 = (bf16[2,4,16,1152]{3,2,1,0:T(8,128)(2,1)S(1)}, bf16[2,4,16,1152]{3,2,1,0:T(8,128)(2,1)}, u32[]{:S(2)}) copy-start(bf16[2,4,16,1152]{3,2,1,0:T(8,128)(2,1)} %q_ref.2) | copy-start | bytes 884740
  13.6 1.0 %copy-start.3 = (bf16[2,4,16,1152]{3,2,1,0:T(8,128)(2,1)S(1)}, bf16[2,4,16,1152]{3,2,1,0:T(8,128)(2,1)}, u32[]{:S(2)}) copy-start(bf16[2,4,16,1152]{3,2,1,0:T(8,128)(2,1)} %refs_0_.4) | copy-start | bytes 884740
  14.6 1.7 %copy-start = (bf16[2,4,16,1152]{3,2,1,0:T(8,128)(2,1)S(1)}, bf16[2,4,16,1152]{3,2,1,0:T(8,128)(2,1)}, u32[]{:S(2)}) copy-start(bf16[2,4,16,1152]{3,2,1,0:T(8,128)(2,1)} %refs_0_.6) | copy-start | bytes 884740
  16.3 3.1 %copy-start.4 = (bf16[2,4,16,1152]{3,2,1,0:T(8,128)(2,1)S(1)}, bf16[2,4,16,1152]{3,2,1,0:T(8,128)(2,1)}, u32[]{:S(2)}) copy-start(bf16[2,4,16,1152]{3,2,1,0:T(8,128)(2,1)} %refs_0_.7) | copy-start | bytes 884740
  16.4 5.0 %copy-start.1 = (bf16[2,4,16,1152]{3,2,1,0:T(8,128)(2,1)S(1)}, bf16[2,4,16,1152]{3,2,1,0:T(8,128)(2,1)}, u32[]{:S(2)}) copy-start(bf16[2,4,16,1152]{3,2,1,0:T(8,128)(2,1)} %refs_0_.5) | copy-start | bytes 884740
  16.4 6.2 %collective-permute-start.5 = (bf16[4,4,16,1152]{3,2,1,0:T(8,128)(2,1)S(1)}, bf16[4,4,16,1152]{3,2,1,0:T(8,128)(2,1)S(1)}, u32[]{:S(2)}, u32[]{:S(2)}) collective-permute-start(bf16[4,4,16,1152]{3,2,1,0:T(8,128)(2,1)S(1)} %join.2.refs_0_), channel_id=1, source_target_pairs={{0,1},{1,0},{2,3},{3,2},{4,5},{5,4},{6,7},{7,6},{8,9},{9,8},{10,11... | collective-permute-start | bytes 1769480 | tf_op jit(solution)/shard_map/ppermute | solution.py:36
  19.5 4.1 %collective-permute-start.7 = (bf16[4,4,16,1152]{3,2,1,0:T(8,128)(2,1)S(1)}, bf16[4,4,16,1152]{3,2,1,0:T(8,128)(2,1)S(1)}, u32[]{:S(2)}, u32[]{:S(2)}) collective-permute-start(bf16[4,4,16,1152]{3,2,1,0:T(8,128)(2,1)S(1)} %join.3.refs_0_), channel_id=1, source_target_pairs={{0,1},{1,0},{2,3},{3,2},{4,5},{5,4},{6,7},{7,6},{8,9},{9,8},{10,11... | collective-permute-start | bytes 1769480 | tf_op jit(solution)/shard_map/ppermute | solution.py:36
  21.3 1.2 %copy-start.5 = (bf16[2,4,16,1152]{3,2,1,0:T(8,128)(2,1)S(1)}, bf16[2,4,16,1152]{3,2,1,0:T(8,128)(2,1)}, u32[]{:S(2)}) copy-start(bf16[2,4,16,1152]{3,2,1,0:T(8,128)(2,1)} %q_ref.3) | copy-start | bytes 884740

commit v5 on v4

--- a/solution.py
+++ b/solution.py
@@ -256,7 +256,7 @@
         [index, key_lists.T],
         [spatial_q, *spatial_keys],
         1,
-        [],
+        [received_keys],
     )
     temporal_keys = gathered(temporal_k, received_keys, [spatial_weights])
     blocks = len(temporal_keys)

time: 25.1 us -> 24.9 us (level)
  the two profiles are of different devices: /device:TPU:13 before, /device:TPU:17 now
where the time goes in v5:
time: 24.9 us; the launch traced here: 24.6 us
  starting transfers between devices  11.7 us (47%)
  Pallas kernels  5.2 us (21%)
  waiting for transfers between devices  5.03 us (20%)
  local copies, waits for them, and re-layouts  1.95 us (8%)
  between operations  0.75 us (3%)
    ppermute x4, starting transfers between devices, swapped(): lax.ppermute(value, axis, [(i, i ^ step) for i in range(lax.axis_size(axi...  6.41 us
    ppermute x4, starting transfers between devices, exchanged(): return lax.ppermute(value, axis, pairs)  5.28 us
    pallas_call x6, Pallas kernels, call(): pl.pallas_call(kernel, out_shape=out_shape, in_specs=[in_smem] * len(scal...  5.2 us
    ppermute x4, waiting for transfers between devices, swapped(): lax.ppermute(value, axis, [(i, i ^ step) for i in range(lax.axis_size(axi...  3.35 us
    unnamed x14, local copies, waits for them, and re-layouts  1.95 us
    ppermute x4, waiting for transfers between devices, exchanged(): return lax.ppermute(value, axis, pairs)  1.68 us
  transfers between devices with their start and end apart: 8, of which 2 were waited for; matrix products, arithmetic and copies ran while one was open for 0% of the time, Pallas kernels for 16%

profile of v5, /device:TPU:17, one launch (start us, length us, event | category | flops | bytes accessed | tf_op | source)
XLA Modules:
  0.0 24.6 jit_solution(5986039223320128378)
XLA Ops:
  0.6 1.3 %collective-permute-start.2 = (bf16[2,4,16,1152]{3,2,1,0:T(8,128)(2,1)}, bf16[2,4,16,1152]{3,2,1,0:T(8,128)(2,1)S(1)}, u32[]{:S(2)}, u32[]{:S(2)}) collective-permute-start(bf16[2,4,16,1152]{3,2,1,0:T(8,128)(2,1)} %refs_0_.6), channel_id=1, source_target_pairs={{0,2},{1,3},{2,0},{3,1},{4,6},{5,7},{6,4},{7,5},{8,10},{9,11},{10,... | collective-permute-start | bytes 884744 | tf_op jit(solution)/shard_map/ppermute | solution.py:36
  1.9 1.3 %collective-permute-start = (bf16[2,4,16,1152]{3,2,1,0:T(8,128)(2,1)}, bf16[2,4,16,1152]{3,2,1,0:T(8,128)(2,1)S(1)}, u32[]{:S(2)}, u32[]{:S(2)}) collective-permute-start(bf16[2,4,16,1152]{3,2,1,0:T(8,128)(2,1)} %refs_0_.4), channel_id=1, source_target_pairs={{0,4},{4,0},{8,12},{12,8},{1,5},{5,1},{9,13},{13,9},{2,6},{6,2},{1... | collective-permute-start | bytes 884744 | tf_op jit(solution)/shard_map/ppermute | solution.py:32
  3.2 1.9 %collective-permute-start.1 = (bf16[2,4,16,1152]{3,2,1,0:T(8,128)(2,1)}, bf16[2,4,16,1152]{3,2,1,0:T(8,128)(2,1)S(1)}, u32[]{:S(2)}, u32[]{:S(2)}) collective-permute-start(bf16[2,4,16,1152]{3,2,1,0:T(8,128)(2,1)} %refs_0_.4), channel_id=1, source_target_pairs={{0,0},{4,8},{8,4},{12,12},{1,1},{5,9},{9,5},{13,13},{2,2},{6,10},{... | collective-permute-start | bytes 884744 | tf_op jit(solution)/shard_map/ppermute | solution.py:32
  5.1 0.3 %collective-permute-start.6 = (bf16[2,4,16,1152]{3,2,1,0:T(8,128)(2,1)}, bf16[2,4,16,1152]{3,2,1,0:T(8,128)(2,1)S(1)}, u32[]{:S(2)}, u32[]{:S(2)}) collective-permute-start(bf16[2,4,16,1152]{3,2,1,0:T(8,128)(2,1)} %refs_0_.7), channel_id=1, source_target_pairs={{0,2},{1,3},{2,0},{3,1},{4,6},{5,7},{6,4},{7,5},{8,10},{9,11},{10,... | collective-permute-start | bytes 884744 | tf_op jit(solution)/shard_map/ppermute | solution.py:36
  5.4 0.0 collective-permute-start.3
  5.4 3.3 %collective-permute-done.2.refs_3_.refs_1_ = bf16[2,4,16,1152]{3,2,1,0:T(8,128)(2,1)S(1)} collective-permute-done((bf16[2,4,16,1152]{3,2,1,0:T(8,128)(2,1)}, bf16[2,4,16,1152]{3,2,1,0:T(8,128)(2,1)S(1)}, u32[]{:S(2)}, u32[]{:S(2)}) %collective-permute-start.2) | collective-permute-done | bytes 294944 | tf_op jit(solution)/shard_map/ppermute | solution.py:36
  8.8 2.1 %collective-permute-start.4 = (bf16[2,4,16,1152]{3,2,1,0:T(8,128)(2,1)}, bf16[2,4,16,1152]{3,2,1,0:T(8,128)(2,1)S(1)}, u32[]{:S(2)}, u32[]{:S(2)}) collective-permute-start(bf16[2,4,16,1152]{3,2,1,0:T(8,128)(2,1)} %refs_0_.5), channel_id=1, source_target_pairs={{0,0},{4,8},{8,4},{12,12},{1,1},{5,9},{9,5},{13,13},{2,2},{6,10},{... | collective-permute-start | bytes 884744 | tf_op jit(solution)/shard_map/ppermute | solution.py:32
  10.9 0.0 copy-start.6
  10.9 0.0 collective-permute-done.refs_1_
  10.9 1.7 %collective-permute-done.1.refs_2_ = bf16[2,4,16,1152]{3,2,1,0:T(8,128)(2,1)S(1)} collective-permute-done((bf16[2,4,16,1152]{3,2,1,0:T(8,128)(2,1)}, bf16[2,4,16,1152]{3,2,1,0:T(8,128)(2,1)S(1)}, u32[]{:S(2)}, u32[]{:S(2)}) %collective-permute-start.1) | collective-permute-done | bytes 294944 | tf_op jit(solution)/shard_map/ppermute | solution.py:32
  12.6 0.0 copy-done.6
  12.6 0.0 copy-start.2
  12.6 1.0 %copy-done.2 = bf16[2,4,16,1152]{3,2,1,0:T(8,128)(2,1)S(1)} copy-done((bf16[2,4,16,1152]{3,2,1,0:T(8,128)(2,1)S(1)}, bf16[2,4,16,1152]{3,2,1,0:T(8,128)(2,1)}, u32[]{:S(2)}) %copy-start.2) | copy-done | bytes 294936
  13.5 0.0 copy-start.3
  13.5 1.0 %copy-done.3 = bf16[2,4,16,1152]{3,2,1,0:T(8,128)(2,1)S(1)} copy-done((bf16[2,4,16,1152]{3,2,1,0:T(8,128)(2,1)S(1)}, bf16[2,4,16,1152]{3,2,1,0:T(8,128)(2,1)}, u32[]{:S(2)}) %copy-start.3) | copy-done | bytes 294936
  14.5 0.0 copy-start
  14.5 1.7 %spatial_weigh.1 = (bf16[2,8,128,192]{3,2,1,0:T(8,128)(2,1)S(1)}, f32[2,8,64,256]{3,2,1,0:T(8,128)S(1)}) custom-call(s32[1]{0:T(128)} %bitcast.index_ref, s32[8,16]{1,0:T(8,128)S(1)} %bitcast.2, bf16[2,4,16,1152]{3,2,1,0:T(8,128)(2,1)S(1)} %copy-done.2, bf16[2,4,16,1152]{3,2,1,0:T(8,128)(2,1)S(1)} %copy-done.3, ...), custom_call_target="tpu_custom_call" | custom-call | flops 1 | bytes 1 | tf_op jit(solution)/shard_map/spatial_weigh/pallas_call | solution.py:178
  16.2 0.0 copy-done
  16.2 0.0 copy-start.4
  16.3 0.0 copy-start.1
  16.3 2.9 %collective-permute-start.5 = (bf16[4,4,16,1152]{3,2,1,0:T(8,128)(2,1)S(1)}, bf16[4,4,16,1152]{3,2,1,0:T(8,128)(2,1)S(1)}, u32[]{:S(2)}, u32[]{:S(2)}) collective-permute-start(bf16[4,4,16,1152]{3,2,1,0:T(8,128)(2,1)S(1)} %join.2.refs_0_), channel_id=1, source_target_pairs={{0,1},{1,0},{2,3},{3,2},{4,5},{5,4},{6,7},{7,6},{8,9},{9,8},{10,11... | collective-permute-start | bytes 1769480 | tf_op jit(solution)/shard_map/ppermute | solution.py:36
  19.2 0.0 collective-permute-done.6.refs_1_
  19.2 0.0 collective-permute-done.3.refs_1_.refs_3_
  19.2 0.0 collective-permute-done.4.refs_2_.refs_4_
  19.2 0.0 copy-done.4
  19.2 1.9 %collective-permute-start.7 = (bf16[4,4,16,1152]{3,2,1,0:T(8,128)(2,1)S(1)}, bf16[4,4,16,1152]{3,2,1,0:T(8,128)(2,1)S(1)}, u32[]{:S(2)}, u32[]{:S(2)}) collective-permute-start(bf16[4,4,16,1152]{3,2,1,0:T(8,128)(2,1)S(1)} %join.3.refs_0_), channel_id=1, source_target_pairs={{0,1},{1,0},{2,3},{3,2},{4,5},{5,4},{6,7},{7,6},{8,9},{9,8},{10,11... | collective-permute-start | bytes 1769480 | tf_op jit(solution)/shard_map/ppermute | solution.py:36
  21.2 0.0 copy-done.1
  21.2 0.0 copy-start.5
  21.2 1.2 %spatial_blend.1 = bf16[2,4,16,1152]{3,2,1,0:T(8,128)(2,1)} custom-call(bf16[2,8,128,192]{3,2,1,0:T(8,128)(2,1)S(1)} %get-tuple-element.6.weights_ref.refs_2_, f32[2,8,64,256]{3,2,1,0:T(8,128)S(1)} %get-tuple-element.7.inverse_ref, bf16[2,4,16,1152]{3,2,1,0:T(8,128)(2,1)S(1)} %copy-done.1, ...), custom_call_target="tpu_custom_call" | custom-call | flops 1 | bytes 1 | tf_op jit(solution)/shard_map/spatial_blend/pallas_call | solution.py:178
  22.4 0.0 collective-permute-done.5.refs_1_
  22.4 0.0 copy-done.5
  22.4 1.0 %temporal_weigh.1 = (bf16[4,8,64,128]{3,2,1,0:T(8,128)(2,1)S(1)}, f32[4,8,32,256]{3,2,1,0:T(8,128)S(1)}) custom-call(bf16[2,4,16,1152]{3,2,1,0:T(8,128)(2,1)S(1)} %copy-done.5, bf16[4,4,16,1152]{3,2,1,0:T(8,128)(2,1)S(1)} %join.2.refs_0_, bf16[4,4,16,1152]{3,2,1,0:T(8,128)(2,1)S(1)} %collective-permute-done.5.refs_1_), custom_call_target="tpu_custom_call" | custom-call | flops 1 | bytes 1 | tf_op jit(solution)/shard_map/temporal_weigh/pallas_call | solution.py:178
  23.4 0.0 collective-permute-done.7.refs_1_
  23.4 1.2 %temporal_blend.1 = bf16[2,4,16,1152]{3,2,1,0:T(8,128)(2,1)} custom-call(bf16[4,8,64,128]{3,2,1,0:T(8,128)(2,1)S(1)} %get-tuple-element.8.weights_ref, f32[4,8,32,256]{3,2,1,0:T(8,128)S(1)} %get-tuple-element.9.inverse_ref, bf16[4,4,16,1152]{3,2,1,0:T(8,128)(2,1)S(1)} %join.3.refs_0_, bf16[4,4,16,1152]{3,2,1,0:T(8,128)(2,1)S(1)} %collective-permute-done.7.refs_1_), custom_call_target="tpu_custom_call" | custom-call | flops 1 | bytes 1 | tf_op jit(solution)/shard_map/temporal_blend/pallas_call | solution.py:178
  (2 shorter events, 0.1 us)
Async XLA Ops:
  0.6 8.2 %collective-permute-start.2 = (bf16[2,4,16,1152]{3,2,1,0:T(8,128)(2,1)}, bf16[2,4,16,1152]{3,2,1,0:T(8,128)(2,1)S(1)}, u32[]{:S(2)}, u32[]{:S(2)}) collective-permute-start(bf16[2,4,16,1152]{3,2,1,0:T(8,128)(2,1)} %refs_0_.6), channel_id=1, source_target_pairs={{0,2},{1,3},{2,0},{3,1},{4,6},{5,7},{6,4},{7,5},{8,10},{9,11},{10,... | collective-permute-start | bytes 884744 | tf_op jit(solution)/shard_map/ppermute | solution.py:36
  1.9 9.0 %collective-permute-start = (bf16[2,4,16,1152]{3,2,1,0:T(8,128)(2,1)}, bf16[2,4,16,1152]{3,2,1,0:T(8,128)(2,1)S(1)}, u32[]{:S(2)}, u32[]{:S(2)}) collective-permute-start(bf16[2,4,16,1152]{3,2,1,0:T(8,128)(2,1)} %refs_0_.4), channel_id=1, source_target_pairs={{0,4},{4,0},{8,12},{12,8},{1,5},{5,1},{9,13},{13,9},{2,6},{6,2},{1... | collective-permute-start | bytes 884744 | tf_op jit(solution)/shard_map/ppermute | solution.py:32
  3.2 9.4 %collective-permute-start.1 = (bf16[2,4,16,1152]{3,2,1,0:T(8,128)(2,1)}, bf16[2,4,16,1152]{3,2,1,0:T(8,128)(2,1)S(1)}, u32[]{:S(2)}, u32[]{:S(2)}) collective-permute-start(bf16[2,4,16,1152]{3,2,1,0:T(8,128)(2,1)} %refs_0_.4), channel_id=1, source_target_pairs={{0,0},{4,8},{8,4},{12,12},{1,1},{5,9},{9,5},{13,13},{2,2},{6,10},{... | collective-permute-start | bytes 884744 | tf_op jit(solution)/shard_map/ppermute | solution.py:32
  5.1 14.0 %collective-permute-start.6 = (bf16[2,4,16,1152]{3,2,1,0:T(8,128)(2,1)}, bf16[2,4,16,1152]{3,2,1,0:T(8,128)(2,1)S(1)}, u32[]{:S(2)}, u32[]{:S(2)}) collective-permute-start(bf16[2,4,16,1152]{3,2,1,0:T(8,128)(2,1)} %refs_0_.7), channel_id=1, source_target_pairs={{0,2},{1,3},{2,0},{3,1},{4,6},{5,7},{6,4},{7,5},{8,10},{9,11},{10,... | collective-permute-start | bytes 884744 | tf_op jit(solution)/shard_map/ppermute | solution.py:36
  5.4 13.7 %collective-permute-start.3 = (bf16[2,4,16,1152]{3,2,1,0:T(8,128)(2,1)}, bf16[2,4,16,1152]{3,2,1,0:T(8,128)(2,1)S(1)}, u32[]{:S(2)}, u32[]{:S(2)}) collective-permute-start(bf16[2,4,16,1152]{3,2,1,0:T(8,128)(2,1)} %refs_0_.5), channel_id=1, source_target_pairs={{0,4},{4,0},{8,12},{12,8},{1,5},{5,1},{9,13},{13,9},{2,6},{6,2},{1... | collective-permute-start | bytes 884744 | tf_op jit(solution)/shard_map/ppermute | solution.py:32
  8.8 10.4 %collective-permute-start.4 = (bf16[2,4,16,1152]{3,2,1,0:T(8,128)(2,1)}, bf16[2,4,16,1152]{3,2,1,0:T(8,128)(2,1)S(1)}, u32[]{:S(2)}, u32[]{:S(2)}) collective-permute-start(bf16[2,4,16,1152]{3,2,1,0:T(8,128)(2,1)} %refs_0_.5), channel_id=1, source_target_pairs={{0,0},{4,8},{8,4},{12,12},{1,1},{5,9},{9,5},{13,13},{2,2},{6,10},{... | collective-permute-start | bytes 884744 | tf_op jit(solution)/shard_map/ppermute | solution.py:32
  10.9 1.7 %copy-start.6 = (s32[16,8]{0,1:T(8,128)S(1)}, s32[16,8]{0,1:T(8,128)}, u32[]{:S(2)}) copy-start(s32[16,8]{0,1:T(8,128)} %param.13) | copy-start | bytes 1540
  12.6 1.0 %copy-start.2 = (bf16[2,4,16,1152]{3,2,1,0:T(8,128)(2,1)S(1)}, bf16[2,4,16,1152]{3,2,1,0:T(8,128)(2,1)}, u32[]{:S(2)}) copy-start(bf16[2,4,16,1152]{3,2,1,0:T(8,128)(2,1)} %q_ref.2) | copy-start | bytes 884740
  13.5 1.0 %copy-start.3 = (bf16[2,4,16,1152]{3,2,1,0:T(8,128)(2,1)S(1)}, bf16[2,4,16,1152]{3,2,1,0:T(8,128)(2,1)}, u32[]{:S(2)}) copy-start(bf16[2,4,16,1152]{3,2,1,0:T(8,128)(2,1)} %refs_0_.4) | copy-start | bytes 884740
  14.5 1.7 %copy-start = (bf16[2,4,16,1152]{3,2,1,0:T(8,128)(2,1)S(1)}, bf16[2,4,16,1152]{3,2,1,0:T(8,128)(2,1)}, u32[]{:S(2)}) copy-start(bf16[2,4,16,1152]{3,2,1,0:T(8,128)(2,1)} %refs_0_.6) | copy-start | bytes 884740
  16.2 3.0 %copy-start.4 = (bf16[2,4,16,1152]{3,2,1,0:T(8,128)(2,1)S(1)}, bf16[2,4,16,1152]{3,2,1,0:T(8,128)(2,1)}, u32[]{:S(2)}) copy-start(bf16[2,4,16,1152]{3,2,1,0:T(8,128)(2,1)} %refs_0_.7) | copy-start | bytes 884740
  16.3 4.9 %copy-start.1 = (bf16[2,4,16,1152]{3,2,1,0:T(8,128)(2,1)S(1)}, bf16[2,4,16,1152]{3,2,1,0:T(8,128)(2,1)}, u32[]{:S(2)}) copy-start(bf16[2,4,16,1152]{3,2,1,0:T(8,128)(2,1)} %refs_0_.5) | copy-start | bytes 884740
  16.3 6.1 %collective-permute-start.5 = (bf16[4,4,16,1152]{3,2,1,0:T(8,128)(2,1)S(1)}, bf16[4,4,16,1152]{3,2,1,0:T(8,128)(2,1)S(1)}, u32[]{:S(2)}, u32[]{:S(2)}) collective-permute-start(bf16[4,4,16,1152]{3,2,1,0:T(8,128)(2,1)S(1)} %join.2.refs_0_), channel_id=1, source_target_pairs={{0,1},{1,0},{2,3},{3,2},{4,5},{5,4},{6,7},{7,6},{8,9},{9,8},{10,11... | collective-permute-start | bytes 1769480 | tf_op jit(solution)/shard_map/ppermute | solution.py:36
  19.2 4.2 %collective-permute-start.7 = (bf16[4,4,16,1152]{3,2,1,0:T(8,128)(2,1)S(1)}, bf16[4,4,16,1152]{3,2,1,0:T(8,128)(2,1)S(1)}, u32[]{:S(2)}, u32[]{:S(2)}) collective-permute-start(bf16[4,4,16,1152]{3,2,1,0:T(8,128)(2,1)S(1)} %join.3.refs_0_), channel_id=1, source_target_pairs={{0,1},{1,0},{2,3},{3,2},{4,5},{5,4},{6,7},{7,6},{8,9},{9,8},{10,11... | collective-permute-start | bytes 1769480 | tf_op jit(solution)/shard_map/ppermute | solution.py:36
  21.2 1.2 %copy-start.5 = (bf16[2,4,16,1152]{3,2,1,0:T(8,128)(2,1)S(1)}, bf16[2,4,16,1152]{3,2,1,0:T(8,128)(2,1)}, u32[]{:S(2)}) copy-start(bf16[2,4,16,1152]{3,2,1,0:T(8,128)(2,1)} %q_ref.3) | copy-start | bytes 884740

commit v6 on v5

--- a/solution.py
+++ b/solution.py
@@ -14,6 +14,7 @@
 WINDOW = 2 * LANES
 SCALE = HEAD_DIM ** (-0.5) * math.log2(math.e)
 big_negative = -1e30
+AXES = ("video", "space", "tm")
 
 
 def partner_of(index, distance, parity):
@@ -23,13 +24,23 @@
     return jnp.where(upward, index + distance, index - distance)
 
 
-def exchanged(value, axis, distance, parity):
-    length = lax.axis_size(axis)
+def exchanged(value, distance, parity):
+    videos, length, others = [lax.axis_size(axis) for axis in AXES]
     pairs = []
-    for index in range(length):
-        partner = partner_of(index, distance, parity)
-        pairs.append((index, partner if 0 <= partner < length else index))
-    return lax.ppermute(value, axis, pairs)
+    for video in range(videos):
+        for index in range(length):
+            there, partner = video, partner_of(index, distance, parity)
+            if not 0 <= partner < length:
+                partner = index
+                there = video ^ 1 if (video ^ 1) < videos else video
+            for other in range(others):
+                pairs.append(
+                    (
+                        (video * length + index) * others + other,
+                        (there * length + partner) * others + other,
+                    )
+                )
+    return lax.ppermute(value, AXES, pairs)
 
 
 def swapped(value, axis, step):
@@ -94,9 +105,16 @@
     return jnp.concatenate([ref[:, row, :, lanes].reshape(-1, WINDOW) for ref in refs], axis=0)
 
 
-def spatial_weigh_kernel(blocks, space, index_ref, lists_ref, q_ref, *refs):
-    k_refs, weights_ref, inverse_ref = refs[:blocks], *refs[-2:]
-    frames, rows, columns, channels = q_ref.shape
+def stage_kernel(blocks, space, index_ref, lists_ref, *refs):
+    count = (len(refs) - 2) // 2
+    sources, bias_ref, copies, sems = refs[:count], refs[count], refs[count + 1 : -1], refs[-1]
+    moves = [
+        pltpu.make_async_copy(source, copy, sems.at[i])
+        for i, (source, copy) in enumerate(zip(sources, copies))
+    ]
+    for move in moves:
+        move.start()
+    _, rows, columns, _ = sources[0].shape
     index = index_ref[0]
     key_rows = []
     for distance in range(blocks // 2 + 1):
@@ -106,14 +124,39 @@
             row = lax.broadcasted_iota(jnp.int32, (columns, rows * columns), 1) // columns
             key_rows.append(row + first)
     key_rows = jnp.concatenate(key_rows, axis=1)
-    bias = []
     for row in range(rows):
         query_row = index * rows + row
         member = key_rows == query_row
         for entry in range(lists_ref.shape[0]):
             member = member | (key_rows == lists_ref[entry, query_row])
-        bias.append(jnp.where(member & (key_rows >= 0), 0.0, big_negative))
-    bias = jnp.concatenate(bias + bias, axis=0)
+        bias = jnp.where(member & (key_rows >= 0), 0.0, big_negative)
+        bias_ref[row * columns : (row + 1) * columns] = bias
+    for move in moves:
+        move.wait()
+
+
+def staged(arrays, index, lists, blocks, space):
+    _, rows, columns, _ = arrays[0].shape
+    in_vmem = pl.BlockSpec(memory_space=pltpu.VMEM)
+    bias = jax.ShapeDtypeStruct((rows * columns, blocks * rows * columns), jnp.float32)
+    return pl.pallas_call(
+        functools.partial(stage_kernel, blocks, space),
+        out_shape=(bias, *[jax.ShapeDtypeStruct(a.shape, a.dtype) for a in arrays]),
+        in_specs=[pl.BlockSpec(memory_space=pltpu.SMEM)] * 2
+        + [pl.BlockSpec(memory_space=pl.ANY)] * len(arrays),
+        out_specs=(in_vmem,) * (1 + len(arrays)),
+        scratch_shapes=[pltpu.SemaphoreType.DMA((len(arrays),))],
+        compiler_params=pltpu.CompilerParams(vmem_limit_bytes=40 * 1024 * 1024),
+        cost_estimate=pl.CostEstimate(flops=1, bytes_accessed=1, transcendentals=0),
+        name="stage",
+    )(index, lists, *arrays)
+
+
+def spatial_weigh_kernel(blocks, bias_ref, q_ref, *refs):
+    k_refs, weights_ref, inverse_ref = refs[:blocks], *refs[-2:]
+    frames, rows, columns, channels = q_ref.shape
+    bias = bias_ref[...]
+    bias = jnp.concatenate([bias, bias], axis=0)
     for frame in range(frames):
         for pair in range(channels // PAIR):
             lanes = window_of(pair)
@@ -226,12 +269,11 @@
     tokens = frames * rows * columns
     first_step = lax.axis_size("tm") // 2
 
-    def halo(value):
-        return [value] + [
-            exchanged(value, "space", distance, parity)
-            for distance in range(1, reach + 1)
-            for parity in range(2)
-        ]
+    exchanges = [(d, parity) for d in range(1, reach + 1) for parity in range(2)]
+    blocks = 1 + len(exchanges)
+    bias, own_q, own_k, own_tv = staged(
+        [spatial_q, spatial_k, temporal_v], index, key_lists.T, blocks, space
+    )
 
     def gathered(own, received, others):
         held, step = [own, received], first_step // 2
@@ -242,19 +284,19 @@
         return held
 
     received_keys = swapped(temporal_k, "tm", first_step)
-    received_values = swapped(temporal_v, "tm", first_step)
-    spatial_keys = halo(spatial_k)
-    spatial_values = halo(spatial_v)
-
-    blocks = len(spatial_keys)
+    received_values = swapped(own_tv, "tm", first_step)
+    spatial_keys = [own_k] + [exchanged(spatial_k, *which) for which in exchanges]
+    spatial_values = [spatial_v] + [
+        exchanged(spatial_v, *which) for which in exchanges
+    ]
+
     keys = blocks * rows * columns
-    flops = 2 * tokens * keys * channels
     spatial_weights, spatial_inverse = call(
-        functools.partial(spatial_weigh_kernel, blocks, space),
+        functools.partial(spatial_weigh_kernel, blocks),
         "spatial_weigh",
         weigh_shapes(frames, channels, rows * columns, keys),
-        [index, key_lists.T],
-        [spatial_q, *spatial_keys],
+        [],
+        [bias, own_q, *spatial_keys],
         1,
         [received_keys],
     )
@@ -269,7 +311,7 @@
         [temporal_q, *temporal_keys],
         1,
     )
-    temporal_values = gathered(temporal_v, received_values, [spatial_weights, *spatial_values[1:]])
+    temporal_values = gathered(own_tv, received_values, [spatial_weights, *spatial_values[1:]])
     spatial_out = call(
         functools.partial(spatial_blend_kernel, len(spatial_values)),
         "spatial_blend",

time: 24.9 us -> 24.3 us (0.976)
  the two profiles are of different devices: /device:TPU:17 before, /device:TPU:0 now
where the time goes in v6:
time: 24.3 us; the launch traced here: 24 us
  starting transfers between devices  8.45 us (35%)
  waiting for transfers between devices  5.9 us (24%)
  Pallas kernels  5.37 us (22%)
  local copies, waits for them, and re-layouts  3.59 us (15%)
  between operations  0.74 us (3%)
    ppermute x4, waiting for transfers between devices, exchanged(): return lax.ppermute(value, AXES, pairs)  5.23 us
    ppermute x4, starting transfers between devices, exchanged(): return lax.ppermute(value, AXES, pairs)  4.71 us
    pallas_call x6, Pallas kernels, call(): pl.pallas_call(kernel, out_shape=out_shape, in_specs=[in_smem] * len(scal...  4.45 us
    ppermute x4, starting transfers between devices, swapped(): lax.ppermute(value, axis, [(i, i ^ step) for i in range(lax.axis_size(axi...  3.75 us
    unnamed x14, local copies, waits for them, and re-layouts  3.59 us
    pallas_call x1, Pallas kernels, staged(): pl.pallas_call(functools.partial(stage_kernel, blocks, space), out_shape=...  0.91 us
    ppermute x4, waiting for transfers between devices, swapped(): lax.ppermute(value, axis, [(i, i ^ step) for i in range(lax.axis_size(axi...  0.67 us
  transfers between devices with their start and end apart: 8, of which 4 were waited for; matrix products, arithmetic and copies ran while one was open for 0% of the time, Pallas kernels for 18%

profile of v6, /device:TPU:0, one launch (start us, length us, event | category | flops | bytes accessed | tf_op | source)
XLA Modules:
  0.0 24.0 jit_solution(3271854500961747830)
XLA Ops:
  0.6 3.0 %collective-permute-start.2 = (bf16[2,4,16,1152]{3,2,1,0:T(8,128)(2,1)}, bf16[2,4,16,1152]{3,2,1,0:T(8,128)(2,1)S(1)}, u32[]{:S(2)}, u32[]{:S(2)}) collective-permute-start(bf16[2,4,16,1152]{3,2,1,0:T(8,128)(2,1)} %refs_0_.5), channel_id=1, source_target_pairs={{0,2},{1,3},{2,0},{3,1},{4,6},{5,7},{6,4},{7,5},{8,10},{9,11},{10,... | collective-permute-start | bytes 884744 | tf_op jit(solution)/shard_map/ppermute | solution.py:47
  3.6 1.5 %collective-permute-start.1 = (bf16[2,4,16,1152]{3,2,1,0:T(8,128)(2,1)}, bf16[2,4,16,1152]{3,2,1,0:T(8,128)(2,1)S(1)}, u32[]{:S(2)}, u32[]{:S(2)}) collective-permute-start(bf16[2,4,16,1152]{3,2,1,0:T(8,128)(2,1)} %refs_1_.1), channel_id=1, source_target_pairs={{0,16},{1,17},{2,18},{3,19},{4,8},{5,9},{6,10},{7,11},{8,4},{9,5},... | collective-permute-start | bytes 884744 | tf_op jit(solution)/shard_map/ppermute | solution.py:43
  5.2 1.6 %collective-permute-start = (bf16[2,4,16,1152]{3,2,1,0:T(8,128)(2,1)}, bf16[2,4,16,1152]{3,2,1,0:T(8,128)(2,1)S(1)}, u32[]{:S(2)}, u32[]{:S(2)}) collective-permute-start(bf16[2,4,16,1152]{3,2,1,0:T(8,128)(2,1)} %refs_1_.1), channel_id=1, source_target_pairs={{0,4},{1,5},{2,6},{3,7},{4,0},{5,1},{6,2},{7,3},{8,12},{9,13},{10,... | collective-permute-start | bytes 884744 | tf_op jit(solution)/shard_map/ppermute | solution.py:43
  6.8 0.4 %collective-permute-start.3 = (bf16[2,4,16,1152]{3,2,1,0:T(8,128)(2,1)}, bf16[2,4,16,1152]{3,2,1,0:T(8,128)(2,1)S(1)}, u32[]{:S(2)}, u32[]{:S(2)}) collective-permute-start(bf16[2,4,16,1152]{3,2,1,0:T(8,128)(2,1)} %refs_0_.4), channel_id=1, source_target_pairs={{0,4},{1,5},{2,6},{3,7},{4,0},{5,1},{6,2},{7,3},{8,12},{9,13},{10,... | collective-permute-start | bytes 884744 | tf_op jit(solution)/shard_map/ppermute | solution.py:43
  7.2 1.2 %collective-permute-start.4 = (bf16[2,4,16,1152]{3,2,1,0:T(8,128)(2,1)}, bf16[2,4,16,1152]{3,2,1,0:T(8,128)(2,1)S(1)}, u32[]{:S(2)}, u32[]{:S(2)}) collective-permute-start(bf16[2,4,16,1152]{3,2,1,0:T(8,128)(2,1)} %refs_0_.4), channel_id=1, source_target_pairs={{0,16},{1,17},{2,18},{3,19},{4,8},{5,9},{6,10},{7,11},{8,4},{9,5},... | collective-permute-start | bytes 884744 | tf_op jit(solution)/shard_map/ppermute | solution.py:43
  8.3 0.0 copy-start.6
  8.3 0.7 %copy-done.6 = s32[16,8]{0,1:T(8,128)S(1)} copy-done((s32[16,8]{0,1:T(8,128)S(1)}, s32[16,8]{0,1:T(8,128)}, u32[]{:S(2)}) %copy-start.6) | copy-done | bytes 536
  9.0 0.0 copy-start.2
  9.0 1.0 %copy-done.2 = bf16[2,4,16,1152]{3,2,1,0:T(8,128)(2,1)S(1)} copy-done((bf16[2,4,16,1152]{3,2,1,0:T(8,128)(2,1)S(1)}, bf16[2,4,16,1152]{3,2,1,0:T(8,128)(2,1)}, u32[]{:S(2)}) %copy-start.2) | copy-done | bytes 294936
  10.0 0.0 copy-start.3
  10.0 1.0 %copy-done.3 = bf16[2,4,16,1152]{3,2,1,0:T(8,128)(2,1)S(1)} copy-done((bf16[2,4,16,1152]{3,2,1,0:T(8,128)(2,1)S(1)}, bf16[2,4,16,1152]{3,2,1,0:T(8,128)(2,1)}, u32[]{:S(2)}) %copy-start.3) | copy-done | bytes 294936
  11.0 0.0 copy-start.4
  11.0 1.0 %copy-done.4 = bf16[2,4,16,1152]{3,2,1,0:T(8,128)(2,1)S(1)} copy-done((bf16[2,4,16,1152]{3,2,1,0:T(8,128)(2,1)S(1)}, bf16[2,4,16,1152]{3,2,1,0:T(8,128)(2,1)}, u32[]{:S(2)}) %copy-start.4) | copy-done | bytes 294936
  11.9 0.9 %stage.1 = (f32[64,192]{1,0:T(8,128)S(1)}, bf16[2,4,16,1152]{3,2,1,0:T(8,128)(2,1)S(1)}, bf16[2,4,16,1152]{3,2,1,0:T(8,128)(2,1)S(1)}, bf16[2,4,16,1152]{3,2,1,0:T(8,128)(2,1)S(1)}) custom-call(s32[1]{0:T(128)} %bitcast.index_ref, s32[8,16]{1,0:T(8,128)S(1)} %bitcast.2, bf16[2,4,16,1152]{3,2,1,0:T(8,128)(2,1)S(1)} %copy-done.2, ...), custom_call_target="tpu_custom_call" | custom-call | flops 1 | bytes 1 | tf_op jit(solution)/shard_map/stage/pallas_call | solution.py:142
  12.8 0.0 collective-permute-done.2.refs_3_.refs_1_
  12.8 0.6 %collective-permute-start.6 = (bf16[2,4,16,1152]{3,2,1,0:T(8,128)(2,1)S(1)}, bf16[2,4,16,1152]{3,2,1,0:T(8,128)(2,1)S(1)}, u32[]{:S(2)}, u32[]{:S(2)}) collective-permute-start(bf16[2,4,16,1152]{3,2,1,0:T(8,128)(2,1)S(1)} %get-tuple-element.17.refs_0_), channel_id=1, source_target_pairs={{0,2},{1,3},{2,0},{3,1},{4,6},{5,7},{6,4},{7,5},{8,10},{9,11},{10,... | collective-permute-start | bytes 884744 | tf_op jit(solution)/shard_map/ppermute | solution.py:47
  13.4 0.3 %collective-permute-done.1.refs_2_ = bf16[2,4,16,1152]{3,2,1,0:T(8,128)(2,1)S(1)} collective-permute-done((bf16[2,4,16,1152]{3,2,1,0:T(8,128)(2,1)}, bf16[2,4,16,1152]{3,2,1,0:T(8,128)(2,1)S(1)}, u32[]{:S(2)}, u32[]{:S(2)}) %collective-permute-start.1) | collective-permute-done | bytes 294944 | tf_op jit(solution)/shard_map/ppermute | solution.py:43
  13.8 1.5 %collective-permute-done.refs_1_ = bf16[2,4,16,1152]{3,2,1,0:T(8,128)(2,1)S(1)} collective-permute-done((bf16[2,4,16,1152]{3,2,1,0:T(8,128)(2,1)}, bf16[2,4,16,1152]{3,2,1,0:T(8,128)(2,1)S(1)}, u32[]{:S(2)}, u32[]{:S(2)}) %collective-permute-start) | collective-permute-done | bytes 294944 | tf_op jit(solution)/shard_map/ppermute | solution.py:43
  15.3 0.0 copy-start
  15.3 1.0 %spatial_weigh.1 = (bf16[2,8,128,192]{3,2,1,0:T(8,128)(2,1)S(1)}, f32[2,8,64,256]{3,2,1,0:T(8,128)S(1)}) custom-call(f32[64,192]{1,0:T(8,128)S(1)} %get-tuple-element.10.bias_ref, bf16[2,4,16,1152]{3,2,1,0:T(8,128)(2,1)S(1)} %get-tuple-element.11.q_ref, bf16[2,4,16,1152]{3,2,1,0:T(8,128)(2,1)S(1)} %get-tuple-element.12.refs_0_, ...), custom_call_target="tpu_custom_call" | custom-call | flops 1 | bytes 1 | tf_op jit(solution)/shard_map/spatial_weigh/pallas_call | solution.py:221
  16.4 0.0 copy-done
  16.4 0.0 copy-start.1
  16.4 0.1 collective-permute-start.5
  16.5 3.4 %collective-permute-done.3.refs_1_.refs_3_ = bf16[2,4,16,1152]{3,2,1,0:T(8,128)(2,1)S(1)} collective-permute-done((bf16[2,4,16,1152]{3,2,1,0:T(8,128)(2,1)}, bf16[2,4,16,1152]{3,2,1,0:T(8,128)(2,1)S(1)}, u32[]{:S(2)}, u32[]{:S(2)}) %collective-permute-start.3) | collective-permute-done | bytes 294944 | tf_op jit(solution)/shard_map/ppermute | solution.py:43
  19.9 0.0 collective-permute-done.4.refs_2_.refs_4_
  19.9 0.7 %collective-permute-done.6.refs_1_ = bf16[2,4,16,1152]{3,2,1,0:T(8,128)(2,1)S(1)} collective-permute-done((bf16[2,4,16,1152]{3,2,1,0:T(8,128)(2,1)S(1)}, bf16[2,4,16,1152]{3,2,1,0:T(8,128)(2,1)S(1)}, u32[]{:S(2)}, u32[]{:S(2)}) %collective-permute-start.6) | collective-permute-done | bytes 294944 | tf_op jit(solution)/shard_map/ppermute | solution.py:47
  20.6 0.1 collective-permute-start.7
  20.7 0.0 copy-done.1
  20.7 0.0 copy-start.5
  20.7 1.1 %spatial_blend.1 = bf16[2,4,16,1152]{3,2,1,0:T(8,128)(2,1)} custom-call(bf16[2,8,128,192]{3,2,1,0:T(8,128)(2,1)S(1)} %get-tuple-element.13.weights_ref.refs_2_, f32[2,8,64,256]{3,2,1,0:T(8,128)S(1)} %get-tuple-element.14.inverse_ref, bf16[2,4,16,1152]{3,2,1,0:T(8,128)(2,1)S(1)} %copy-done.1, ...), custom_call_target="tpu_custom_call" | custom-call | flops 1 | bytes 1 | tf_op jit(solution)/shard_map/spatial_blend/pallas_call | solution.py:221
  21.8 0.0 collective-permute-done.5.refs_1_
  21.8 0.0 copy-done.5
  21.8 1.0 %temporal_weigh.1 = (bf16[4,8,64,128]{3,2,1,0:T(8,128)(2,1)S(1)}, f32[4,8,32,256]{3,2,1,0:T(8,128)S(1)}) custom-call(bf16[2,4,16,1152]{3,2,1,0:T(8,128)(2,1)S(1)} %copy-done.5, bf16[4,4,16,1152]{3,2,1,0:T(8,128)(2,1)S(1)} %join.2.refs_0_, bf16[4,4,16,1152]{3,2,1,0:T(8,128)(2,1)S(1)} %collective-permute-done.5.refs_1_), custom_call_target="tpu_custom_call" | custom-call | flops 1 | bytes 1 | tf_op jit(solution)/shard_map/temporal_weigh/pallas_call | solution.py:221
  22.9 0.0 collective-permute-done.7.refs_1_
  22.9 1.1 %temporal_blend.1 = bf16[2,4,16,1152]{3,2,1,0:T(8,128)(2,1)} custom-call(bf16[4,8,64,128]{3,2,1,0:T(8,128)(2,1)S(1)} %get-tuple-element.15.weights_ref, f32[4,8,32,256]{3,2,1,0:T(8,128)S(1)} %get-tuple-element.16.inverse_ref, bf16[4,4,16,1152]{3,2,1,0:T(8,128)(2,1)S(1)} %join.3.refs_0_, bf16[4,4,16,1152]{3,2,1,0:T(8,128)(2,1)S(1)} %collective-permute-done.7.refs_1_), custom_call_target="tpu_custom_call" | custom-call | flops 1 | bytes 1 | tf_op jit(solution)/shard_map/temporal_blend/pallas_call | solution.py:221
  (2 shorter events, 0.1 us)
Async XLA Ops:
  0.6 12.2 %collective-permute-start.2 = (bf16[2,4,16,1152]{3,2,1,0:T(8,128)(2,1)}, bf16[2,4,16,1152]{3,2,1,0:T(8,128)(2,1)S(1)}, u32[]{:S(2)}, u32[]{:S(2)}) collective-permute-start(bf16[2,4,16,1152]{3,2,1,0:T(8,128)(2,1)} %refs_0_.5), channel_id=1, source_target_pairs={{0,2},{1,3},{2,0},{3,1},{4,6},{5,7},{6,4},{7,5},{8,10},{9,11},{10,... | collective-permute-start | bytes 884744 | tf_op jit(solution)/shard_map/ppermute | solution.py:47
  3.6 10.1 %collective-permute-start.1 = (bf16[2,4,16,1152]{3,2,1,0:T(8,128)(2,1)}, bf16[2,4,16,1152]{3,2,1,0:T(8,128)(2,1)S(1)}, u32[]{:S(2)}, u32[]{:S(2)}) collective-permute-start(bf16[2,4,16,1152]{3,2,1,0:T(8,128)(2,1)} %refs_1_.1), channel_id=1, source_target_pairs={{0,16},{1,17},{2,18},{3,19},{4,8},{5,9},{6,10},{7,11},{8,4},{9,5},... | collective-permute-start | bytes 884744 | tf_op jit(solution)/shard_map/ppermute | solution.py:43
  5.2 10.2 %collective-permute-start = (bf16[2,4,16,1152]{3,2,1,0:T(8,128)(2,1)}, bf16[2,4,16,1152]{3,2,1,0:T(8,128)(2,1)S(1)}, u32[]{:S(2)}, u32[]{:S(2)}) collective-permute-start(bf16[2,4,16,1152]{3,2,1,0:T(8,128)(2,1)} %refs_1_.1), channel_id=1, source_target_pairs={{0,4},{1,5},{2,6},{3,7},{4,0},{5,1},{6,2},{7,3},{8,12},{9,13},{10,... | collective-permute-start | bytes 884744 | tf_op jit(solution)/shard_map/ppermute | solution.py:43
  6.8 13.1 %collective-permute-start.3 = (bf16[2,4,16,1152]{3,2,1,0:T(8,128)(2,1)}, bf16[2,4,16,1152]{3,2,1,0:T(8,128)(2,1)S(1)}, u32[]{:S(2)}, u32[]{:S(2)}) collective-permute-start(bf16[2,4,16,1152]{3,2,1,0:T(8,128)(2,1)} %refs_0_.4), channel_id=1, source_target_pairs={{0,4},{1,5},{2,6},{3,7},{4,0},{5,1},{6,2},{7,3},{8,12},{9,13},{10,... | collective-permute-start | bytes 884744 | tf_op jit(solution)/shard_map/ppermute | solution.py:43
  7.2 12.7 %collective-permute-start.4 = (bf16[2,4,16,1152]{3,2,1,0:T(8,128)(2,1)}, bf16[2,4,16,1152]{3,2,1,0:T(8,128)(2,1)S(1)}, u32[]{:S(2)}, u32[]{:S(2)}) collective-permute-start(bf16[2,4,16,1152]{3,2,1,0:T(8,128)(2,1)} %refs_0_.4), channel_id=1, source_target_pairs={{0,16},{1,17},{2,18},{3,19},{4,8},{5,9},{6,10},{7,11},{8,4},{9,5},... | collective-permute-start | bytes 884744 | tf_op jit(solution)/shard_map/ppermute | solution.py:43
  8.3 0.7 %copy-start.6 = (s32[16,8]{0,1:T(8,128)S(1)}, s32[16,8]{0,1:T(8,128)}, u32[]{:S(2)}) copy-start(s32[16,8]{0,1:T(8,128)} %param.13) | copy-start | bytes 1540
  9.0 1.0 %copy-start.2 = (bf16[2,4,16,1152]{3,2,1,0:T(8,128)(2,1)S(1)}, bf16[2,4,16,1152]{3,2,1,0:T(8,128)(2,1)}, u32[]{:S(2)}) copy-start(bf16[2,4,16,1152]{3,2,1,0:T(8,128)(2,1)} %refs_0_.3) | copy-start | bytes 884740
  10.0 1.0 %copy-start.3 = (bf16[2,4,16,1152]{3,2,1,0:T(8,128)(2,1)S(1)}, bf16[2,4,16,1152]{3,2,1,0:T(8,128)(2,1)}, u32[]{:S(2)}) copy-start(bf16[2,4,16,1152]{3,2,1,0:T(8,128)(2,1)} %refs_2_.1) | copy-start | bytes 884740
  11.0 1.0 %copy-start.4 = (bf16[2,4,16,1152]{3,2,1,0:T(8,128)(2,1)S(1)}, bf16[2,4,16,1152]{3,2,1,0:T(8,128)(2,1)}, u32[]{:S(2)}) copy-start(bf16[2,4,16,1152]{3,2,1,0:T(8,128)(2,1)} %refs_1_.1) | copy-start | bytes 884740
  12.8 7.7 %collective-permute-start.6 = (bf16[2,4,16,1152]{3,2,1,0:T(8,128)(2,1)S(1)}, bf16[2,4,16,1152]{3,2,1,0:T(8,128)(2,1)S(1)}, u32[]{:S(2)}, u32[]{:S(2)}) collective-permute-start(bf16[2,4,16,1152]{3,2,1,0:T(8,128)(2,1)S(1)} %get-tuple-element.17.refs_0_), channel_id=1, source_target_pairs={{0,2},{1,3},{2,0},{3,1},{4,6},{5,7},{6,4},{7,5},{8,10},{9,11},{10,... | collective-permute-start | bytes 884744 | tf_op jit(solution)/shard_map/ppermute | solution.py:47
  15.3 1.1 %copy-start = (bf16[2,4,16,1152]{3,2,1,0:T(8,128)(2,1)S(1)}, bf16[2,4,16,1152]{3,2,1,0:T(8,128)(2,1)}, u32[]{:S(2)}) copy-start(bf16[2,4,16,1152]{3,2,1,0:T(8,128)(2,1)} %refs_0_.5) | copy-start | bytes 884740
  16.4 4.2 %copy-start.1 = (bf16[2,4,16,1152]{3,2,1,0:T(8,128)(2,1)S(1)}, bf16[2,4,16,1152]{3,2,1,0:T(8,128)(2,1)}, u32[]{:S(2)}) copy-start(bf16[2,4,16,1152]{3,2,1,0:T(8,128)(2,1)} %refs_0_.4) | copy-start | bytes 884740
  16.4 5.4 %collective-permute-start.5 = (bf16[4,4,16,1152]{3,2,1,0:T(8,128)(2,1)S(1)}, bf16[4,4,16,1152]{3,2,1,0:T(8,128)(2,1)S(1)}, u32[]{:S(2)}, u32[]{:S(2)}) collective-permute-start(bf16[4,4,16,1152]{3,2,1,0:T(8,128)(2,1)S(1)} %join.2.refs_0_), channel_id=1, source_target_pairs={{0,1},{1,0},{2,3},{3,2},{4,5},{5,4},{6,7},{7,6},{8,9},{9,8},{10,11... | collective-permute-start | bytes 1769480 | tf_op jit(solution)/shard_map/ppermute | solution.py:47
  20.6 2.3 %collective-permute-start.7 = (bf16[4,4,16,1152]{3,2,1,0:T(8,128)(2,1)S(1)}, bf16[4,4,16,1152]{3,2,1,0:T(8,128)(2,1)S(1)}, u32[]{:S(2)}, u32[]{:S(2)}) collective-permute-start(bf16[4,4,16,1152]{3,2,1,0:T(8,128)(2,1)S(1)} %join.3.refs_0_), channel_id=1, source_target_pairs={{0,1},{1,0},{2,3},{3,2},{4,5},{5,4},{6,7},{7,6},{8,9},{9,8},{10,11... | collective-permute-start | bytes 1769480 | tf_op jit(solution)/shard_map/ppermute | solution.py:47
  20.7 1.2 %copy-start.5 = (bf16[2,4,16,1152]{3,2,1,0:T(8,128)(2,1)S(1)}, bf16[2,4,16,1152]{3,2,1,0:T(8,128)(2,1)}, u32[]{:S(2)}) copy-start(bf16[2,4,16,1152]{3,2,1,0:T(8,128)(2,1)} %q_ref.1) | copy-start | bytes 884740

commit v7 on v6

--- a/solution.py
+++ b/solution.py
@@ -118,7 +118,7 @@
     index = index_ref[0]
     key_rows = []
     for distance in range(blocks // 2 + 1):
-        for parity in range(2 if distance else 1):
+        for parity in (1, 0) if distance else (0,):
             owner = partner_of(index, distance, parity) if distance else index
             first = jnp.where((owner >= 0) & (owner < space), owner * rows, -(2**20))
             row = lax.broadcasted_iota(jnp.int32, (columns, rows * columns), 1) // columns
@@ -146,7 +146,7 @@
         + [pl.BlockSpec(memory_space=pl.ANY)] * len(arrays),
         out_specs=(in_vmem,) * (1 + len(arrays)),
         scratch_shapes=[pltpu.SemaphoreType.DMA((len(arrays),))],
-        compiler_params=pltpu.CompilerParams(vmem_limit_bytes=40 * 1024 * 1024),
+        compiler_params=pltpu.CompilerParams(vmem_limit_bytes=53 * 1024 * 1024),
         cost_estimate=pl.CostEstimate(flops=1, bytes_accessed=1, transcendentals=0),
         name="stage",
     )(index, lists, *arrays)
@@ -269,7 +269,7 @@
     tokens = frames * rows * columns
     first_step = lax.axis_size("tm") // 2
 
-    exchanges = [(d, parity) for d in range(1, reach + 1) for parity in range(2)]
+    exchanges = [(d, parity) for d in range(1, reach + 1) for parity in (1, 0)]
     blocks = 1 + len(exchanges)
     bias, own_q, own_k, own_tv = staged(
         [spatial_q, spatial_k, temporal_v], index, key_lists.T, blocks, space

time: 24.3 us -> 23.6 us (0.971)
  local copies, waits for them, and re-layouts: 3.59 us -> 0.7 us
  starting transfers between devices: 8.45 us -> 9.62 us
  Pallas kernels: 5.37 us -> 6.22 us
  waiting for transfers between devices: 5.9 us -> 6.15 us
    unnamed x14 -> x8, local copies, waits for them, and re-layouts: 3.59 us -> 0.7 us
    ppermute x4, starting transfers between devices: 3.75 us -> 4.86 us  [swapped(): lax.ppermute(value, axis, [(i, i ^ step) for i in range(lax.axis_size(axi...]
    ppermute x4, waiting for transfers between devices: 5.23 us -> 6.14 us  [exchanged(): return lax.ppermute(value, AXES, pairs)]
    pallas_call x1, Pallas kernels: 0.91 us -> 1.77 us  [staged(): pl.pallas_call(functools.partial(stage_kernel, blocks, space), out_shape=...]
    ppermute x4, waiting for transfers between devices: 0.67 us -> 0.01 us  [swapped(): lax.ppermute(value, axis, [(i, i ^ step) for i in range(lax.axis_size(axi...]
  transfers between devices with their start and end apart: 8 -> 8, of which waited for: 4 -> 3; matrix products, arithmetic and copies ran while one was open for 0% -> 0% of each run, Pallas kernels for 18% -> 22%
where the time goes in v7:
time: 23.6 us; the launch traced here: 23.4 us
  starting transfers between devices  9.62 us (41%)
  Pallas kernels  6.22 us (26%)
  waiting for transfers between devices  6.15 us (26%)
  between operations  0.74 us (3%)
  local copies, waits for them, and re-layouts  0.7 us (3%)
    ppermute x4, waiting for transfers between devices, exchanged(): return lax.ppermute(value, AXES, pairs)  6.14 us
    ppermute x4, starting transfers between devices, swapped(): lax.ppermute(value, axis, [(i, i ^ step) for i in range(lax.axis_size(axi...  4.86 us
    ppermute x4, starting transfers between devices, exchanged(): return lax.ppermute(value, AXES, pairs)  4.76 us
    pallas_call x6, Pallas kernels, call(): pl.pallas_call(kernel, out_shape=out_shape, in_specs=[in_smem] * len(scal...  4.45 us
    pallas_call x1, Pallas kernels, staged(): pl.pallas_call(functools.partial(stage_kernel, blocks, space), out_shape=...  1.77 us
    unnamed x8, local copies, waits for them, and re-layouts  0.7 us
  transfers between devices with their start and end apart: 8, of which 3 were waited for; matrix products, arithmetic and copies ran while one was open for 0% of the time, Pallas kernels for 22%

profile of v7, /device:TPU:0, one launch (start us, length us, event | category | flops | bytes accessed | tf_op | source)
XLA Modules:
  0.0 23.4 jit_solution(7557940405958881331)
XLA Ops:
  0.6 3.0 %collective-permute-start.2 = (bf16[2,4,16,1152]{3,2,1,0:T(8,128)(2,1)}, bf16[2,4,16,1152]{3,2,1,0:T(8,128)(2,1)S(1)}, u32[]{:S(2)}, u32[]{:S(2)}) collective-permute-start(bf16[2,4,16,1152]{3,2,1,0:T(8,128)(2,1)} %refs_0_.5), channel_id=1, source_target_pairs={{0,2},{1,3},{2,0},{3,1},{4,6},{5,7},{6,4},{7,5},{8,10},{9,11},{10,... | collective-permute-start | bytes 884744 | tf_op jit(solution)/shard_map/ppermute | solution.py:47
  3.6 1.6 %collective-permute-start.1 = (bf16[2,4,16,1152]{3,2,1,0:T(8,128)(2,1)}, bf16[2,4,16,1152]{3,2,1,0:T(8,128)(2,1)S(1)}, u32[]{:S(2)}, u32[]{:S(2)}) collective-permute-start(bf16[2,4,16,1152]{3,2,1,0:T(8,128)(2,1)} %refs_1_.1), channel_id=1, source_target_pairs={{0,4},{1,5},{2,6},{3,7},{4,0},{5,1},{6,2},{7,3},{8,12},{9,13},{10,... | collective-permute-start | bytes 884744 | tf_op jit(solution)/shard_map/ppermute | solution.py:43
  5.2 1.5 %collective-permute-start = (bf16[2,4,16,1152]{3,2,1,0:T(8,128)(2,1)}, bf16[2,4,16,1152]{3,2,1,0:T(8,128)(2,1)S(1)}, u32[]{:S(2)}, u32[]{:S(2)}) collective-permute-start(bf16[2,4,16,1152]{3,2,1,0:T(8,128)(2,1)} %refs_1_.1), channel_id=1, source_target_pairs={{0,16},{1,17},{2,18},{3,19},{4,8},{5,9},{6,10},{7,11},{8,4},{9,5},... | collective-permute-start | bytes 884744 | tf_op jit(solution)/shard_map/ppermute | solution.py:43
  6.7 0.5 %collective-permute-start.3 = (bf16[2,4,16,1152]{3,2,1,0:T(8,128)(2,1)}, bf16[2,4,16,1152]{3,2,1,0:T(8,128)(2,1)S(1)}, u32[]{:S(2)}, u32[]{:S(2)}) collective-permute-start(bf16[2,4,16,1152]{3,2,1,0:T(8,128)(2,1)} %refs_0_.4), channel_id=1, source_target_pairs={{0,16},{1,17},{2,18},{3,19},{4,8},{5,9},{6,10},{7,11},{8,4},{9,5},... | collective-permute-start | bytes 884744 | tf_op jit(solution)/shard_map/ppermute | solution.py:43
  7.2 1.2 %collective-permute-start.4 = (bf16[2,4,16,1152]{3,2,1,0:T(8,128)(2,1)}, bf16[2,4,16,1152]{3,2,1,0:T(8,128)(2,1)S(1)}, u32[]{:S(2)}, u32[]{:S(2)}) collective-permute-start(bf16[2,4,16,1152]{3,2,1,0:T(8,128)(2,1)} %refs_0_.4), channel_id=1, source_target_pairs={{0,4},{1,5},{2,6},{3,7},{4,0},{5,1},{6,2},{7,3},{8,12},{9,13},{10,... | collective-permute-start | bytes 884744 | tf_op jit(solution)/shard_map/ppermute | solution.py:43
  8.4 0.0 copy-start.3
  8.4 0.7 %copy-done.3 = s32[16,8]{0,1:T(8,128)S(1)} copy-done((s32[16,8]{0,1:T(8,128)S(1)}, s32[16,8]{0,1:T(8,128)}, u32[]{:S(2)}) %copy-start.3) | copy-done | bytes 536
  9.1 1.8 %stage.1 = (f32[64,192]{1,0:T(8,128)S(1)}, bf16[2,4,16,1152]{3,2,1,0:T(8,128)(2,1)S(1)}, bf16[2,4,16,1152]{3,2,1,0:T(8,128)(2,1)S(1)}, bf16[2,4,16,1152]{3,2,1,0:T(8,128)(2,1)S(1)}) custom-call(s32[1]{0:T(128)} %bitcast.index_ref, s32[8,16]{1,0:T(8,128)S(1)} %bitcast.2, bf16[2,4,16,1152]{3,2,1,0:T(8,128)(2,1)} %refs_0_.3, bf16[2,4,16,1152]{3,2,1,0:T(8,128)(2,1)} %refs_1_.1, ...), custom_call_target="tpu_custom_call" | custom-call | flops 1 | bytes 1 | tf_op jit(solution)/shard_map/stage/pallas_call | solution.py:142
  10.9 0.0 collective-permute-done.2.refs_3_.refs_1_
  10.9 1.7 %collective-permute-start.6 = (bf16[2,4,16,1152]{3,2,1,0:T(8,128)(2,1)S(1)}, bf16[2,4,16,1152]{3,2,1,0:T(8,128)(2,1)S(1)}, u32[]{:S(2)}, u32[]{:S(2)}) collective-permute-start(bf16[2,4,16,1152]{3,2,1,0:T(8,128)(2,1)S(1)} %get-tuple-element.17.refs_0_), channel_id=1, source_target_pairs={{0,2},{1,3},{2,0},{3,1},{4,6},{5,7},{6,4},{7,5},{8,10},{9,11},{10,... | collective-permute-start | bytes 884744 | tf_op jit(solution)/shard_map/ppermute | solution.py:47
  12.6 1.2 %collective-permute-done.1.refs_2_ = bf16[2,4,16,1152]{3,2,1,0:T(8,128)(2,1)S(1)} collective-permute-done((bf16[2,4,16,1152]{3,2,1,0:T(8,128)(2,1)}, bf16[2,4,16,1152]{3,2,1,0:T(8,128)(2,1)S(1)}, u32[]{:S(2)}, u32[]{:S(2)}) %collective-permute-start.1) | collective-permute-done | bytes 294944 | tf_op jit(solution)/shard_map/ppermute | solution.py:43
  13.8 1.6 %collective-permute-done.refs_1_ = bf16[2,4,16,1152]{3,2,1,0:T(8,128)(2,1)S(1)} collective-permute-done((bf16[2,4,16,1152]{3,2,1,0:T(8,128)(2,1)}, bf16[2,4,16,1152]{3,2,1,0:T(8,128)(2,1)S(1)}, u32[]{:S(2)}, u32[]{:S(2)}) %collective-permute-start) | collective-permute-done | bytes 294944 | tf_op jit(solution)/shard_map/ppermute | solution.py:43
  15.4 0.0 copy-start
  15.4 1.0 %spatial_weigh.1 = (bf16[2,8,128,192]{3,2,1,0:T(8,128)(2,1)S(1)}, f32[2,8,64,256]{3,2,1,0:T(8,128)S(1)}) custom-call(f32[64,192]{1,0:T(8,128)S(1)} %get-tuple-element.10.bias_ref, bf16[2,4,16,1152]{3,2,1,0:T(8,128)(2,1)S(1)} %get-tuple-element.11.q_ref, bf16[2,4,16,1152]{3,2,1,0:T(8,128)(2,1)S(1)} %get-tuple-element.12.refs_0_, ...), custom_call_target="tpu_custom_call" | custom-call | flops 1 | bytes 1 | tf_op jit(solution)/shard_map/spatial_weigh/pallas_call | solution.py:221
  16.4 0.0 copy-done
  16.5 0.0 copy-start.1
  16.5 0.1 collective-permute-start.5
  16.6 3.4 %collective-permute-done.3.refs_1_.refs_3_ = bf16[2,4,16,1152]{3,2,1,0:T(8,128)(2,1)S(1)} collective-permute-done((bf16[2,4,16,1152]{3,2,1,0:T(8,128)(2,1)}, bf16[2,4,16,1152]{3,2,1,0:T(8,128)(2,1)S(1)}, u32[]{:S(2)}, u32[]{:S(2)}) %collective-permute-start.3) | collective-permute-done | bytes 294944 | tf_op jit(solution)/shard_map/ppermute | solution.py:43
  19.9 0.0 collective-permute-done.4.refs_2_.refs_4_
  19.9 0.0 collective-permute-done.6.refs_1_
  20.0 0.1 collective-permute-start.7
  20.1 0.0 copy-done.1
  20.1 0.0 copy-start.2
  20.1 1.1 %spatial_blend.1 = bf16[2,4,16,1152]{3,2,1,0:T(8,128)(2,1)} custom-call(bf16[2,8,128,192]{3,2,1,0:T(8,128)(2,1)S(1)} %get-tuple-element.13.weights_ref.refs_2_, f32[2,8,64,256]{3,2,1,0:T(8,128)S(1)} %get-tuple-element.14.inverse_ref, bf16[2,4,16,1152]{3,2,1,0:T(8,128)(2,1)S(1)} %copy-done.1, ...), custom_call_target="tpu_custom_call" | custom-call | flops 1 | bytes 1 | tf_op jit(solution)/shard_map/spatial_blend/pallas_call | solution.py:221
  21.2 0.0 collective-permute-done.5.refs_1_
  21.2 0.0 copy-done.2
  21.2 1.0 %temporal_weigh.1 = (bf16[4,8,64,128]{3,2,1,0:T(8,128)(2,1)S(1)}, f32[4,8,32,256]{3,2,1,0:T(8,128)S(1)}) custom-call(bf16[2,4,16,1152]{3,2,1,0:T(8,128)(2,1)S(1)} %copy-done.2, bf16[4,4,16,1152]{3,2,1,0:T(8,128)(2,1)S(1)} %join.2.refs_0_, bf16[4,4,16,1152]{3,2,1,0:T(8,128)(2,1)S(1)} %collective-permute-done.5.refs_1_), custom_call_target="tpu_custom_call" | custom-call | flops 1 | bytes 1 | tf_op jit(solution)/shard_map/temporal_weigh/pallas_call | solution.py:221
  22.3 0.0 collective-permute-done.7.refs_1_
  22.3 1.1 %temporal_blend.1 = bf16[2,4,16,1152]{3,2,1,0:T(8,128)(2,1)} custom-call(bf16[4,8,64,128]{3,2,1,0:T(8,128)(2,1)S(1)} %get-tuple-element.15.weights_ref, f32[4,8,32,256]{3,2,1,0:T(8,128)S(1)} %get-tuple-element.16.inverse_ref, bf16[4,4,16,1152]{3,2,1,0:T(8,128)(2,1)S(1)} %join.3.refs_0_, bf16[4,4,16,1152]{3,2,1,0:T(8,128)(2,1)S(1)} %collective-permute-done.7.refs_1_), custom_call_target="tpu_custom_call" | custom-call | flops 1 | bytes 1 | tf_op jit(solution)/shard_map/temporal_blend/pallas_call | solution.py:221
  (2 shorter events, 0.1 us)
Async XLA Ops:
  0.6 10.2 %collective-permute-start.2 = (bf16[2,4,16,1152]{3,2,1,0:T(8,128)(2,1)}, bf16[2,4,16,1152]{3,2,1,0:T(8,128)(2,1)S(1)}, u32[]{:S(2)}, u32[]{:S(2)}) collective-permute-start(bf16[2,4,16,1152]{3,2,1,0:T(8,128)(2,1)} %refs_0_.5), channel_id=1, source_target_pairs={{0,2},{1,3},{2,0},{3,1},{4,6},{5,7},{6,4},{7,5},{8,10},{9,11},{10,... | collective-permute-start | bytes 884744 | tf_op jit(solution)/shard_map/ppermute | solution.py:47
  3.6 10.1 %collective-permute-start.1 = (bf16[2,4,16,1152]{3,2,1,0:T(8,128)(2,1)}, bf16[2,4,16,1152]{3,2,1,0:T(8,128)(2,1)S(1)}, u32[]{:S(2)}, u32[]{:S(2)}) collective-permute-start(bf16[2,4,16,1152]{3,2,1,0:T(8,128)(2,1)} %refs_1_.1), channel_id=1, source_target_pairs={{0,4},{1,5},{2,6},{3,7},{4,0},{5,1},{6,2},{7,3},{8,12},{9,13},{10,... | collective-permute-start | bytes 884744 | tf_op jit(solution)/shard_map/ppermute | solution.py:43
  5.2 10.2 %collective-permute-start = (bf16[2,4,16,1152]{3,2,1,0:T(8,128)(2,1)}, bf16[2,4,16,1152]{3,2,1,0:T(8,128)(2,1)S(1)}, u32[]{:S(2)}, u32[]{:S(2)}) collective-permute-start(bf16[2,4,16,1152]{3,2,1,0:T(8,128)(2,1)} %refs_1_.1), channel_id=1, source_target_pairs={{0,16},{1,17},{2,18},{3,19},{4,8},{5,9},{6,10},{7,11},{8,4},{9,5},... | collective-permute-start | bytes 884744 | tf_op jit(solution)/shard_map/ppermute | solution.py:43
  6.7 13.2 %collective-permute-start.3 = (bf16[2,4,16,1152]{3,2,1,0:T(8,128)(2,1)}, bf16[2,4,16,1152]{3,2,1,0:T(8,128)(2,1)S(1)}, u32[]{:S(2)}, u32[]{:S(2)}) collective-permute-start(bf16[2,4,16,1152]{3,2,1,0:T(8,128)(2,1)} %refs_0_.4), channel_id=1, source_target_pairs={{0,16},{1,17},{2,18},{3,19},{4,8},{5,9},{6,10},{7,11},{8,4},{9,5},... | collective-permute-start | bytes 884744 | tf_op jit(solution)/shard_map/ppermute | solution.py:43
  7.2 12.7 %collective-permute-start.4 = (bf16[2,4,16,1152]{3,2,1,0:T(8,128)(2,1)}, bf16[2,4,16,1152]{3,2,1,0:T(8,128)(2,1)S(1)}, u32[]{:S(2)}, u32[]{:S(2)}) collective-permute-start(bf16[2,4,16,1152]{3,2,1,0:T(8,128)(2,1)} %refs_0_.4), channel_id=1, source_target_pairs={{0,4},{1,5},{2,6},{3,7},{4,0},{5,1},{6,2},{7,3},{8,12},{9,13},{10,... | collective-permute-start | bytes 884744 | tf_op jit(solution)/shard_map/ppermute | solution.py:43
  8.4 0.7 %copy-start.3 = (s32[16,8]{0,1:T(8,128)S(1)}, s32[16,8]{0,1:T(8,128)}, u32[]{:S(2)}) copy-start(s32[16,8]{0,1:T(8,128)} %param.13) | copy-start | bytes 1540
  10.9 9.1 %collective-permute-start.6 = (bf16[2,4,16,1152]{3,2,1,0:T(8,128)(2,1)S(1)}, bf16[2,4,16,1152]{3,2,1,0:T(8,128)(2,1)S(1)}, u32[]{:S(2)}, u32[]{:S(2)}) collective-permute-start(bf16[2,4,16,1152]{3,2,1,0:T(8,128)(2,1)S(1)} %get-tuple-element.17.refs_0_), channel_id=1, source_target_pairs={{0,2},{1,3},{2,0},{3,1},{4,6},{5,7},{6,4},{7,5},{8,10},{9,11},{10,... | collective-permute-start | bytes 884744 | tf_op jit(solution)/shard_map/ppermute | solution.py:47
  15.4 1.1 %copy-start = (bf16[2,4,16,1152]{3,2,1,0:T(8,128)(2,1)S(1)}, bf16[2,4,16,1152]{3,2,1,0:T(8,128)(2,1)}, u32[]{:S(2)}) copy-start(bf16[2,4,16,1152]{3,2,1,0:T(8,128)(2,1)} %refs_0_.5) | copy-start | bytes 884740
  16.5 3.6 %copy-start.1 = (bf16[2,4,16,1152]{3,2,1,0:T(8,128)(2,1)S(1)}, bf16[2,4,16,1152]{3,2,1,0:T(8,128)(2,1)}, u32[]{:S(2)}) copy-start(bf16[2,4,16,1152]{3,2,1,0:T(8,128)(2,1)} %refs_0_.4) | copy-start | bytes 884740
  16.5 4.7 %collective-permute-start.5 = (bf16[4,4,16,1152]{3,2,1,0:T(8,128)(2,1)S(1)}, bf16[4,4,16,1152]{3,2,1,0:T(8,128)(2,1)S(1)}, u32[]{:S(2)}, u32[]{:S(2)}) collective-permute-start(bf16[4,4,16,1152]{3,2,1,0:T(8,128)(2,1)S(1)} %join.2.refs_0_), channel_id=1, source_target_pairs={{0,1},{1,0},{2,3},{3,2},{4,5},{5,4},{6,7},{7,6},{8,9},{9,8},{10,11... | collective-permute-start | bytes 1769480 | tf_op jit(solution)/shard_map/ppermute | solution.py:47
  20.0 2.3 %collective-permute-start.7 = (bf16[4,4,16,1152]{3,2,1,0:T(8,128)(2,1)S(1)}, bf16[4,4,16,1152]{3,2,1,0:T(8,128)(2,1)S(1)}, u32[]{:S(2)}, u32[]{:S(2)}) collective-permute-start(bf16[4,4,16,1152]{3,2,1,0:T(8,128)(2,1)S(1)} %join.3.refs_0_), channel_id=1, source_target_pairs={{0,1},{1,0},{2,3},{3,2},{4,5},{5,4},{6,7},{7,6},{8,9},{9,8},{10,11... | collective-permute-start | bytes 1769480 | tf_op jit(solution)/shard_map/ppermute | solution.py:47
  20.1 1.2 %copy-start.2 = (bf16[2,4,16,1152]{3,2,1,0:T(8,128)(2,1)S(1)}, bf16[2,4,16,1152]{3,2,1,0:T(8,128)(2,1)}, u32[]{:S(2)}) copy-start(bf16[2,4,16,1152]{3,2,1,0:T(8,128)(2,1)} %q_ref.1) | copy-start | bytes 884740

commit v8 on v7

--- a/solution.py
+++ b/solution.py
@@ -166,20 +166,33 @@
 
 
 def spatial_blend_kernel(blocks, weights_ref, inverse_ref, *refs):
-    v_refs, out_ref = refs[:blocks], refs[blocks]
-    frames, rows, columns, channels = out_ref.shape
+    v_refs, (out_ref, held, sems) = refs[:blocks], refs[-3:]
+    frames, rows, columns, channels = held.shape
+    pairs = channels // PAIR
+    moves = []
     for frame in range(frames):
+        sent = 0
 
         def write(lanes, value):
-            out_ref[frame, :, :, lanes] = value.reshape(rows, columns, LANES)
+            nonlocal sent
+            held[frame, :, :, lanes] = value.reshape(rows, columns, LANES)
+            if lanes.stop in (channels // 2 // LANES * LANES, channels):
+                part = (frame, slice(None), slice(None), slice(sent, lanes.stop))
+                moves.append(
+                    pltpu.make_async_copy(held.at[part], out_ref.at[part], sems.at[len(moves)])
+                )
+                moves[-1].start()
+                sent = lanes.stop
 
         blend_pairs(
-            channels // PAIR,
+            pairs,
             lambda pair: weights_ref[frame, pair],
             lambda pair: inverse_ref[frame, pair],
             lambda lanes: read_tokens(v_refs, frame, lanes),
             write,
         )
+    for move in moves:
+        move.wait()
 
 
 def temporal_weigh_kernel(blocks, q_ref, *refs):
@@ -198,12 +211,13 @@
 
 
 def temporal_blend_kernel(blocks, weights_ref, inverse_ref, *refs):
-    v_refs, out_ref = refs[:blocks], refs[blocks]
-    frames, rows, columns, channels = out_ref.shape
+    v_refs, (out_ref, held, sems) = refs[:blocks], refs[-3:]
+    frames, rows, columns, channels = held.shape
+    moves = []
     for row in range(rows):
 
         def write(lanes, value):
-            out_ref[:, row, :, lanes] = value.reshape(frames, columns, LANES)
+            held[:, row, :, lanes] = value.reshape(frames, columns, LANES)
 
         blend_pairs(
             channels // PAIR,
@@ -212,9 +226,15 @@
             lambda lanes: read_row(v_refs, row, lanes),
             write,
         )
-
-
-def call(kernel, name, out_shape, scalars, arrays, flops, others=()):
+        moves.append(
+            pltpu.make_async_copy(held.at[:, row], out_ref.at[:, row], sems.at[row])
+        )
+        moves[-1].start()
+    for move in moves:
+        move.wait()
+
+
+def call(kernel, name, out_shape, scalars, arrays, flops, others=(), parts=0):
     in_vmem = pl.BlockSpec(memory_space=pltpu.VMEM)
     in_smem = pl.BlockSpec(memory_space=pltpu.SMEM)
     anywhere = pl.BlockSpec(memory_space=pl.ANY)
@@ -222,7 +242,13 @@
         kernel,
         out_shape=out_shape,
         in_specs=[in_smem] * len(scalars) + [in_vmem] * len(arrays) + [anywhere] * len(others),
-        out_specs=jax.tree.map(lambda _: in_vmem, out_shape),
+        out_specs=jax.tree.map(lambda _: anywhere if parts else in_vmem, out_shape),
+        scratch_shapes=[
+            pltpu.VMEM(out_shape.shape, out_shape.dtype),
+            pltpu.SemaphoreType.DMA((parts,)),
+        ]
+        if parts
+        else [],
         compiler_params=pltpu.CompilerParams(vmem_limit_bytes=40 * 1024 * 1024),
         cost_estimate=pl.CostEstimate(
             flops=flops, bytes_accessed=1, transcendentals=0
@@ -319,6 +345,7 @@
         [],
         [spatial_weights, spatial_inverse, *spatial_values],
         1,
+        parts=2 * frames,
     )
     temporal_out = call(
         functools.partial(temporal_blend_kernel, blocks),
@@ -327,6 +354,7 @@
         [],
         [temporal_weights, temporal_inverse, *temporal_values],
         1,
+        parts=rows,
     )
     return (spatial_out, temporal_out)
 

time: 23.6 us -> 23.6 us (level)
  transfers between devices with their start and end apart: 8 -> 8, of which waited for: 3 -> 3; matrix products, arithmetic and copies ran while one was open for 0% -> 0% of each run, Pallas kernels for 22% -> 21%
where the time goes in v8:
time: 23.6 us; the launch traced here: 23.4 us
  starting transfers between devices  9.62 us (41%)
  waiting for transfers between devices  6.15 us (26%)
  Pallas kernels  6.14 us (26%)
  between operations  0.76 us (3%)
  local copies, waits for them, and re-layouts  0.7 us (3%)
    ppermute x4, waiting for transfers between devices, exchanged(): return lax.ppermute(value, AXES, pairs)  6.14 us
    ppermute x4, starting transfers between devices, swapped(): lax.ppermute(value, axis, [(i, i ^ step) for i in range(lax.axis_size(axi...  4.86 us
    ppermute x4, starting transfers between devices, exchanged(): return lax.ppermute(value, AXES, pairs)  4.76 us
    pallas_call x6, Pallas kernels, call(): pl.pallas_call(kernel, out_shape=out_shape, in_specs=[in_smem] * len(scal...  4.36 us
    pallas_call x1, Pallas kernels, staged(): pl.pallas_call(functools.partial(stage_kernel, blocks, space), out_shape=...  1.77 us
    unnamed x8, local copies, waits for them, and re-layouts  0.7 us
  transfers between devices with their start and end apart: 8, of which 3 were waited for; matrix products, arithmetic and copies ran while one was open for 0% of the time, Pallas kernels for 21%

profile of v8, /device:TPU:0, one launch (start us, length us, event | category | flops | bytes accessed | tf_op | source)
XLA Modules:
  0.0 23.4 jit_solution(12862448329975460904)
XLA Ops:
  0.6 3.0 %collective-permute-start.2 = (bf16[2,4,16,1152]{3,2,1,0:T(8,128)(2,1)}, bf16[2,4,16,1152]{3,2,1,0:T(8,128)(2,1)S(1)}, u32[]{:S(2)}, u32[]{:S(2)}) collective-permute-start(bf16[2,4,16,1152]{3,2,1,0:T(8,128)(2,1)} %refs_0_.5), channel_id=1, source_target_pairs={{0,2},{1,3},{2,0},{3,1},{4,6},{5,7},{6,4},{7,5},{8,10},{9,11},{10,... | collective-permute-start | bytes 884744 | tf_op jit(solution)/shard_map/ppermute | solution.py:47
  3.6 1.6 %collective-permute-start.1 = (bf16[2,4,16,1152]{3,2,1,0:T(8,128)(2,1)}, bf16[2,4,16,1152]{3,2,1,0:T(8,128)(2,1)S(1)}, u32[]{:S(2)}, u32[]{:S(2)}) collective-permute-start(bf16[2,4,16,1152]{3,2,1,0:T(8,128)(2,1)} %refs_1_.1), channel_id=1, source_target_pairs={{0,4},{1,5},{2,6},{3,7},{4,0},{5,1},{6,2},{7,3},{8,12},{9,13},{10,... | collective-permute-start | bytes 884744 | tf_op jit(solution)/shard_map/ppermute | solution.py:43
  5.2 1.5 %collective-permute-start = (bf16[2,4,16,1152]{3,2,1,0:T(8,128)(2,1)}, bf16[2,4,16,1152]{3,2,1,0:T(8,128)(2,1)S(1)}, u32[]{:S(2)}, u32[]{:S(2)}) collective-permute-start(bf16[2,4,16,1152]{3,2,1,0:T(8,128)(2,1)} %refs_1_.1), channel_id=1, source_target_pairs={{0,16},{1,17},{2,18},{3,19},{4,8},{5,9},{6,10},{7,11},{8,4},{9,5},... | collective-permute-start | bytes 884744 | tf_op jit(solution)/shard_map/ppermute | solution.py:43
  6.7 0.5 %collective-permute-start.3 = (bf16[2,4,16,1152]{3,2,1,0:T(8,128)(2,1)}, bf16[2,4,16,1152]{3,2,1,0:T(8,128)(2,1)S(1)}, u32[]{:S(2)}, u32[]{:S(2)}) collective-permute-start(bf16[2,4,16,1152]{3,2,1,0:T(8,128)(2,1)} %refs_0_.4), channel_id=1, source_target_pairs={{0,16},{1,17},{2,18},{3,19},{4,8},{5,9},{6,10},{7,11},{8,4},{9,5},... | collective-permute-start | bytes 884744 | tf_op jit(solution)/shard_map/ppermute | solution.py:43
  7.2 1.2 %collective-permute-start.4 = (bf16[2,4,16,1152]{3,2,1,0:T(8,128)(2,1)}, bf16[2,4,16,1152]{3,2,1,0:T(8,128)(2,1)S(1)}, u32[]{:S(2)}, u32[]{:S(2)}) collective-permute-start(bf16[2,4,16,1152]{3,2,1,0:T(8,128)(2,1)} %refs_0_.4), channel_id=1, source_target_pairs={{0,4},{1,5},{2,6},{3,7},{4,0},{5,1},{6,2},{7,3},{8,12},{9,13},{10,... | collective-permute-start | bytes 884744 | tf_op jit(solution)/shard_map/ppermute | solution.py:43
  8.4 0.0 copy-start.3
  8.4 0.7 %copy-done.3 = s32[16,8]{0,1:T(8,128)S(1)} copy-done((s32[16,8]{0,1:T(8,128)S(1)}, s32[16,8]{0,1:T(8,128)}, u32[]{:S(2)}) %copy-start.3) | copy-done | bytes 536
  9.1 1.8 %stage.1 = (f32[64,192]{1,0:T(8,128)S(1)}, bf16[2,4,16,1152]{3,2,1,0:T(8,128)(2,1)S(1)}, bf16[2,4,16,1152]{3,2,1,0:T(8,128)(2,1)S(1)}, bf16[2,4,16,1152]{3,2,1,0:T(8,128)(2,1)S(1)}) custom-call(s32[1]{0:T(128)} %bitcast.index_ref, s32[8,16]{1,0:T(8,128)S(1)} %bitcast.2, bf16[2,4,16,1152]{3,2,1,0:T(8,128)(2,1)} %refs_0_.3, bf16[2,4,16,1152]{3,2,1,0:T(8,128)(2,1)} %refs_1_.1, ...), custom_call_target="tpu_custom_call" | custom-call | flops 1 | bytes 1 | tf_op jit(solution)/shard_map/stage/pallas_call | solution.py:142
  10.9 0.0 collective-permute-done.2.refs_3_.refs_1_
  10.9 1.7 %collective-permute-start.6 = (bf16[2,4,16,1152]{3,2,1,0:T(8,128)(2,1)S(1)}, bf16[2,4,16,1152]{3,2,1,0:T(8,128)(2,1)S(1)}, u32[]{:S(2)}, u32[]{:S(2)}) collective-permute-start(bf16[2,4,16,1152]{3,2,1,0:T(8,128)(2,1)S(1)} %get-tuple-element.17.refs_0_), channel_id=1, source_target_pairs={{0,2},{1,3},{2,0},{3,1},{4,6},{5,7},{6,4},{7,5},{8,10},{9,11},{10,... | collective-permute-start | bytes 884744 | tf_op jit(solution)/shard_map/ppermute | solution.py:47
  12.6 1.2 %collective-permute-done.1.refs_2_ = bf16[2,4,16,1152]{3,2,1,0:T(8,128)(2,1)S(1)} collective-permute-done((bf16[2,4,16,1152]{3,2,1,0:T(8,128)(2,1)}, bf16[2,4,16,1152]{3,2,1,0:T(8,128)(2,1)S(1)}, u32[]{:S(2)}, u32[]{:S(2)}) %collective-permute-start.1) | collective-permute-done | bytes 294944 | tf_op jit(solution)/shard_map/ppermute | solution.py:43
  13.8 1.6 %collective-permute-done.refs_1_ = bf16[2,4,16,1152]{3,2,1,0:T(8,128)(2,1)S(1)} collective-permute-done((bf16[2,4,16,1152]{3,2,1,0:T(8,128)(2,1)}, bf16[2,4,16,1152]{3,2,1,0:T(8,128)(2,1)S(1)}, u32[]{:S(2)}, u32[]{:S(2)}) %collective-permute-start) | collective-permute-done | bytes 294944 | tf_op jit(solution)/shard_map/ppermute | solution.py:43
  15.4 0.0 copy-start
  15.4 1.0 %spatial_weigh.1 = (bf16[2,8,128,192]{3,2,1,0:T(8,128)(2,1)S(1)}, f32[2,8,64,256]{3,2,1,0:T(8,128)S(1)}) custom-call(f32[64,192]{1,0:T(8,128)S(1)} %get-tuple-element.10.bias_ref, bf16[2,4,16,1152]{3,2,1,0:T(8,128)(2,1)S(1)} %get-tuple-element.11.q_ref, bf16[2,4,16,1152]{3,2,1,0:T(8,128)(2,1)S(1)} %get-tuple-element.12.refs_0_, ...), custom_call_target="tpu_custom_call" | custom-call | flops 1 | bytes 1 | tf_op jit(solution)/shard_map/spatial_weigh/pallas_call | solution.py:241
  16.4 0.0 copy-done
  16.5 0.0 copy-start.1
  16.5 0.1 collective-permute-start.5
  16.6 3.4 %collective-permute-done.3.refs_1_.refs_3_ = bf16[2,4,16,1152]{3,2,1,0:T(8,128)(2,1)S(1)} collective-permute-done((bf16[2,4,16,1152]{3,2,1,0:T(8,128)(2,1)}, bf16[2,4,16,1152]{3,2,1,0:T(8,128)(2,1)S(1)}, u32[]{:S(2)}, u32[]{:S(2)}) %collective-permute-start.3) | collective-permute-done | bytes 294944 | tf_op jit(solution)/shard_map/ppermute | solution.py:43
  19.9 0.0 collective-permute-done.4.refs_2_.refs_4_
  19.9 0.0 collective-permute-done.6.refs_1_
  20.0 0.1 collective-permute-start.7
  20.1 0.0 copy-done.1
  20.1 0.0 copy-start.2
  20.1 1.1 %spatial_blend.1 = bf16[2,4,16,1152]{3,2,1,0:T(8,128)(2,1)} custom-call(bf16[2,8,128,192]{3,2,1,0:T(8,128)(2,1)S(1)} %get-tuple-element.13.weights_ref.refs_2_, f32[2,8,64,256]{3,2,1,0:T(8,128)S(1)} %get-tuple-element.14.inverse_ref, bf16[2,4,16,1152]{3,2,1,0:T(8,128)(2,1)S(1)} %copy-done.1, ...), custom_call_target="tpu_custom_call" | custom-call | flops 1 | bytes 1 | tf_op jit(solution)/shard_map/spatial_blend/pallas_call | solution.py:241
  21.2 0.0 collective-permute-done.5.refs_1_
  21.2 0.0 copy-done.2
  21.2 1.0 %temporal_weigh.1 = (bf16[4,8,64,128]{3,2,1,0:T(8,128)(2,1)S(1)}, f32[4,8,32,256]{3,2,1,0:T(8,128)S(1)}) custom-call(bf16[2,4,16,1152]{3,2,1,0:T(8,128)(2,1)S(1)} %copy-done.2, bf16[4,4,16,1152]{3,2,1,0:T(8,128)(2,1)S(1)} %join.2.refs_0_, bf16[4,4,16,1152]{3,2,1,0:T(8,128)(2,1)S(1)} %collective-permute-done.5.refs_1_), custom_call_target="tpu_custom_call" | custom-call | flops 1 | bytes 1 | tf_op jit(solution)/shard_map/temporal_weigh/pallas_call | solution.py:241
  22.3 0.0 collective-permute-done.7.refs_1_
  22.3 1.1 %temporal_blend.1 = bf16[2,4,16,1152]{3,2,1,0:T(8,128)(2,1)} custom-call(bf16[4,8,64,128]{3,2,1,0:T(8,128)(2,1)S(1)} %get-tuple-element.15.weights_ref, f32[4,8,32,256]{3,2,1,0:T(8,128)S(1)} %get-tuple-element.16.inverse_ref, bf16[4,4,16,1152]{3,2,1,0:T(8,128)(2,1)S(1)} %join.3.refs_0_, bf16[4,4,16,1152]{3,2,1,0:T(8,128)(2,1)S(1)} %collective-permute-done.7.refs_1_), custom_call_target="tpu_custom_call" | custom-call | flops 1 | bytes 1 | tf_op jit(solution)/shard_map/temporal_blend/pallas_call | solution.py:241
  (2 shorter events, 0.1 us)
Async XLA Ops:
  0.6 10.2 %collective-permute-start.2 = (bf16[2,4,16,1152]{3,2,1,0:T(8,128)(2,1)}, bf16[2,4,16,1152]{3,2,1,0:T(8,128)(2,1)S(1)}, u32[]{:S(2)}, u32[]{:S(2)}) collective-permute-start(bf16[2,4,16,1152]{3,2,1,0:T(8,128)(2,1)} %refs_0_.5), channel_id=1, source_target_pairs={{0,2},{1,3},{2,0},{3,1},{4,6},{5,7},{6,4},{7,5},{8,10},{9,11},{10,... | collective-permute-start | bytes 884744 | tf_op jit(solution)/shard_map/ppermute | solution.py:47
  3.6 10.1 %collective-permute-start.1 = (bf16[2,4,16,1152]{3,2,1,0:T(8,128)(2,1)}, bf16[2,4,16,1152]{3,2,1,0:T(8,128)(2,1)S(1)}, u32[]{:S(2)}, u32[]{:S(2)}) collective-permute-start(bf16[2,4,16,1152]{3,2,1,0:T(8,128)(2,1)} %refs_1_.1), channel_id=1, source_target_pairs={{0,4},{1,5},{2,6},{3,7},{4,0},{5,1},{6,2},{7,3},{8,12},{9,13},{10,... | collective-permute-start | bytes 884744 | tf_op jit(solution)/shard_map/ppermute | solution.py:43
  5.2 10.2 %collective-permute-start = (bf16[2,4,16,1152]{3,2,1,0:T(8,128)(2,1)}, bf16[2,4,16,1152]{3,2,1,0:T(8,128)(2,1)S(1)}, u32[]{:S(2)}, u32[]{:S(2)}) collective-permute-start(bf16[2,4,16,1152]{3,2,1,0:T(8,128)(2,1)} %refs_1_.1), channel_id=1, source_target_pairs={{0,16},{1,17},{2,18},{3,19},{4,8},{5,9},{6,10},{7,11},{8,4},{9,5},... | collective-permute-start | bytes 884744 | tf_op jit(solution)/shard_map/ppermute | solution.py:43
  6.7 13.2 %collective-permute-start.3 = (bf16[2,4,16,1152]{3,2,1,0:T(8,128)(2,1)}, bf16[2,4,16,1152]{3,2,1,0:T(8,128)(2,1)S(1)}, u32[]{:S(2)}, u32[]{:S(2)}) collective-permute-start(bf16[2,4,16,1152]{3,2,1,0:T(8,128)(2,1)} %refs_0_.4), channel_id=1, source_target_pairs={{0,16},{1,17},{2,18},{3,19},{4,8},{5,9},{6,10},{7,11},{8,4},{9,5},... | collective-permute-start | bytes 884744 | tf_op jit(solution)/shard_map/ppermute | solution.py:43
  7.2 12.7 %collective-permute-start.4 = (bf16[2,4,16,1152]{3,2,1,0:T(8,128)(2,1)}, bf16[2,4,16,1152]{3,2,1,0:T(8,128)(2,1)S(1)}, u32[]{:S(2)}, u32[]{:S(2)}) collective-permute-start(bf16[2,4,16,1152]{3,2,1,0:T(8,128)(2,1)} %refs_0_.4), channel_id=1, source_target_pairs={{0,4},{1,5},{2,6},{3,7},{4,0},{5,1},{6,2},{7,3},{8,12},{9,13},{10,... | collective-permute-start | bytes 884744 | tf_op jit(solution)/shard_map/ppermute | solution.py:43
  8.4 0.7 %copy-start.3 = (s32[16,8]{0,1:T(8,128)S(1)}, s32[16,8]{0,1:T(8,128)}, u32[]{:S(2)}) copy-start(s32[16,8]{0,1:T(8,128)} %param.13) | copy-start | bytes 1540
  10.9 9.1 %collective-permute-start.6 = (bf16[2,4,16,1152]{3,2,1,0:T(8,128)(2,1)S(1)}, bf16[2,4,16,1152]{3,2,1,0:T(8,128)(2,1)S(1)}, u32[]{:S(2)}, u32[]{:S(2)}) collective-permute-start(bf16[2,4,16,1152]{3,2,1,0:T(8,128)(2,1)S(1)} %get-tuple-element.17.refs_0_), channel_id=1, source_target_pairs={{0,2},{1,3},{2,0},{3,1},{4,6},{5,7},{6,4},{7,5},{8,10},{9,11},{10,... | collective-permute-start | bytes 884744 | tf_op jit(solution)/shard_map/ppermute | solution.py:47
  15.4 1.1 %copy-start = (bf16[2,4,16,1152]{3,2,1,0:T(8,128)(2,1)S(1)}, bf16[2,4,16,1152]{3,2,1,0:T(8,128)(2,1)}, u32[]{:S(2)}) copy-start(bf16[2,4,16,1152]{3,2,1,0:T(8,128)(2,1)} %refs_0_.5) | copy-start | bytes 884740
  16.5 3.6 %copy-start.1 = (bf16[2,4,16,1152]{3,2,1,0:T(8,128)(2,1)S(1)}, bf16[2,4,16,1152]{3,2,1,0:T(8,128)(2,1)}, u32[]{:S(2)}) copy-start(bf16[2,4,16,1152]{3,2,1,0:T(8,128)(2,1)} %refs_0_.4) | copy-start | bytes 884740
  16.5 4.7 %collective-permute-start.5 = (bf16[4,4,16,1152]{3,2,1,0:T(8,128)(2,1)S(1)}, bf16[4,4,16,1152]{3,2,1,0:T(8,128)(2,1)S(1)}, u32[]{:S(2)}, u32[]{:S(2)}) collective-permute-start(bf16[4,4,16,1152]{3,2,1,0:T(8,128)(2,1)S(1)} %join.2.refs_0_), channel_id=1, source_target_pairs={{0,1},{1,0},{2,3},{3,2},{4,5},{5,4},{6,7},{7,6},{8,9},{9,8},{10,11... | collective-permute-start | bytes 1769480 | tf_op jit(solution)/shard_map/ppermute | solution.py:47
  20.0 2.3 %collective-permute-start.7 = (bf16[4,4,16,1152]{3,2,1,0:T(8,128)(2,1)S(1)}, bf16[4,4,16,1152]{3,2,1,0:T(8,128)(2,1)S(1)}, u32[]{:S(2)}, u32[]{:S(2)}) collective-permute-start(bf16[4,4,16,1152]{3,2,1,0:T(8,128)(2,1)S(1)} %join.3.refs_0_), channel_id=1, source_target_pairs={{0,1},{1,0},{2,3},{3,2},{4,5},{5,4},{6,7},{7,6},{8,9},{9,8},{10,11... | collective-permute-start | bytes 1769480 | tf_op jit(solution)/shard_map/ppermute | solution.py:47
  20.1 1.1 %copy-start.2 = (bf16[2,4,16,1152]{3,2,1,0:T(8,128)(2,1)S(1)}, bf16[2,4,16,1152]{3,2,1,0:T(8,128)(2,1)}, u32[]{:S(2)}) copy-start(bf16[2,4,16,1152]{3,2,1,0:T(8,128)(2,1)} %q_ref.1) | copy-start | bytes 884740

commit v9 on v8

--- a/solution.py
+++ b/solution.py
@@ -118,7 +118,7 @@
     index = index_ref[0]
     key_rows = []
     for distance in range(blocks // 2 + 1):
-        for parity in (1, 0) if distance else (0,):
+        for parity in (0, 1) if distance else (0,):
             owner = partner_of(index, distance, parity) if distance else index
             first = jnp.where((owner >= 0) & (owner < space), owner * rows, -(2**20))
             row = lax.broadcasted_iota(jnp.int32, (columns, rows * columns), 1) // columns
@@ -295,19 +295,17 @@
     tokens = frames * rows * columns
     first_step = lax.axis_size("tm") // 2
 
-    exchanges = [(d, parity) for d in range(1, reach + 1) for parity in (1, 0)]
+    exchanges = [(d, parity) for d in range(1, reach + 1) for parity in (0, 1)]
     blocks = 1 + len(exchanges)
     bias, own_q, own_k, own_tv = staged(
         [spatial_q, spatial_k, temporal_v], index, key_lists.T, blocks, space
     )
 
-    def gathered(own, received, others):
-        held, step = [own, received], first_step // 2
-        while step:
-            held = [joined(held, others)]
-            held.append(swapped(held[0], "tm", step))
-            step //= 2
-        return held
+    def gathered(held, step):
+        other = swapped(held, "tm", step)
+        if step == 1:
+            return [held, other]
+        return gathered(joined([held, other], []), step // 2)
 
     received_keys = swapped(temporal_k, "tm", first_step)
     received_values = swapped(own_tv, "tm", first_step)
@@ -317,6 +315,7 @@
     ]
 
     keys = blocks * rows * columns
+    joined_keys = joined([temporal_k, received_keys], [])
     spatial_weights, spatial_inverse = call(
         functools.partial(spatial_weigh_kernel, blocks),
         "spatial_weigh",
@@ -324,31 +323,46 @@
         [],
         [bias, own_q, *spatial_keys],
         1,
-        [received_keys],
-    )
-    temporal_keys = gathered(temporal_k, received_keys, [spatial_weights])
-    blocks = len(temporal_keys)
-    keys = sum(k.shape[0] for k in temporal_keys) * columns
-    temporal_weights, temporal_inverse = call(
-        functools.partial(temporal_weigh_kernel, blocks),
-        "temporal_weigh",
-        weigh_shapes(rows, channels, frames * columns, keys),
-        [],
-        [temporal_q, *temporal_keys],
-        1,
-    )
-    temporal_values = gathered(own_tv, received_values, [spatial_weights, *spatial_values[1:]])
+        [joined_keys],
+    )
+    def weigh_all(queries, keyset, before):
+        keysets = gathered(keyset, first_step // 2)
+        keys = sum(k.shape[0] for k in keysets) * columns
+        return call(
+            functools.partial(temporal_weigh_kernel, len(keysets)),
+            "temporal_weigh",
+            weigh_shapes(rows, channels, frames * columns, keys),
+            [],
+            [queries, *keysets],
+            1,
+            [before],
+        )
+
+    def weigh_none(queries, keyset, before):
+        keys = lax.axis_size("tm") * frames * columns
+        shapes = weigh_shapes(rows, channels, frames * columns, keys)
+        return tuple(jnp.zeros(shape.shape, shape.dtype) for shape in shapes)
+
+    temporal_weights, temporal_inverse = lax.cond(
+        lax.axis_index("tm") >= 0,
+        weigh_all,
+        weigh_none,
+        temporal_q,
+        joined_keys,
+        spatial_weights,
+    )
+    temporal_values = gathered(joined([own_tv, received_values], [temporal_weights]), first_step // 2)
     spatial_out = call(
         functools.partial(spatial_blend_kernel, len(spatial_values)),
         "spatial_blend",
         out_shape,
         [],
         [spatial_weights, spatial_inverse, *spatial_values],
-        1,
+        10**10,
         parts=2 * frames,
     )
     temporal_out = call(
-        functools.partial(temporal_blend_kernel, blocks),
+        functools.partial(temporal_blend_kernel, len(temporal_values)),
         "temporal_blend",
         out_shape,
         [],

time: 23.6 us -> 25 us (1.059)
  waiting for transfers between devices: 6.15 us -> 2.4 us
  Pallas kernels: 6.14 us -> 9.11 us
  starting transfers between devices: 9.62 us -> 10.9 us
  local copies, waits for them, and re-layouts: 0.7 us -> 1.64 us
    ppermute x4, waiting for transfers between devices: 6.14 us -> 0.39 us  [exchanged(): return lax.ppermute(value, AXES, pairs)]
    pallas_call x6, Pallas kernels: 4.36 us -> 7.34 us  [call(): pl.pallas_call(kernel, out_shape=out_shape, in_specs=[in_smem] * len(scal...]
    ppermute x4, starting transfers between devices: 4.76 us -> 7.06 us  [exchanged(): return lax.ppermute(value, AXES, pairs)]
    ppermute x4, waiting for transfers between devices: 0.01 us -> 2.01 us  [swapped(): lax.ppermute(value, axis, [(i, i ^ step) for i in range(lax.axis_size(axi...]
    ppermute x4, starting transfers between devices: 4.86 us -> 3.81 us  [swapped(): lax.ppermute(value, axis, [(i, i ^ step) for i in range(lax.axis_size(axi...]
    unnamed x8 -> x6, local copies, waits for them, and re-layouts: 0.7 us -> 1.64 us
  transfers between devices with their start and end apart: 8 -> 8, of which waited for: 3 -> 2; matrix products, arithmetic and copies ran while one was open for 0% -> 0% of each run, Pallas kernels for 21% -> 32%
where the time goes in v9:
time: 25 us; the launch traced here: 24.7 us
  starting transfers between devices  10.9 us (44%)
  Pallas kernels  9.11 us (36%)
  waiting for transfers between devices  2.4 us (10%)
  local copies, waits for them, and re-layouts  1.64 us (7%)
  between operations  0.71 us (3%)
    pallas_call x6, Pallas kernels, call(): pl.pallas_call(kernel, out_shape=out_shape, in_specs=[in_smem] * len(scal...  7.34 us
    ppermute x4, starting transfers between devices, exchanged(): return lax.ppermute(value, AXES, pairs)  7.06 us
    ppermute x4, starting transfers between devices, swapped(): lax.ppermute(value, axis, [(i, i ^ step) for i in range(lax.axis_size(axi...  3.81 us
    ppermute x4, waiting for transfers between devices, swapped(): lax.ppermute(value, axis, [(i, i ^ step) for i in range(lax.axis_size(axi...  2.01 us
    pallas_call x1, Pallas kernels, staged(): pl.pallas_call(functools.partial(stage_kernel, blocks, space), out_shape=...  1.77 us
    unnamed x6, local copies, waits for them, and re-layouts  1.64 us
  transfers between devices with their start and end apart: 8, of which 2 were waited for; matrix products, arithmetic and copies ran while one was open for 0% of the time, Pallas kernels for 32%

profile of v9, /device:TPU:0, one launch (start us, length us, event | category | flops | bytes accessed | tf_op | source)
XLA Modules:
  0.0 24.7 jit_solution(7844003694137007641)
XLA Ops:
  0.6 3.0 %collective-permute-start.3 = (bf16[2,4,16,1152]{3,2,1,0:T(8,128)(2,1)}, bf16[2,4,16,1152]{3,2,1,0:T(8,128)(2,1)S(1)}, u32[]{:S(2)}, u32[]{:S(2)}) collective-permute-start(bf16[2,4,16,1152]{3,2,1,0:T(8,128)(2,1)} %refs_0_.4), channel_id=1, source_target_pairs={{0,2},{1,3},{2,0},{3,1},{4,6},{5,7},{6,4},{7,5},{8,10},{9,11},{10,... | collective-permute-start | bytes 884744 | tf_op jit(solution)/shard_map/ppermute | solution.py:47
  3.6 1.6 %collective-permute-start.1 = (bf16[2,4,16,1152]{3,2,1,0:T(8,128)(2,1)}, bf16[2,4,16,1152]{3,2,1,0:T(8,128)(2,1)S(1)}, u32[]{:S(2)}, u32[]{:S(2)}) collective-permute-start(bf16[2,4,16,1152]{3,2,1,0:T(8,128)(2,1)} %refs_1_.1), channel_id=1, source_target_pairs={{0,4},{1,5},{2,6},{3,7},{4,0},{5,1},{6,2},{7,3},{8,12},{9,13},{10,... | collective-permute-start | bytes 884744 | tf_op jit(solution)/shard_map/ppermute | solution.py:43
  5.2 1.5 %collective-permute-start.2 = (bf16[2,4,16,1152]{3,2,1,0:T(8,128)(2,1)}, bf16[2,4,16,1152]{3,2,1,0:T(8,128)(2,1)S(1)}, u32[]{:S(2)}, u32[]{:S(2)}) collective-permute-start(bf16[2,4,16,1152]{3,2,1,0:T(8,128)(2,1)} %refs_1_.1), channel_id=1, source_target_pairs={{0,16},{1,17},{2,18},{3,19},{4,8},{5,9},{6,10},{7,11},{8,4},{9,5},... | collective-permute-start | bytes 884744 | tf_op jit(solution)/shard_map/ppermute | solution.py:43
  6.7 0.0 copy-start.1
  6.7 0.7 %copy-done.1 = s32[16,8]{0,1:T(8,128)S(1)} copy-done((s32[16,8]{0,1:T(8,128)S(1)}, s32[16,8]{0,1:T(8,128)}, u32[]{:S(2)}) %copy-start.1) | copy-done | bytes 536
  7.4 0.0 copy-start
  7.4 1.8 %stage.1 = (f32[64,192]{1,0:T(8,128)S(1)}, bf16[2,4,16,1152]{3,2,1,0:T(8,128)(2,1)S(1)}, bf16[2,4,16,1152]{3,2,1,0:T(8,128)(2,1)S(1)}, bf16[2,4,16,1152]{3,2,1,0:T(8,128)(2,1)S(1)}) custom-call(s32[1]{0:T(128)} %bitcast.index_ref, s32[8,16]{1,0:T(8,128)S(1)} %bitcast.2, bf16[2,4,16,1152]{3,2,1,0:T(8,128)(2,1)} %refs_0_.3, bf16[2,4,16,1152]{3,2,1,0:T(8,128)(2,1)} %refs_1_.1, ...), custom_call_target="tpu_custom_call" | custom-call | flops 1 | bytes 1 | tf_op jit(solution)/shard_map/stage/pallas_call | solution.py:142
  9.2 0.6 %collective-permute-start.6 = (bf16[2,4,16,1152]{3,2,1,0:T(8,128)(2,1)S(1)}, bf16[2,4,16,1152]{3,2,1,0:T(8,128)(2,1)S(1)}, u32[]{:S(2)}, u32[]{:S(2)}) collective-permute-start(bf16[2,4,16,1152]{3,2,1,0:T(8,128)(2,1)S(1)} %get-tuple-element.26.refs_0_), channel_id=1, source_target_pairs={{0,2},{1,3},{2,0},{3,1},{4,6},{5,7},{6,4},{7,5},{8,10},{9,11},{10,... | collective-permute-start | bytes 884744 | tf_op jit(solution)/shard_map/ppermute | solution.py:47
  9.8 1.6 %collective-permute-start.4 = (bf16[2,4,16,1152]{3,2,1,0:T(8,128)(2,1)}, bf16[2,4,16,1152]{3,2,1,0:T(8,128)(2,1)}, u32[]{:S(2)}, u32[]{:S(2)}) collective-permute-start(bf16[2,4,16,1152]{3,2,1,0:T(8,128)(2,1)} %refs_0_.5), channel_id=1, source_target_pairs={{0,4},{1,5},{2,6},{3,7},{4,0},{5,1},{6,2},{7,3},{8,12},{9,13},{10,... | collective-permute-start | bytes 884744 | tf_op jit(solution)/shard_map/ppermute | solution.py:43
  11.4 0.0 collective-permute-done.3.refs_1_
  11.4 2.3 %collective-permute-start.5 = (bf16[2,4,16,1152]{3,2,1,0:T(8,128)(2,1)}, bf16[2,4,16,1152]{3,2,1,0:T(8,128)(2,1)}, u32[]{:S(2)}, u32[]{:S(2)}) collective-permute-start(bf16[2,4,16,1152]{3,2,1,0:T(8,128)(2,1)} %refs_0_.5), channel_id=1, source_target_pairs={{0,16},{1,17},{2,18},{3,19},{4,8},{5,9},{6,10},{7,11},{8,4},{9,5},... | collective-permute-start | bytes 884744 | tf_op jit(solution)/shard_map/ppermute | solution.py:43
  13.8 0.0 copy-done
  13.8 0.0 collective-permute-done.1.refs_1_
  13.8 0.4 %collective-permute-done.2.refs_2_ = bf16[2,4,16,1152]{3,2,1,0:T(8,128)(2,1)S(1)} collective-permute-done((bf16[2,4,16,1152]{3,2,1,0:T(8,128)(2,1)}, bf16[2,4,16,1152]{3,2,1,0:T(8,128)(2,1)S(1)}, u32[]{:S(2)}, u32[]{:S(2)}) %collective-permute-start.2) | collective-permute-done | bytes 294944 | tf_op jit(solution)/shard_map/ppermute | solution.py:43
  14.2 1.9 %spatial_weigh.1 = (bf16[2,8,128,192]{3,2,1,0:T(8,128)(2,1)}, f32[2,8,64,256]{3,2,1,0:T(8,128)S(1)}) custom-call(f32[64,192]{1,0:T(8,128)S(1)} %get-tuple-element.19.bias_ref, bf16[2,4,16,1152]{3,2,1,0:T(8,128)(2,1)S(1)} %get-tuple-element.20.q_ref, bf16[2,4,16,1152]{3,2,1,0:T(8,128)(2,1)S(1)} %get-tuple-element.21.refs_0_, ...), custom_call_target="tpu_custom_call" | custom-call | flops 1 | bytes 1 | tf_op jit(solution)/shard_map/spatial_weigh/pallas_call | solution.py:241
  16.1 4.0 %conditional.1 = ((bf16[4,8,64,128]{3,2,1,0:T(8,128)(2,1)S(1)}, f32[4,8,32,256]{3,2,1,0:T(8,128)S(1)})) conditional(s32[]{:T(128)} %convert_element_type.3, () %tuple.15, (bf16[4,4,16,1152]{3,2,1,0:T(8,128)(2,1)S(1)}, bf16[2,4,16,1152]{3,2,1,0:T(8,128)(2,1)}, bf16[2,8,128,192]{3,2,1,0:T(8,128)(2,1)}) %tuple.16), branch_computations={%region_0.0_spmd, %region_1.0_spmd} | conditional | flops 1 | bytes 2359345 | solution.py:346
  16.1 0.0 collective-permute-start
  16.1 2.0 %collective-permute-done.refs_1_ = bf16[4,4,16,1152]{3,2,1,0:T(8,128)(2,1)S(1)} collective-permute-done((bf16[4,4,16,1152]{3,2,1,0:T(8,128)(2,1)S(1)}, bf16[4,4,16,1152]{3,2,1,0:T(8,128)(2,1)S(1)}, u32[]{:S(2)}, u32[]{:S(2)}) %collective-permute-start) | collective-permute-done | bytes 589856 | tf_op jit(solution)/shard_map/cond/branch_1_fun/ppermute | solution.py:47
  18.1 2.0 %temporal_weigh.1 = (bf16[4,8,64,128]{3,2,1,0:T(8,128)(2,1)S(1)}, f32[4,8,32,256]{3,2,1,0:T(8,128)S(1)}) custom-call(bf16[2,4,16,1152]{3,2,1,0:T(8,128)(2,1)} %get-tuple-element.28.q_ref, bf16[4,4,16,1152]{3,2,1,0:T(8,128)(2,1)S(1)} %get-tuple-element.7.refs_0_, bf16[4,4,16,1152]{3,2,1,0:T(8,128)(2,1)S(1)} %collective-permute-done.refs_1_, ...), custom_call_target="tpu_custom_call" | custom-call | flops 1 | bytes 1 | tf_op jit(solution)/shard_map/cond/branch_1_fun/temporal_weigh/pallas_call | solution.py:241
  20.1 0.0 copy-start.2
  20.1 0.0 collective-permute-done.6.refs_1_
  20.2 0.2 collective-permute-start.7
  20.4 0.0 collective-permute-done.4.refs_1_
  20.4 0.0 collective-permute-done.5.refs_2_
  20.4 0.9 %copy-done.2 = bf16[2,8,128,192]{3,2,1,0:T(8,128)(2,1)S(1)} copy-done((bf16[2,8,128,192]{3,2,1,0:T(8,128)(2,1)S(1)}, bf16[2,8,128,192]{3,2,1,0:T(8,128)(2,1)}, u32[]{:S(2)}) %copy-start.2) | copy-done | bytes 786456
  21.4 2.2 %spatial_blend.1 = bf16[2,4,16,1152]{3,2,1,0:T(8,128)(2,1)} custom-call(bf16[2,8,128,192]{3,2,1,0:T(8,128)(2,1)S(1)} %copy-done.2, f32[2,8,64,256]{3,2,1,0:T(8,128)S(1)} %get-tuple-element.23.inverse_ref, bf16[2,4,16,1152]{3,2,1,0:T(8,128)(2,1)} %refs_0_.5, bf16[2,4,16,1152]{3,2,1,0:T(8,128)(2,1)} %collective-permute-done.4.refs_1_, ...), custom_call_target="tpu_custom_call" | custom-call | flops 10000000000 | bytes 1 | tf_op jit(solution)/shard_map/spatial_blend/pallas_call | solution.py:241
  23.6 0.0 collective-permute-done.7.refs_1_
  23.6 1.1 %temporal_blend.1 = bf16[2,4,16,1152]{3,2,1,0:T(8,128)(2,1)} custom-call(bf16[4,8,64,128]{3,2,1,0:T(8,128)(2,1)S(1)} %get-tuple-element.24.refs_2_.weights_ref, f32[4,8,32,256]{3,2,1,0:T(8,128)S(1)} %get-tuple-element.25.inverse_ref, bf16[4,4,16,1152]{3,2,1,0:T(8,128)(2,1)S(1)} %join.3.refs_0_, bf16[4,4,16,1152]{3,2,1,0:T(8,128)(2,1)S(1)} %collective-permute-done.7.refs_1_), custom_call_target="tpu_custom_call" | custom-call | flops 1 | bytes 1 | tf_op jit(solution)/shard_map/temporal_blend/pallas_call | solution.py:241
  (2 shorter events, 0.1 us)
Async XLA Ops:
  0.6 10.8 %collective-permute-start.3 = (bf16[2,4,16,1152]{3,2,1,0:T(8,128)(2,1)}, bf16[2,4,16,1152]{3,2,1,0:T(8,128)(2,1)S(1)}, u32[]{:S(2)}, u32[]{:S(2)}) collective-permute-start(bf16[2,4,16,1152]{3,2,1,0:T(8,128)(2,1)} %refs_0_.4), channel_id=1, source_target_pairs={{0,2},{1,3},{2,0},{3,1},{4,6},{5,7},{6,4},{7,5},{8,10},{9,11},{10,... | collective-permute-start | bytes 884744 | tf_op jit(solution)/shard_map/ppermute | solution.py:47
  3.6 10.2 %collective-permute-start.1 = (bf16[2,4,16,1152]{3,2,1,0:T(8,128)(2,1)}, bf16[2,4,16,1152]{3,2,1,0:T(8,128)(2,1)S(1)}, u32[]{:S(2)}, u32[]{:S(2)}) collective-permute-start(bf16[2,4,16,1152]{3,2,1,0:T(8,128)(2,1)} %refs_1_.1), channel_id=1, source_target_pairs={{0,4},{1,5},{2,6},{3,7},{4,0},{5,1},{6,2},{7,3},{8,12},{9,13},{10,... | collective-permute-start | bytes 884744 | tf_op jit(solution)/shard_map/ppermute | solution.py:43
  5.2 9.0 %collective-permute-start.2 = (bf16[2,4,16,1152]{3,2,1,0:T(8,128)(2,1)}, bf16[2,4,16,1152]{3,2,1,0:T(8,128)(2,1)S(1)}, u32[]{:S(2)}, u32[]{:S(2)}) collective-permute-start(bf16[2,4,16,1152]{3,2,1,0:T(8,128)(2,1)} %refs_1_.1), channel_id=1, source_target_pairs={{0,16},{1,17},{2,18},{3,19},{4,8},{5,9},{6,10},{7,11},{8,4},{9,5},... | collective-permute-start | bytes 884744 | tf_op jit(solution)/shard_map/ppermute | solution.py:43
  6.7 0.7 %copy-start.1 = (s32[16,8]{0,1:T(8,128)S(1)}, s32[16,8]{0,1:T(8,128)}, u32[]{:S(2)}) copy-start(s32[16,8]{0,1:T(8,128)} %param.15) | copy-start | bytes 1540
  7.4 6.4 %copy-start = (bf16[2,4,16,1152]{3,2,1,0:T(8,128)(2,1)S(1)}, bf16[2,4,16,1152]{3,2,1,0:T(8,128)(2,1)}, u32[]{:S(2)}) copy-start(bf16[2,4,16,1152]{3,2,1,0:T(8,128)(2,1)} %refs_0_.4) | copy-start | bytes 884740
  9.2 11.0 %collective-permute-start.6 = (bf16[2,4,16,1152]{3,2,1,0:T(8,128)(2,1)S(1)}, bf16[2,4,16,1152]{3,2,1,0:T(8,128)(2,1)S(1)}, u32[]{:S(2)}, u32[]{:S(2)}) collective-permute-start(bf16[2,4,16,1152]{3,2,1,0:T(8,128)(2,1)S(1)} %get-tuple-element.26.refs_0_), channel_id=1, source_target_pairs={{0,2},{1,3},{2,0},{3,1},{4,6},{5,7},{6,4},{7,5},{8,10},{9,11},{10,... | collective-permute-start | bytes 884744 | tf_op jit(solution)/shard_map/ppermute | solution.py:47
  9.8 10.6 %collective-permute-start.4 = (bf16[2,4,16,1152]{3,2,1,0:T(8,128)(2,1)}, bf16[2,4,16,1152]{3,2,1,0:T(8,128)(2,1)}, u32[]{:S(2)}, u32[]{:S(2)}) collective-permute-start(bf16[2,4,16,1152]{3,2,1,0:T(8,128)(2,1)} %refs_0_.5), channel_id=1, source_target_pairs={{0,4},{1,5},{2,6},{3,7},{4,0},{5,1},{6,2},{7,3},{8,12},{9,13},{10,... | collective-permute-start | bytes 884744 | tf_op jit(solution)/shard_map/ppermute | solution.py:43
  11.4 9.0 %collective-permute-start.5 = (bf16[2,4,16,1152]{3,2,1,0:T(8,128)(2,1)}, bf16[2,4,16,1152]{3,2,1,0:T(8,128)(2,1)}, u32[]{:S(2)}, u32[]{:S(2)}) collective-permute-start(bf16[2,4,16,1152]{3,2,1,0:T(8,128)(2,1)} %refs_0_.5), channel_id=1, source_target_pairs={{0,16},{1,17},{2,18},{3,19},{4,8},{5,9},{6,10},{7,11},{8,4},{9,5},... | collective-permute-start | bytes 884744 | tf_op jit(solution)/shard_map/ppermute | solution.py:43
  16.1 2.0 %collective-permute-start = (bf16[4,4,16,1152]{3,2,1,0:T(8,128)(2,1)S(1)}, bf16[4,4,16,1152]{3,2,1,0:T(8,128)(2,1)S(1)}, u32[]{:S(2)}, u32[]{:S(2)}) collective-permute-start(bf16[4,4,16,1152]{3,2,1,0:T(8,128)(2,1)S(1)} %get-tuple-element.7.refs_0_), channel_id=1, source_target_pairs={{0,1},{1,0},{2,3},{3,2},{4,5},{5,4},{6,7},{7,6},{8,9},{9,8},{10,11... | collective-permute-start | bytes 1769480 | tf_op jit(solution)/shard_map/cond/branch_1_fun/ppermute | solution.py:47
  20.1 1.2 %copy-start.2 = (bf16[2,8,128,192]{3,2,1,0:T(8,128)(2,1)S(1)}, bf16[2,8,128,192]{3,2,1,0:T(8,128)(2,1)}, u32[]{:S(2)}) copy-start(bf16[2,8,128,192]{3,2,1,0:T(8,128)(2,1)} %get-tuple-element.22.weights_ref) | copy-start | bytes 2359300
  20.2 3.4 %collective-permute-start.7 = (bf16[4,4,16,1152]{3,2,1,0:T(8,128)(2,1)S(1)}, bf16[4,4,16,1152]{3,2,1,0:T(8,128)(2,1)S(1)}, u32[]{:S(2)}, u32[]{:S(2)}) collective-permute-start(bf16[4,4,16,1152]{3,2,1,0:T(8,128)(2,1)S(1)} %join.3.refs_0_), channel_id=1, source_target_pairs={{0,1},{1,0},{2,3},{3,2},{4,5},{5,4},{6,7},{7,6},{8,9},{9,8},{10,11... | collective-permute-start | bytes 1769480 | tf_op jit(solution)/shard_map/ppermute | solution.py:47

commit v10 on v9

--- a/solution.py
+++ b/solution.py
@@ -146,15 +146,16 @@
         + [pl.BlockSpec(memory_space=pl.ANY)] * len(arrays),
         out_specs=(in_vmem,) * (1 + len(arrays)),
         scratch_shapes=[pltpu.SemaphoreType.DMA((len(arrays),))],
-        compiler_params=pltpu.CompilerParams(vmem_limit_bytes=53 * 1024 * 1024),
+        compiler_params=pltpu.CompilerParams(vmem_limit_bytes=53568 * 1024),
         cost_estimate=pl.CostEstimate(flops=1, bytes_accessed=1, transcendentals=0),
         name="stage",
     )(index, lists, *arrays)
 
 
 def spatial_weigh_kernel(blocks, bias_ref, q_ref, *refs):
-    k_refs, weights_ref, inverse_ref = refs[:blocks], *refs[-2:]
+    k_refs, weights_ref, inverse_ref, token_ref = refs[:blocks], *refs[-3:]
     frames, rows, columns, channels = q_ref.shape
+    token_ref[...] = jnp.zeros(token_ref.shape, token_ref.dtype)
     bias = bias_ref[...]
     bias = jnp.concatenate([bias, bias], axis=0)
     for frame in range(frames):
@@ -297,8 +298,12 @@
 
     exchanges = [(d, parity) for d in range(1, reach + 1) for parity in (0, 1)]
     blocks = 1 + len(exchanges)
-    bias, own_q, own_k, own_tv = staged(
-        [spatial_q, spatial_k, temporal_v], index, key_lists.T, blocks, space
+    bias, own_sq, own_sk, own_sv, own_tq, own_tk, own_tv = staged(
+        [spatial_q, spatial_k, spatial_v, temporal_q, temporal_k, temporal_v],
+        index,
+        key_lists.T,
+        blocks,
+        space,
     )
 
     def gathered(held, step):
@@ -309,19 +314,18 @@
 
     received_keys = swapped(temporal_k, "tm", first_step)
     received_values = swapped(own_tv, "tm", first_step)
-    spatial_keys = [own_k] + [exchanged(spatial_k, *which) for which in exchanges]
-    spatial_values = [spatial_v] + [
-        exchanged(spatial_v, *which) for which in exchanges
-    ]
+    spatial_keys = [own_sk] + [exchanged(spatial_k, *which) for which in exchanges]
+    spatial_values = [own_sv] + [exchanged(own_sv, *which) for which in exchanges]
 
     keys = blocks * rows * columns
-    joined_keys = joined([temporal_k, received_keys], [])
-    spatial_weights, spatial_inverse = call(
+    joined_keys = joined([own_tk, received_keys], [])
+    spatial_weights, spatial_inverse, token = call(
         functools.partial(spatial_weigh_kernel, blocks),
         "spatial_weigh",
-        weigh_shapes(frames, channels, rows * columns, keys),
+        weigh_shapes(frames, channels, rows * columns, keys)
+        + (jax.ShapeDtypeStruct((8, LANES), jnp.float32),),
         [],
-        [bias, own_q, *spatial_keys],
+        [bias, own_sq, *spatial_keys],
         1,
         [joined_keys],
     )
@@ -347,9 +351,9 @@
         lax.axis_index("tm") >= 0,
         weigh_all,
         weigh_none,
-        temporal_q,
+        own_tq,
         joined_keys,
-        spatial_weights,
+        token,
     )
     temporal_values = gathered(joined([own_tv, received_values], [temporal_weights]), first_step // 2)
     spatial_out = call(

time: 25 us -> 26.4 us (1.056)
  Pallas kernels: 9.11 us -> 10.8 us
  local copies, waits for them, and re-layouts: 1.64 us -> 2.63 us
  starting transfers between devices: 10.9 us -> 10.1 us
  waiting for transfers between devices: 2.4 us -> 2.02 us
    pallas_call x1, Pallas kernels: 1.77 us -> 2.8 us  [staged(): pl.pallas_call(functools.partial(stage_kernel, blocks, space), out_shape=...]
    unnamed x6, local copies, waits for them, and re-layouts: 1.64 us -> 2.63 us
    ppermute x4, starting transfers between devices: 7.06 us -> 6.25 us  [exchanged(): return lax.ppermute(value, AXES, pairs)]
    pallas_call x6, Pallas kernels: 7.34 us -> 7.96 us  [call(): pl.pallas_call(kernel, out_shape=out_shape, in_specs=[in_smem] * len(scal...]
    ppermute x4, waiting for transfers between devices: 0.39 us -> 0.01 us  [exchanged(): return lax.ppermute(value, AXES, pairs)]
  transfers between devices with their start and end apart: 8 -> 8, of which waited for: 2 -> 1; matrix products, arithmetic and copies ran while one was open for 0% -> 0% of each run, Pallas kernels for 32% -> 32%
where the time goes in v10:
time: 26.4 us; the launch traced here: 26.2 us
  Pallas kernels  10.8 us (41%)
  starting transfers between devices  10.1 us (38%)
  local copies, waits for them, and re-layouts  2.63 us (10%)
  waiting for transfers between devices  2.02 us (8%)
  between operations  0.7 us (3%)
    pallas_call x6, Pallas kernels, call(): pl.pallas_call(kernel, out_shape=out_shape, in_specs=[in_smem] * len(scal...  7.96 us
    ppermute x4, starting transfers between devices, exchanged(): return lax.ppermute(value, AXES, pairs)  6.25 us
    ppermute x4, starting transfers between devices, swapped(): lax.ppermute(value, axis, [(i, i ^ step) for i in range(lax.axis_size(axi...  3.81 us
    pallas_call x1, Pallas kernels, staged(): pl.pallas_call(functools.partial(stage_kernel, blocks, space), out_shape=...  2.8 us
    unnamed x6, local copies, waits for them, and re-layouts  2.63 us
    ppermute x4, waiting for transfers between devices, swapped(): lax.ppermute(value, axis, [(i, i ^ step) for i in range(lax.axis_size(axi...  2.01 us
  transfers between devices with their start and end apart: 8, of which 1 were waited for; matrix products, arithmetic and copies ran while one was open for 0% of the time, Pallas kernels for 32%

profile of v10, /device:TPU:0, one launch (start us, length us, event | category | flops | bytes accessed | tf_op | source)
XLA Modules:
  0.0 26.2 jit_solution(14140986310626932544)
XLA Ops:
  0.6 3.0 %collective-permute-start.3 = (bf16[2,4,16,1152]{3,2,1,0:T(8,128)(2,1)}, bf16[2,4,16,1152]{3,2,1,0:T(8,128)(2,1)S(1)}, u32[]{:S(2)}, u32[]{:S(2)}) collective-permute-start(bf16[2,4,16,1152]{3,2,1,0:T(8,128)(2,1)} %refs_4_.1), channel_id=1, source_target_pairs={{0,2},{1,3},{2,0},{3,1},{4,6},{5,7},{6,4},{7,5},{8,10},{9,11},{10,... | collective-permute-start | bytes 884744 | tf_op jit(solution)/shard_map/ppermute | solution.py:47
  3.6 1.6 %collective-permute-start.1 = (bf16[2,4,16,1152]{3,2,1,0:T(8,128)(2,1)}, bf16[2,4,16,1152]{3,2,1,0:T(8,128)(2,1)S(1)}, u32[]{:S(2)}, u32[]{:S(2)}) collective-permute-start(bf16[2,4,16,1152]{3,2,1,0:T(8,128)(2,1)} %refs_1_.1), channel_id=1, source_target_pairs={{0,4},{1,5},{2,6},{3,7},{4,0},{5,1},{6,2},{7,3},{8,12},{9,13},{10,... | collective-permute-start | bytes 884744 | tf_op jit(solution)/shard_map/ppermute | solution.py:43
  5.2 1.5 %collective-permute-start.2 = (bf16[2,4,16,1152]{3,2,1,0:T(8,128)(2,1)}, bf16[2,4,16,1152]{3,2,1,0:T(8,128)(2,1)S(1)}, u32[]{:S(2)}, u32[]{:S(2)}) collective-permute-start(bf16[2,4,16,1152]{3,2,1,0:T(8,128)(2,1)} %refs_1_.1), channel_id=1, source_target_pairs={{0,16},{1,17},{2,18},{3,19},{4,8},{5,9},{6,10},{7,11},{8,4},{9,5},... | collective-permute-start | bytes 884744 | tf_op jit(solution)/shard_map/ppermute | solution.py:43
  6.7 0.0 copy-start
  6.7 0.7 %copy-done = s32[16,8]{0,1:T(8,128)S(1)} copy-done((s32[16,8]{0,1:T(8,128)S(1)}, s32[16,8]{0,1:T(8,128)}, u32[]{:S(2)}) %copy-start) | copy-done | bytes 536
  7.4 2.8 %stage.1 = (f32[64,192]{1,0:T(8,128)S(1)}, bf16[2,4,16,1152]{3,2,1,0:T(8,128)(2,1)S(1)}, bf16[2,4,16,1152]{3,2,1,0:T(8,128)(2,1)S(1)}, bf16[2,4,16,1152]{3,2,1,0...) custom-call(s32[1]{0:T(128)} %bitcast.index_ref, ...), custom_call_target="tpu_custom_call" | custom-call | flops 1 | bytes 1 | tf_op jit(solution)/shard_map/stage/pallas_call | solution.py:142
  10.2 0.6 %collective-permute-start.6 = (bf16[2,4,16,1152]{3,2,1,0:T(8,128)(2,1)S(1)}, bf16[2,4,16,1152]{3,2,1,0:T(8,128)(2,1)S(1)}, u32[]{:S(2)}, u32[]{:S(2)}) collective-permute-start(bf16[2,4,16,1152]{3,2,1,0:T(8,128)(2,1)S(1)} %get-tuple-element.34.refs_0_), channel_id=1, source_target_pairs={{0,2},{1,3},{2,0},{3,1},{4,6},{5,7},{6,4},{7,5},{8,10},{9,11},{10,... | collective-permute-start | bytes 884744 | tf_op jit(solution)/shard_map/ppermute | solution.py:47
  10.8 1.6 %collective-permute-start.4 = (bf16[2,4,16,1152]{3,2,1,0:T(8,128)(2,1)}, bf16[2,4,16,1152]{3,2,1,0:T(8,128)(2,1)}, u32[]{:S(2)}, u32[]{:S(2)}) collective-permute-start(bf16[2,4,16,1152]{3,2,1,0:T(8,128)(2,1)} %get-tuple-element.29.refs_0_), channel_id=1, source_target_pairs={{0,4},{1,5},{2,6},{3,7},{4,0},{5,1},{6,2},{7,3},{8,12},{9,13},{10,... | collective-permute-start | bytes 884744 | tf_op jit(solution)/shard_map/ppermute | solution.py:43
  12.5 0.0 collective-permute-done.3.refs_1_
  12.5 1.5 %collective-permute-start.5 = (bf16[2,4,16,1152]{3,2,1,0:T(8,128)(2,1)}, bf16[2,4,16,1152]{3,2,1,0:T(8,128)(2,1)}, u32[]{:S(2)}, u32[]{:S(2)}) collective-permute-start(bf16[2,4,16,1152]{3,2,1,0:T(8,128)(2,1)} %get-tuple-element.29.refs_0_), channel_id=1, source_target_pairs={{0,16},{1,17},{2,18},{3,19},{4,8},{5,9},{6,10},{7,11},{8,4},{9,5},... | collective-permute-start | bytes 884744 | tf_op jit(solution)/shard_map/ppermute | solution.py:43
  14.0 0.0 collective-permute-done.1.refs_1_
  14.0 0.0 collective-permute-done.2.refs_2_
  14.1 1.0 %spatial_weigh.1 = (bf16[2,8,128,192]{3,2,1,0:T(8,128)(2,1)S(1)}, f32[2,8,64,256]{3,2,1,0:T(8,128)S(1)}, f32[8,128]{1,0:T(8,128)S(1)}) custom-call(f32[64,192]{1,0:T(8,128)S(1)} %get-tuple-element.23.bias_ref, bf16[2,4,16,1152]{3,2,1,0:T(8,128)(2,1)S(1)} %get-tuple-element.24.q_ref, bf16[2,4,16,1152]{3,2,1,0:T(8,128)(2,1)S(1)} %get-tuple-element.25.refs_0_, ...), custom_call_target="tpu_custom_call" | custom-call | flops 1 | bytes 1 | tf_op jit(solution)/shard_map/spatial_weigh/pallas_call | solution.py:242
  15.1 0.0 copy-start.1
  15.1 1.0 %copy-done.1 = f32[2,8,64,256]{3,2,1,0:T(8,128)} copy-done((f32[2,8,64,256]{3,2,1,0:T(8,128)}, f32[2,8,64,256]{3,2,1,0:T(8,128)S(1)}, u32[]{:S(2)}) %copy-start.1) | copy-done | bytes 1048600
  16.1 4.1 %conditional.1 = ((bf16[4,8,64,128]{3,2,1,0:T(8,128)(2,1)}, f32[4,8,32,256]{3,2,1,0:T(8,128)})) conditional(s32[]{:T(128)} %convert_element_type.3, () %tuple.15, (bf16[4,4,16,1152]{3,2,1,0:T(8,128)(2,1)S(1)}, bf16[2,4,16,1152]{3,2,1,0:T(8,128)(2,1)S(1)}, f32[8,128]{1,0:T(8,128)S(1)}) %tuple.16), branch_computations={%region_0.0_spmd, %region_1.0_spmd} | conditional | flops 1 | bytes 2359345 | solution.py:350
  16.1 0.0 collective-permute-start
  16.1 2.0 %collective-permute-done.refs_1_ = bf16[4,4,16,1152]{3,2,1,0:T(8,128)(2,1)S(1)} collective-permute-done((bf16[4,4,16,1152]{3,2,1,0:T(8,128)(2,1)S(1)}, bf16[4,4,16,1152]{3,2,1,0:T(8,128)(2,1)S(1)}, u32[]{:S(2)}, u32[]{:S(2)}) %collective-permute-start) | collective-permute-done | bytes 589856 | tf_op jit(solution)/shard_map/cond/branch_1_fun/ppermute | solution.py:47
  18.1 2.1 %temporal_weigh.1 = (bf16[4,8,64,128]{3,2,1,0:T(8,128)(2,1)}, f32[4,8,32,256]{3,2,1,0:T(8,128)}) custom-call(bf16[2,4,16,1152]{3,2,1,0:T(8,128)(2,1)S(1)} %get-tuple-element.6.q_ref, bf16[4,4,16,1152]{3,2,1,0:T(8,128)(2,1)S(1)} %get-tuple-element.7.refs_0_, bf16[4,4,16,1152]{3,2,1,0:T(8,128)(2,1)S(1)} %collective-permute-done.refs_1_, ...), custom_call_target="tpu_custom_call" | custom-call | flops 1 | bytes 1 | tf_op jit(solution)/shard_map/cond/branch_1_fun/temporal_weigh/pallas_call | solution.py:242
  20.2 0.0 copy-start.2
  20.2 0.0 collective-permute-done.6.refs_1_
  20.2 0.2 collective-permute-start.7
  20.4 0.0 collective-permute-done.4.refs_1_
  20.4 0.0 collective-permute-done.5.refs_2_
  20.4 1.0 %copy-done.2 = f32[2,8,64,256]{3,2,1,0:T(8,128)S(1)} copy-done((f32[2,8,64,256]{3,2,1,0:T(8,128)S(1)}, f32[2,8,64,256]{3,2,1,0:T(8,128)}, u32[]{:S(2)}) %copy-start.2) | copy-done | bytes 1048600
  21.4 2.2 %spatial_blend.1 = bf16[2,4,16,1152]{3,2,1,0:T(8,128)(2,1)} custom-call(bf16[2,8,128,192]{3,2,1,0:T(8,128)(2,1)S(1)} %get-tuple-element.27.weights_ref, f32[2,8,64,256]{3,2,1,0:T(8,128)S(1)} %copy-done.2, bf16[2,4,16,1152]{3,2,1,0:T(8,128)(2,1)} %get-tuple-element.29.refs_0_, bf16[2,4,16,1152]{3,2,1,0:T(8,128)(2,1)} %collective-permute-done.4.refs_1_, ...), custom_call_target="tpu_custom_call" | custom-call | flops 10000000000 | bytes 1 | tf_op jit(solution)/shard_map/spatial_blend/pallas_call | solution.py:242
  23.7 0.0 collective-permute-done.7.refs_1_
  23.7 2.5 %temporal_blend.1 = bf16[2,4,16,1152]{3,2,1,0:T(8,128)(2,1)} custom-call(bf16[4,8,64,128]{3,2,1,0:T(8,128)(2,1)} %get-tuple-element.32.refs_2_.weights_ref, f32[4,8,32,256]{3,2,1,0:T(8,128)} %get-tuple-element.33.inverse_ref, bf16[4,4,16,1152]{3,2,1,0:T(8,128)(2,1)S(1)} %join.3.refs_0_, bf16[4,4,16,1152]{3,2,1,0:T(8,128)(2,1)S(1)} %collective-permute-done.7.refs_1_), custom_call_target="tpu_custom_call" | custom-call | flops 1 | bytes 1 | tf_op jit(solution)/shard_map/temporal_blend/pallas_call | solution.py:242
  (2 shorter events, 0.1 us)
Async XLA Ops:
  0.6 11.8 %collective-permute-start.3 = (bf16[2,4,16,1152]{3,2,1,0:T(8,128)(2,1)}, bf16[2,4,16,1152]{3,2,1,0:T(8,128)(2,1)S(1)}, u32[]{:S(2)}, u32[]{:S(2)}) collective-permute-start(bf16[2,4,16,1152]{3,2,1,0:T(8,128)(2,1)} %refs_4_.1), channel_id=1, source_target_pairs={{0,2},{1,3},{2,0},{3,1},{4,6},{5,7},{6,4},{7,5},{8,10},{9,11},{10,... | collective-permute-start | bytes 884744 | tf_op jit(solution)/shard_map/ppermute | solution.py:47
  3.6 10.4 %collective-permute-start.1 = (bf16[2,4,16,1152]{3,2,1,0:T(8,128)(2,1)}, bf16[2,4,16,1152]{3,2,1,0:T(8,128)(2,1)S(1)}, u32[]{:S(2)}, u32[]{:S(2)}) collective-permute-start(bf16[2,4,16,1152]{3,2,1,0:T(8,128)(2,1)} %refs_1_.1), channel_id=1, source_target_pairs={{0,4},{1,5},{2,6},{3,7},{4,0},{5,1},{6,2},{7,3},{8,12},{9,13},{10,... | collective-permute-start | bytes 884744 | tf_op jit(solution)/shard_map/ppermute | solution.py:43
  5.2 8.8 %collective-permute-start.2 = (bf16[2,4,16,1152]{3,2,1,0:T(8,128)(2,1)}, bf16[2,4,16,1152]{3,2,1,0:T(8,128)(2,1)S(1)}, u32[]{:S(2)}, u32[]{:S(2)}) collective-permute-start(bf16[2,4,16,1152]{3,2,1,0:T(8,128)(2,1)} %refs_1_.1), channel_id=1, source_target_pairs={{0,16},{1,17},{2,18},{3,19},{4,8},{5,9},{6,10},{7,11},{8,4},{9,5},... | collective-permute-start | bytes 884744 | tf_op jit(solution)/shard_map/ppermute | solution.py:43
  6.7 0.7 %copy-start = (s32[16,8]{0,1:T(8,128)S(1)}, s32[16,8]{0,1:T(8,128)}, u32[]{:S(2)}) copy-start(s32[16,8]{0,1:T(8,128)} %param.15) | copy-start | bytes 1540
  10.2 10.0 %collective-permute-start.6 = (bf16[2,4,16,1152]{3,2,1,0:T(8,128)(2,1)S(1)}, bf16[2,4,16,1152]{3,2,1,0:T(8,128)(2,1)S(1)}, u32[]{:S(2)}, u32[]{:S(2)}) collective-permute-start(bf16[2,4,16,1152]{3,2,1,0:T(8,128)(2,1)S(1)} %get-tuple-element.34.refs_0_), channel_id=1, source_target_pairs={{0,2},{1,3},{2,0},{3,1},{4,6},{5,7},{6,4},{7,5},{8,10},{9,11},{10,... | collective-permute-start | bytes 884744 | tf_op jit(solution)/shard_map/ppermute | solution.py:47
  10.8 9.6 %collective-permute-start.4 = (bf16[2,4,16,1152]{3,2,1,0:T(8,128)(2,1)}, bf16[2,4,16,1152]{3,2,1,0:T(8,128)(2,1)}, u32[]{:S(2)}, u32[]{:S(2)}) collective-permute-start(bf16[2,4,16,1152]{3,2,1,0:T(8,128)(2,1)} %get-tuple-element.29.refs_0_), channel_id=1, source_target_pairs={{0,4},{1,5},{2,6},{3,7},{4,0},{5,1},{6,2},{7,3},{8,12},{9,13},{10,... | collective-permute-start | bytes 884744 | tf_op jit(solution)/shard_map/ppermute | solution.py:43
  12.5 8.0 %collective-permute-start.5 = (bf16[2,4,16,1152]{3,2,1,0:T(8,128)(2,1)}, bf16[2,4,16,1152]{3,2,1,0:T(8,128)(2,1)}, u32[]{:S(2)}, u32[]{:S(2)}) collective-permute-start(bf16[2,4,16,1152]{3,2,1,0:T(8,128)(2,1)} %get-tuple-element.29.refs_0_), channel_id=1, source_target_pairs={{0,16},{1,17},{2,18},{3,19},{4,8},{5,9},{6,10},{7,11},{8,4},{9,5},... | collective-permute-start | bytes 884744 | tf_op jit(solution)/shard_map/ppermute | solution.py:43
  15.1 1.0 %copy-start.1 = (f32[2,8,64,256]{3,2,1,0:T(8,128)}, f32[2,8,64,256]{3,2,1,0:T(8,128)S(1)}, u32[]{:S(2)}) copy-start(f32[2,8,64,256]{3,2,1,0:T(8,128)S(1)} %get-tuple-element.28.inverse_ref) | copy-start | bytes 3145732
  16.1 2.0 %collective-permute-start = (bf16[4,4,16,1152]{3,2,1,0:T(8,128)(2,1)S(1)}, bf16[4,4,16,1152]{3,2,1,0:T(8,128)(2,1)S(1)}, u32[]{:S(2)}, u32[]{:S(2)}) collective-permute-start(bf16[4,4,16,1152]{3,2,1,0:T(8,128)(2,1)S(1)} %get-tuple-element.7.refs_0_), channel_id=1, source_target_pairs={{0,1},{1,0},{2,3},{3,2},{4,5},{5,4},{6,7},{7,6},{8,9},{9,8},{10,11... | collective-permute-start | bytes 1769480 | tf_op jit(solution)/shard_map/cond/branch_1_fun/ppermute | solution.py:47
  20.2 1.2 %copy-start.2 = (f32[2,8,64,256]{3,2,1,0:T(8,128)S(1)}, f32[2,8,64,256]{3,2,1,0:T(8,128)}, u32[]{:S(2)}) copy-start(f32[2,8,64,256]{3,2,1,0:T(8,128)} %copy-done.1) | copy-start | bytes 3145732
  20.2 3.4 %collective-permute-start.7 = (bf16[4,4,16,1152]{3,2,1,0:T(8,128)(2,1)S(1)}, bf16[4,4,16,1152]{3,2,1,0:T(8,128)(2,1)S(1)}, u32[]{:S(2)}, u32[]{:S(2)}) collective-permute-start(bf16[4,4,16,1152]{3,2,1,0:T(8,128)(2,1)S(1)} %join.3.refs_0_), channel_id=1, source_target_pairs={{0,1},{1,0},{2,3},{3,2},{4,5},{5,4},{6,7},{7,6},{8,9},{9,8},{10,11... | collective-permute-start | bytes 1769480 | tf_op jit(solution)/shard_map/ppermute | solution.py:47

commit v11 on v8

--- a/solution.py
+++ b/solution.py
@@ -9,7 +9,6 @@
 from jax.sharding import PartitionSpec as P
 
 HEAD_DIM = 72
-PAIR = 2 * HEAD_DIM
 LANES = 128
 WINDOW = 2 * LANES
 SCALE = HEAD_DIM ** (-0.5) * math.log2(math.e)
@@ -47,62 +46,84 @@
     return lax.ppermute(value, axis, [(i, i ^ step) for i in range(lax.axis_size(axis))])
 
 
-def head_masks(pair, rows):
-    lane = lax.broadcasted_iota(jnp.int32, (rows, WINDOW), 1)
-    first = (PAIR - LANES) * pair
-    return [
-        (lane >= first + head * HEAD_DIM) & (lane < first + (head + 1) * HEAD_DIM)
-        for head in range(2)
-    ]
-
-
-def window_of(pair):
-    return slice(pair * LANES, pair * LANES + WINDOW)
-
-
-def weigh_pair(pair, queries, keyset, bias):
-    rows = queries.shape[0]
-    masks = head_masks(pair, rows)
-    stacked = jnp.concatenate(
-        [queries * mask.astype(jnp.bfloat16) for mask in masks], axis=0
-    )
-    scores = lax.dot_general(
-        stacked, keyset, (((1,), (1,)), ((), ())), preferred_element_type=jnp.float32
-    )
-    scores = scores * SCALE + bias
-    highest = jnp.max(scores, axis=-1, keepdims=True)
-    weights = jnp.exp2(scores - highest)
-    inverse = 1.0 / jnp.sum(weights, axis=-1, keepdims=True)
-    inverse = jnp.where(masks[0], inverse[:rows], jnp.where(masks[1], inverse[rows:], 0.0))
-    return weights.astype(jnp.bfloat16), inverse
-
-
-def blend_pairs(pairs, read_weights, read_inverse, read_values, write):
-    carry = None
-    for pair in range(pairs):
-        inverse = read_inverse(pair)
-        rows = inverse.shape[0]
+def windows_of(channels):
+    windows = []
+    for first in range(0, channels, WINDOW):
+        last = min(first + WINDOW, channels)
+        windows.append((slice(first, last), range(first // HEAD_DIM, (last - 1) // HEAD_DIM + 1)))
+    return windows
+
+
+def by_head(parts, heads, first, rows):
+    lane = lax.broadcasted_iota(jnp.int32, (rows, LANES), 1) + first
+    chosen = parts[0]
+    for head, part in zip(heads[1:], parts[1:]):
+        chosen = jnp.where(lane >= head * HEAD_DIM, part, chosen)
+    return chosen
+
+
+def tile_heads(first):
+    return range(first // HEAD_DIM, (first + LANES - 1) // HEAD_DIM + 1)
+
+
+def weigh(channels, read_queries, read_keys, bias, write_weights, write_inverse):
+    scores, inverses = {}, {}
+    rows = bias.shape[0]
+    for lanes, heads in windows_of(channels):
+        queries = read_queries(lanes)
+        lane = lax.broadcasted_iota(jnp.int32, queries.shape, 1) + lanes.start
+        stacked = []
+        for head in heads:
+            mask = (lane >= head * HEAD_DIM) & (lane < (head + 1) * HEAD_DIM)
+            stacked.append(queries * mask.astype(jnp.bfloat16))
+        both = lax.dot_general(
+            jnp.concatenate(stacked, axis=0),
+            read_keys(lanes),
+            (((1,), (1,)), ((), ())),
+            preferred_element_type=jnp.float32,
+        )
+        for place, head in enumerate(heads):
+            part = both[place * rows : (place + 1) * rows]
+            scores[head] = scores[head] + part if head in scores else part
+            if (head + 1) * HEAD_DIM > lanes.stop:
+                continue
+            masked = scores.pop(head) * SCALE + bias
+            highest = jnp.max(masked, axis=-1, keepdims=True)
+            weights = jnp.exp2(masked - highest)
+            inverses[head] = 1.0 / jnp.sum(weights, axis=-1, keepdims=True)
+            write_weights(head, weights.astype(jnp.bfloat16))
+    for first in range(0, channels, LANES):
+        heads = tile_heads(first)
+        parts = [jnp.broadcast_to(inverses[head], (rows, LANES)) for head in heads]
+        write_inverse(slice(first, first + LANES), by_head(parts, heads, first, rows))
+
+
+def blend(channels, rows, read_weights, read_inverse, read_values, write):
+    for lanes, heads in windows_of(channels):
         blended = jnp.dot(
-            read_weights(pair), read_values(window_of(pair)), preferred_element_type=jnp.float32
-        )
-        mask = head_masks(pair, rows)[0]
-        both = jnp.where(mask, blended[:rows], blended[rows:]) * inverse
-        low = both[:, :LANES]
-        if carry is not None:
-            low = low + carry
-        write(slice(pair * LANES, (pair + 1) * LANES), low.astype(jnp.bfloat16))
-        carry = both[:, LANES:]
-    write(slice(pairs * LANES, (pairs + 1) * LANES), carry.astype(jnp.bfloat16))
+            read_weights(heads), read_values(lanes), preferred_element_type=jnp.float32
+        )
+        for first in range(lanes.start, lanes.stop, LANES):
+            tile = slice(first, first + LANES)
+            inside = slice(first - lanes.start, first - lanes.start + LANES)
+            parts = []
+            for head in tile_heads(first):
+                place = (head - heads[0]) * rows
+                parts.append(blended[place : place + rows, inside])
+            chosen = by_head(parts, tile_heads(first), first, rows) * read_inverse(tile)
+            write(tile, chosen.astype(jnp.bfloat16))
 
 
 def read_tokens(refs, frame, lanes):
     return jnp.concatenate(
-        [ref[frame, :, :, lanes].reshape(-1, WINDOW) for ref in refs], axis=0
+        [ref[frame, :, :, lanes].reshape(-1, lanes.stop - lanes.start) for ref in refs], axis=0
     )
 
 
 def read_row(refs, row, lanes):
-    return jnp.concatenate([ref[:, row, :, lanes].reshape(-1, WINDOW) for ref in refs], axis=0)
+    return jnp.concatenate(
+        [ref[:, row, :, lanes].reshape(-1, lanes.stop - lanes.start) for ref in refs], axis=0
+    )
 
 
 def stage_kernel(blocks, space, index_ref, lists_ref, *refs):
@@ -154,21 +175,33 @@
 
 def spatial_weigh_kernel(blocks, bias_ref, q_ref, *refs):
     k_refs, weights_ref, inverse_ref = refs[:blocks], *refs[-2:]
-    frames, rows, columns, channels = q_ref.shape
     bias = bias_ref[...]
-    bias = jnp.concatenate([bias, bias], axis=0)
-    for frame in range(frames):
-        for pair in range(channels // PAIR):
-            lanes = window_of(pair)
-            weights_ref[frame, pair], inverse_ref[frame, pair] = weigh_pair(
-                pair, read_tokens([q_ref], frame, lanes), read_tokens(k_refs, frame, lanes), bias
-            )
+    for frame in range(q_ref.shape[0]):
+
+        def write_weights(head, value):
+            weights_ref[frame, head] = value
+
+        def write_inverse(lanes, value):
+            inverse_ref[frame, :, lanes] = value
+
+        weigh(
+            q_ref.shape[-1],
+            lambda lanes: read_tokens([q_ref], frame, lanes),
+            lambda lanes: read_tokens(k_refs, frame, lanes),
+            bias,
+            write_weights,
+            write_inverse,
+        )
+
+
+def read_weights(weights_ref, group, heads):
+    _, _, rows, keys = weights_ref.shape
+    return weights_ref[group, heads[0] : heads[-1] + 1].reshape(len(heads) * rows, keys)
 
 
 def spatial_blend_kernel(blocks, weights_ref, inverse_ref, *refs):
     v_refs, (out_ref, held, sems) = refs[:blocks], refs[-3:]
     frames, rows, columns, channels = held.shape
-    pairs = channels // PAIR
     moves = []
     for frame in range(frames):
         sent = 0
@@ -176,7 +209,7 @@
         def write(lanes, value):
             nonlocal sent
             held[frame, :, :, lanes] = value.reshape(rows, columns, LANES)
-            if lanes.stop in (channels // 2 // LANES * LANES, channels):
+            if lanes.stop in (channels // 2 // WINDOW * WINDOW, channels):
                 part = (frame, slice(None), slice(None), slice(sent, lanes.stop))
                 moves.append(
                     pltpu.make_async_copy(held.at[part], out_ref.at[part], sems.at[len(moves)])
@@ -184,10 +217,11 @@
                 moves[-1].start()
                 sent = lanes.stop
 
-        blend_pairs(
-            pairs,
-            lambda pair: weights_ref[frame, pair],
-            lambda pair: inverse_ref[frame, pair],
+        blend(
+            channels,
+            rows * columns,
+            lambda heads: read_weights(weights_ref, frame, heads),
+            lambda lanes: inverse_ref[frame, :, lanes],
             lambda lanes: read_tokens(v_refs, frame, lanes),
             write,
         )
@@ -198,16 +232,26 @@
 def temporal_weigh_kernel(blocks, q_ref, *refs):
     k_refs, weights_ref, inverse_ref = refs[:blocks], *refs[-2:]
     frames, rows, columns, channels = q_ref.shape
-    shape = (2 * frames * columns, sum(ref.shape[0] for ref in k_refs) * columns)
+    shape = (frames * columns, sum(ref.shape[0] for ref in k_refs) * columns)
     own = lax.broadcasted_iota(jnp.int32, shape, 0) % columns
     other = lax.broadcasted_iota(jnp.int32, shape, 1) % columns
     bias = jnp.where(own == other, 0.0, big_negative)
     for row in range(rows):
-        for pair in range(channels // PAIR):
-            lanes = window_of(pair)
-            weights_ref[row, pair], inverse_ref[row, pair] = weigh_pair(
-                pair, read_row([q_ref], row, lanes), read_row(k_refs, row, lanes), bias
-            )
+
+        def write_weights(head, value):
+            weights_ref[row, head] = value
+
+        def write_inverse(lanes, value):
+            inverse_ref[row, :, lanes] = value
+
+        weigh(
+            channels,
+            lambda lanes: read_row([q_ref], row, lanes),
+            lambda lanes: read_row(k_refs, row, lanes),
+            bias,
+            write_weights,
+            write_inverse,
+        )
 
 
 def temporal_blend_kernel(blocks, weights_ref, inverse_ref, *refs):
@@ -219,10 +263,11 @@
         def write(lanes, value):
             held[:, row, :, lanes] = value.reshape(frames, columns, LANES)
 
-        blend_pairs(
-            channels // PAIR,
-            lambda pair: weights_ref[row, pair],
-            lambda pair: inverse_ref[row, pair],
+        blend(
+            channels,
+            frames * columns,
+            lambda heads: read_weights(weights_ref, row, heads),
+            lambda lanes: inverse_ref[row, :, lanes],
             lambda lanes: read_row(v_refs, row, lanes),
             write,
         )
@@ -279,10 +324,10 @@
 
 
 def weigh_shapes(groups, channels, queries, keys):
-    pairs = channels // PAIR
+    heads = channels // HEAD_DIM
     return (
-        jax.ShapeDtypeStruct((groups, pairs, 2 * queries, keys), jnp.bfloat16),
-        jax.ShapeDtypeStruct((groups, pairs, queries, WINDOW), jnp.float32),
+        jax.ShapeDtypeStruct((groups, heads, queries, keys), jnp.bfloat16),
+        jax.ShapeDtypeStruct((groups, queries, channels), jnp.float32),
     )
 
 

time: 23.6 us -> 23.5 us (level)
  no operation moved by 1% of the time
where the time goes in v11:
time: 23.5 us; the launch traced here: 23.3 us
  starting transfers between devices  9.62 us (41%)
  waiting for transfers between devices  6.2 us (26%)
  Pallas kernels  6.02 us (26%)
  between operations  0.76 us (3%)
  local copies, waits for them, and re-layouts  0.7 us (3%)
    ppermute x4, waiting for transfers between devices, exchanged(): return lax.ppermute(value, AXES, pairs)  6.18 us
    ppermute x4, starting transfers between devices, swapped(): lax.ppermute(value, axis, [(i, i ^ step) for i in range(lax.axis_size(axi...  4.86 us
    ppermute x4, starting transfers between devices, exchanged(): return lax.ppermute(value, AXES, pairs)  4.76 us
    pallas_call x6, Pallas kernels, call(): pl.pallas_call(kernel, out_shape=out_shape, in_specs=[in_smem] * len(scal...  4.24 us
    pallas_call x1, Pallas kernels, staged(): pl.pallas_call(functools.partial(stage_kernel, blocks, space), out_shape=...  1.77 us
    unnamed x8, local copies, waits for them, and re-layouts  0.7 us
  transfers between devices with their start and end apart: 8, of which 3 were waited for; matrix products, arithmetic and copies ran while one was open for 0% of the time, Pallas kernels for 21%

profile of v11, /device:TPU:0, one launch (start us, length us, event | category | flops | bytes accessed | tf_op | source)
XLA Modules:
  0.0 23.3 jit_solution(11415141530276123523)
XLA Ops:
  0.6 3.0 %collective-permute-start.2 = (bf16[2,4,16,1152]{3,2,1,0:T(8,128)(2,1)}, bf16[2,4,16,1152]{3,2,1,0:T(8,128)(2,1)S(1)}, u32[]{:S(2)}, u32[]{:S(2)}) collective-permute-start(bf16[2,4,16,1152]{3,2,1,0:T(8,128)(2,1)} %refs_0_.5), channel_id=1, source_target_pairs={{0,2},{1,3},{2,0},{3,1},{4,6},{5,7},{6,4},{7,5},{8,10},{9,11},{10,... | collective-permute-start | bytes 884744 | tf_op jit(solution)/shard_map/ppermute | solution.py:46
  3.6 1.6 %collective-permute-start.1 = (bf16[2,4,16,1152]{3,2,1,0:T(8,128)(2,1)}, bf16[2,4,16,1152]{3,2,1,0:T(8,128)(2,1)S(1)}, u32[]{:S(2)}, u32[]{:S(2)}) collective-permute-start(bf16[2,4,16,1152]{3,2,1,0:T(8,128)(2,1)} %refs_1_.1), channel_id=1, source_target_pairs={{0,4},{1,5},{2,6},{3,7},{4,0},{5,1},{6,2},{7,3},{8,12},{9,13},{10,... | collective-permute-start | bytes 884744 | tf_op jit(solution)/shard_map/ppermute | solution.py:42
  5.2 1.5 %collective-permute-start = (bf16[2,4,16,1152]{3,2,1,0:T(8,128)(2,1)}, bf16[2,4,16,1152]{3,2,1,0:T(8,128)(2,1)S(1)}, u32[]{:S(2)}, u32[]{:S(2)}) collective-permute-start(bf16[2,4,16,1152]{3,2,1,0:T(8,128)(2,1)} %refs_1_.1), channel_id=1, source_target_pairs={{0,16},{1,17},{2,18},{3,19},{4,8},{5,9},{6,10},{7,11},{8,4},{9,5},... | collective-permute-start | bytes 884744 | tf_op jit(solution)/shard_map/ppermute | solution.py:42
  6.7 0.5 %collective-permute-start.3 = (bf16[2,4,16,1152]{3,2,1,0:T(8,128)(2,1)}, bf16[2,4,16,1152]{3,2,1,0:T(8,128)(2,1)S(1)}, u32[]{:S(2)}, u32[]{:S(2)}) collective-permute-start(bf16[2,4,16,1152]{3,2,1,0:T(8,128)(2,1)} %refs_0_.4), channel_id=1, source_target_pairs={{0,16},{1,17},{2,18},{3,19},{4,8},{5,9},{6,10},{7,11},{8,4},{9,5},... | collective-permute-start | bytes 884744 | tf_op jit(solution)/shard_map/ppermute | solution.py:42
  7.2 1.2 %collective-permute-start.4 = (bf16[2,4,16,1152]{3,2,1,0:T(8,128)(2,1)}, bf16[2,4,16,1152]{3,2,1,0:T(8,128)(2,1)S(1)}, u32[]{:S(2)}, u32[]{:S(2)}) collective-permute-start(bf16[2,4,16,1152]{3,2,1,0:T(8,128)(2,1)} %refs_0_.4), channel_id=1, source_target_pairs={{0,4},{1,5},{2,6},{3,7},{4,0},{5,1},{6,2},{7,3},{8,12},{9,13},{10,... | collective-permute-start | bytes 884744 | tf_op jit(solution)/shard_map/ppermute | solution.py:42
  8.4 0.0 copy-start.3
  8.4 0.7 %copy-done.3 = s32[16,8]{0,1:T(8,128)S(1)} copy-done((s32[16,8]{0,1:T(8,128)S(1)}, s32[16,8]{0,1:T(8,128)}, u32[]{:S(2)}) %copy-start.3) | copy-done | bytes 536
  9.1 1.8 %stage.1 = (f32[64,192]{1,0:T(8,128)S(1)}, bf16[2,4,16,1152]{3,2,1,0:T(8,128)(2,1)S(1)}, bf16[2,4,16,1152]{3,2,1,0:T(8,128)(2,1)S(1)}, bf16[2,4,16,1152]{3,2,1,0:T(8,128)(2,1)S(1)}) custom-call(s32[1]{0:T(128)} %bitcast.index_ref, s32[8,16]{1,0:T(8,128)S(1)} %bitcast.2, bf16[2,4,16,1152]{3,2,1,0:T(8,128)(2,1)} %refs_0_.3, bf16[2,4,16,1152]{3,2,1,0:T(8,128)(2,1)} %refs_1_.1, ...), custom_call_target="tpu_custom_call" | custom-call | flops 1 | bytes 1 | tf_op jit(solution)/shard_map/stage/pallas_call | solution.py:163
  10.9 0.0 collective-permute-done.2.refs_3_.refs_1_
  10.9 1.7 %collective-permute-start.6 = (bf16[2,4,16,1152]{3,2,1,0:T(8,128)(2,1)S(1)}, bf16[2,4,16,1152]{3,2,1,0:T(8,128)(2,1)S(1)}, u32[]{:S(2)}, u32[]{:S(2)}) collective-permute-start(bf16[2,4,16,1152]{3,2,1,0:T(8,128)(2,1)S(1)} %get-tuple-element.17.refs_0_), channel_id=1, source_target_pairs={{0,2},{1,3},{2,0},{3,1},{4,6},{5,7},{6,4},{7,5},{8,10},{9,11},{10,... | collective-permute-start | bytes 884744 | tf_op jit(solution)/shard_map/ppermute | solution.py:46
  12.6 1.2 %collective-permute-done.1.refs_2_ = bf16[2,4,16,1152]{3,2,1,0:T(8,128)(2,1)S(1)} collective-permute-done((bf16[2,4,16,1152]{3,2,1,0:T(8,128)(2,1)}, bf16[2,4,16,1152]{3,2,1,0:T(8,128)(2,1)S(1)}, u32[]{:S(2)}, u32[]{:S(2)}) %collective-permute-start.1) | collective-permute-done | bytes 294944 | tf_op jit(solution)/shard_map/ppermute | solution.py:42
  13.8 1.6 %collective-permute-done.refs_1_ = bf16[2,4,16,1152]{3,2,1,0:T(8,128)(2,1)S(1)} collective-permute-done((bf16[2,4,16,1152]{3,2,1,0:T(8,128)(2,1)}, bf16[2,4,16,1152]{3,2,1,0:T(8,128)(2,1)S(1)}, u32[]{:S(2)}, u32[]{:S(2)}) %collective-permute-start) | collective-permute-done | bytes 294944 | tf_op jit(solution)/shard_map/ppermute | solution.py:42
  15.4 0.0 copy-start
  15.4 1.0 %spatial_weigh.1 = (bf16[2,16,64,192]{3,2,1,0:T(8,128)(2,1)S(1)}, f32[2,64,1152]{2,1,0:T(8,128)S(1)}) custom-call(f32[64,192]{1,0:T(8,128)S(1)} %get-tuple-element.10.bias_ref, bf16[2,4,16,1152]{3,2,1,0:T(8,128)(2,1)S(1)} %get-tuple-element.11.q_ref, bf16[2,4,16,1152]{3,2,1,0:T(8,128)(2,1)S(1)} %get-tuple-element.12.refs_0_, ...), custom_call_target="tpu_custom_call" | custom-call | flops 1 | bytes 1 | tf_op jit(solution)/shard_map/spatial_weigh/pallas_call | solution.py:286
  16.4 0.0 copy-done
  16.4 0.0 copy-start.1
  16.4 0.1 collective-permute-start.5
  16.5 3.4 %collective-permute-done.3.refs_1_.refs_3_ = bf16[2,4,16,1152]{3,2,1,0:T(8,128)(2,1)S(1)} collective-permute-done((bf16[2,4,16,1152]{3,2,1,0:T(8,128)(2,1)}, bf16[2,4,16,1152]{3,2,1,0:T(8,128)(2,1)S(1)}, u32[]{:S(2)}, u32[]{:S(2)}) %collective-permute-start.3) | collective-permute-done | bytes 294944 | tf_op jit(solution)/shard_map/ppermute | solution.py:42
  19.9 0.0 collective-permute-done.4.refs_2_.refs_4_
  19.9 0.0 collective-permute-done.6.refs_1_
  20.0 0.1 collective-permute-start.7
  20.1 0.0 copy-done.1
  20.1 0.0 copy-start.2
  20.1 1.2 %spatial_blend.1 = bf16[2,4,16,1152]{3,2,1,0:T(8,128)(2,1)} custom-call(bf16[2,16,64,192]{3,2,1,0:T(8,128)(2,1)S(1)} %get-tuple-element.13.weights_ref.refs_2_, f32[2,64,1152]{2,1,0:T(8,128)S(1)} %get-tuple-element.14.inverse_ref, bf16[2,4,16,1152]{3,2,1,0:T(8,128)(2,1)S(1)} %copy-done.1, ...), custom_call_target="tpu_custom_call" | custom-call | flops 1 | bytes 1 | tf_op jit(solution)/shard_map/spatial_blend/pallas_call | solution.py:286
  21.3 0.0 collective-permute-done.5.refs_1_
  21.3 0.0 copy-done.2
  21.3 0.8 %temporal_weigh.1 = (bf16[4,16,32,128]{3,2,1,0:T(8,128)(2,1)S(1)}, f32[4,32,1152]{2,1,0:T(8,128)S(1)}) custom-call(bf16[2,4,16,1152]{3,2,1,0:T(8,128)(2,1)S(1)} %copy-done.2, bf16[4,4,16,1152]{3,2,1,0:T(8,128)(2,1)S(1)} %join.2.refs_0_, bf16[4,4,16,1152]{3,2,1,0:T(8,128)(2,1)S(1)} %collective-permute-done.5.refs_1_), custom_call_target="tpu_custom_call" | custom-call | flops 1 | bytes 1 | tf_op jit(solution)/shard_map/temporal_weigh/pallas_call | solution.py:286
  22.1 0.0 collective-permute-done.7.refs_1_
  22.1 1.2 %temporal_blend.1 = bf16[2,4,16,1152]{3,2,1,0:T(8,128)(2,1)} custom-call(bf16[4,16,32,128]{3,2,1,0:T(8,128)(2,1)S(1)} %get-tuple-element.15.weights_ref, f32[4,32,1152]{2,1,0:T(8,128)S(1)} %get-tuple-element.16.inverse_ref, bf16[4,4,16,1152]{3,2,1,0:T(8,128)(2,1)S(1)} %join.3.refs_0_, bf16[4,4,16,1152]{3,2,1,0:T(8,128)(2,1)S(1)} %collective-permute-done.7.refs_1_), custom_call_target="tpu_custom_call" | custom-call | flops 1 | bytes 1 | tf_op jit(solution)/shard_map/temporal_blend/pallas_call | solution.py:286
  (2 shorter events, 0.1 us)
Async XLA Ops:
  0.6 10.2 %collective-permute-start.2 = (bf16[2,4,16,1152]{3,2,1,0:T(8,128)(2,1)}, bf16[2,4,16,1152]{3,2,1,0:T(8,128)(2,1)S(1)}, u32[]{:S(2)}, u32[]{:S(2)}) collective-permute-start(bf16[2,4,16,1152]{3,2,1,0:T(8,128)(2,1)} %refs_0_.5), channel_id=1, source_target_pairs={{0,2},{1,3},{2,0},{3,1},{4,6},{5,7},{6,4},{7,5},{8,10},{9,11},{10,... | collective-permute-start | bytes 884744 | tf_op jit(solution)/shard_map/ppermute | solution.py:46
  3.6 10.1 %collective-permute-start.1 = (bf16[2,4,16,1152]{3,2,1,0:T(8,128)(2,1)}, bf16[2,4,16,1152]{3,2,1,0:T(8,128)(2,1)S(1)}, u32[]{:S(2)}, u32[]{:S(2)}) collective-permute-start(bf16[2,4,16,1152]{3,2,1,0:T(8,128)(2,1)} %refs_1_.1), channel_id=1, source_target_pairs={{0,4},{1,5},{2,6},{3,7},{4,0},{5,1},{6,2},{7,3},{8,12},{9,13},{10,... | collective-permute-start | bytes 884744 | tf_op jit(solution)/shard_map/ppermute | solution.py:42
  5.2 10.2 %collective-permute-start = (bf16[2,4,16,1152]{3,2,1,0:T(8,128)(2,1)}, bf16[2,4,16,1152]{3,2,1,0:T(8,128)(2,1)S(1)}, u32[]{:S(2)}, u32[]{:S(2)}) collective-permute-start(bf16[2,4,16,1152]{3,2,1,0:T(8,128)(2,1)} %refs_1_.1), channel_id=1, source_target_pairs={{0,16},{1,17},{2,18},{3,19},{4,8},{5,9},{6,10},{7,11},{8,4},{9,5},... | collective-permute-start | bytes 884744 | tf_op jit(solution)/shard_map/ppermute | solution.py:42
  6.7 13.2 %collective-permute-start.3 = (bf16[2,4,16,1152]{3,2,1,0:T(8,128)(2,1)}, bf16[2,4,16,1152]{3,2,1,0:T(8,128)(2,1)S(1)}, u32[]{:S(2)}, u32[]{:S(2)}) collective-permute-start(bf16[2,4,16,1152]{3,2,1,0:T(8,128)(2,1)} %refs_0_.4), channel_id=1, source_target_pairs={{0,16},{1,17},{2,18},{3,19},{4,8},{5,9},{6,10},{7,11},{8,4},{9,5},... | collective-permute-start | bytes 884744 | tf_op jit(solution)/shard_map/ppermute | solution.py:42
  7.2 12.7 %collective-permute-start.4 = (bf16[2,4,16,1152]{3,2,1,0:T(8,128)(2,1)}, bf16[2,4,16,1152]{3,2,1,0:T(8,128)(2,1)S(1)}, u32[]{:S(2)}, u32[]{:S(2)}) collective-permute-start(bf16[2,4,16,1152]{3,2,1,0:T(8,128)(2,1)} %refs_0_.4), channel_id=1, source_target_pairs={{0,4},{1,5},{2,6},{3,7},{4,0},{5,1},{6,2},{7,3},{8,12},{9,13},{10,... | collective-permute-start | bytes 884744 | tf_op jit(solution)/shard_map/ppermute | solution.py:42
  8.4 0.7 %copy-start.3 = (s32[16,8]{0,1:T(8,128)S(1)}, s32[16,8]{0,1:T(8,128)}, u32[]{:S(2)}) copy-start(s32[16,8]{0,1:T(8,128)} %param.13) | copy-start | bytes 1540
  10.9 9.1 %collective-permute-start.6 = (bf16[2,4,16,1152]{3,2,1,0:T(8,128)(2,1)S(1)}, bf16[2,4,16,1152]{3,2,1,0:T(8,128)(2,1)S(1)}, u32[]{:S(2)}, u32[]{:S(2)}) collective-permute-start(bf16[2,4,16,1152]{3,2,1,0:T(8,128)(2,1)S(1)} %get-tuple-element.17.refs_0_), channel_id=1, source_target_pairs={{0,2},{1,3},{2,0},{3,1},{4,6},{5,7},{6,4},{7,5},{8,10},{9,11},{10,... | collective-permute-start | bytes 884744 | tf_op jit(solution)/shard_map/ppermute | solution.py:46
  15.4 1.0 %copy-start = (bf16[2,4,16,1152]{3,2,1,0:T(8,128)(2,1)S(1)}, bf16[2,4,16,1152]{3,2,1,0:T(8,128)(2,1)}, u32[]{:S(2)}) copy-start(bf16[2,4,16,1152]{3,2,1,0:T(8,128)(2,1)} %refs_0_.5) | copy-start | bytes 884740
  16.4 3.6 %copy-start.1 = (bf16[2,4,16,1152]{3,2,1,0:T(8,128)(2,1)S(1)}, bf16[2,4,16,1152]{3,2,1,0:T(8,128)(2,1)}, u32[]{:S(2)}) copy-start(bf16[2,4,16,1152]{3,2,1,0:T(8,128)(2,1)} %refs_0_.4) | copy-start | bytes 884740
  16.4 4.8 %collective-permute-start.5 = (bf16[4,4,16,1152]{3,2,1,0:T(8,128)(2,1)S(1)}, bf16[4,4,16,1152]{3,2,1,0:T(8,128)(2,1)S(1)}, u32[]{:S(2)}, u32[]{:S(2)}) collective-permute-start(bf16[4,4,16,1152]{3,2,1,0:T(8,128)(2,1)S(1)} %join.2.refs_0_), channel_id=1, source_target_pairs={{0,1},{1,0},{2,3},{3,2},{4,5},{5,4},{6,7},{7,6},{8,9},{9,8},{10,11... | collective-permute-start | bytes 1769480 | tf_op jit(solution)/shard_map/ppermute | solution.py:46
  20.0 2.1 %collective-permute-start.7 = (bf16[4,4,16,1152]{3,2,1,0:T(8,128)(2,1)S(1)}, bf16[4,4,16,1152]{3,2,1,0:T(8,128)(2,1)S(1)}, u32[]{:S(2)}, u32[]{:S(2)}) collective-permute-start(bf16[4,4,16,1152]{3,2,1,0:T(8,128)(2,1)S(1)} %join.3.refs_0_), channel_id=1, source_target_pairs={{0,1},{1,0},{2,3},{3,2},{4,5},{5,4},{6,7},{7,6},{8,9},{9,8},{10,11... | collective-permute-start | bytes 1769480 | tf_op jit(solution)/shard_map/ppermute | solution.py:46
  20.1 1.2 %copy-start.2 = (bf16[2,4,16,1152]{3,2,1,0:T(8,128)(2,1)S(1)}, bf16[2,4,16,1152]{3,2,1,0:T(8,128)(2,1)}, u32[]{:S(2)}) copy-start(bf16[2,4,16,1152]{3,2,1,0:T(8,128)(2,1)} %q_ref.1) | copy-start | bytes 884740

commit v12 on v11

--- a/solution.py
+++ b/solution.py
@@ -13,7 +13,7 @@
 WINDOW = 2 * LANES
 SCALE = HEAD_DIM ** (-0.5) * math.log2(math.e)
 big_negative = -1e30
-AXES = ("video", "space", "tm")
+AXES = ("space", "tm")
 
 
 def partner_of(index, distance, parity):
@@ -24,21 +24,16 @@
 
 
 def exchanged(value, distance, parity):
-    videos, length, others = [lax.axis_size(axis) for axis in AXES]
+    length, others = [lax.axis_size(axis) for axis in AXES]
     pairs = []
-    for video in range(videos):
-        for index in range(length):
-            there, partner = video, partner_of(index, distance, parity)
-            if not 0 <= partner < length:
-                partner = index
-                there = video ^ 1 if (video ^ 1) < videos else video
-            for other in range(others):
-                pairs.append(
-                    (
-                        (video * length + index) * others + other,
-                        (there * length + partner) * others + other,
-                    )
-                )
+    for index in range(length):
+        partner = partner_of(index, distance, parity)
+        for other in range(others):
+            if 0 <= partner < length:
+                target = partner * others + other
+            else:
+                target = index * others + (other ^ 1 if (other ^ 1) < others else other)
+            pairs.append((index * others + other, target))
     return lax.ppermute(value, AXES, pairs)
 
 
@@ -99,19 +94,21 @@
 
 
 def blend(channels, rows, read_weights, read_inverse, read_values, write):
-    for lanes, heads in windows_of(channels):
-        blended = jnp.dot(
-            read_weights(heads), read_values(lanes), preferred_element_type=jnp.float32
-        )
-        for first in range(lanes.start, lanes.stop, LANES):
-            tile = slice(first, first + LANES)
-            inside = slice(first - lanes.start, first - lanes.start + LANES)
-            parts = []
-            for head in tile_heads(first):
-                place = (head - heads[0]) * rows
-                parts.append(blended[place : place + rows, inside])
-            chosen = by_head(parts, tile_heads(first), first, rows) * read_inverse(tile)
-            write(tile, chosen.astype(jnp.bfloat16))
+    blended = []
+    for first in range(0, channels, LANES):
+        heads = tile_heads(first)
+        pair = first // LANES
+        if first + WINDOW <= channels:
+            values = read_values(slice(first, first + WINDOW))
+            weights = read_weights(range(2 * pair, 2 * pair + 2))
+            blended.append(jnp.dot(weights, values, preferred_element_type=jnp.float32))
+        parts = []
+        for head in heads:
+            place, lane = head % 2 * rows, first - head // 2 * LANES
+            parts.append(blended[head // 2][place : place + rows, lane : lane + LANES])
+        tile = slice(first, first + LANES)
+        chosen = by_head(parts, heads, first, rows) * read_inverse(tile)
+        write(tile, chosen.astype(jnp.bfloat16))
 
 
 def read_tokens(refs, frame, lanes):

time: 23.5 us -> 22.6 us (0.962)
  waiting for transfers between devices: 6.2 us -> 5.3 us
    ppermute x4, waiting for transfers between devices: 6.18 us -> 4.88 us  [exchanged(): return lax.ppermute(value, AXES, pairs)]
    ppermute x4, waiting for transfers between devices: 0.01 us -> 0.42 us  [swapped(): lax.ppermute(value, axis, [(i, i ^ step) for i in range(lax.axis_size(axi...]
where the time goes in v12:
time: 22.6 us; the launch traced here: 22.3 us
  starting transfers between devices  9.62 us (43%)
  Pallas kernels  5.9 us (26%)
  waiting for transfers between devices  5.3 us (23%)
  between operations  0.77 us (3%)
  local copies, waits for them, and re-layouts  0.7 us (3%)
    ppermute x4, waiting for transfers between devices, exchanged(): return lax.ppermute(value, AXES, pairs)  4.88 us
    ppermute x4, starting transfers between devices, swapped(): lax.ppermute(value, axis, [(i, i ^ step) for i in range(lax.axis_size(axi...  4.86 us
    ppermute x4, starting transfers between devices, exchanged(): return lax.ppermute(value, AXES, pairs)  4.76 us
    pallas_call x6, Pallas kernels, call(): pl.pallas_call(kernel, out_shape=out_shape, in_specs=[in_smem] * len(scal...  4.12 us
    pallas_call x1, Pallas kernels, staged(): pl.pallas_call(functools.partial(stage_kernel, blocks, space), out_shape=...  1.77 us
    unnamed x8, local copies, waits for them, and re-layouts  0.7 us
  transfers between devices with their start and end apart: 8, of which 3 were waited for; matrix products, arithmetic and copies ran while one was open for 0% of the time, Pallas kernels for 21%

profile of v12, /device:TPU:0, one launch (start us, length us, event | category | flops | bytes accessed | tf_op | source)
XLA Modules:
  0.0 22.3 jit_solution(16146984424678597512)
XLA Ops:
  0.6 3.0 %collective-permute-start.2 = (bf16[2,4,16,1152]{3,2,1,0:T(8,128)(2,1)}, bf16[2,4,16,1152]{3,2,1,0:T(8,128)(2,1)S(1)}, u32[]{:S(2)}, u32[]{:S(2)}) collective-permute-start(bf16[2,4,16,1152]{3,2,1,0:T(8,128)(2,1)} %refs_0_.5), channel_id=1, source_target_pairs={{0,2},{1,3},{2,0},{3,1},{4,6},{5,7},{6,4},{7,5},{8,10},{9,11},{10,... | collective-permute-start | bytes 884744 | tf_op jit(solution)/shard_map/ppermute | solution.py:41
  3.6 1.6 %collective-permute-start.1 = (bf16[2,4,16,1152]{3,2,1,0:T(8,128)(2,1)}, bf16[2,4,16,1152]{3,2,1,0:T(8,128)(2,1)S(1)}, u32[]{:S(2)}, u32[]{:S(2)}) collective-permute-start(bf16[2,4,16,1152]{3,2,1,0:T(8,128)(2,1)} %refs_1_.1), channel_id=1, source_target_pairs={{0,4},{1,5},{2,6},{3,7},{4,0},{5,1},{6,2},{7,3},{8,12},{9,13},{10,... | collective-permute-start | bytes 884744 | tf_op jit(solution)/shard_map/ppermute | solution.py:37
  5.2 0.0 collective-permute-start
  5.2 0.5 %collective-permute-start.3 = (bf16[2,4,16,1152]{3,2,1,0:T(8,128)(2,1)}, bf16[2,4,16,1152]{3,2,1,0:T(8,128)(2,1)S(1)}, u32[]{:S(2)}, u32[]{:S(2)}) collective-permute-start(bf16[2,4,16,1152]{3,2,1,0:T(8,128)(2,1)} %refs_0_.4), channel_id=1, source_target_pairs={{0,1},{1,0},{2,3},{3,2},{4,8},{5,9},{6,10},{7,11},{8,4},{9,5},{10,... | collective-permute-start | bytes 884744 | tf_op jit(solution)/shard_map/ppermute | solution.py:37
  5.7 2.7 %collective-permute-start.4 = (bf16[2,4,16,1152]{3,2,1,0:T(8,128)(2,1)}, bf16[2,4,16,1152]{3,2,1,0:T(8,128)(2,1)S(1)}, u32[]{:S(2)}, u32[]{:S(2)}) collective-permute-start(bf16[2,4,16,1152]{3,2,1,0:T(8,128)(2,1)} %refs_0_.4), channel_id=1, source_target_pairs={{0,4},{1,5},{2,6},{3,7},{4,0},{5,1},{6,2},{7,3},{8,12},{9,13},{10,... | collective-permute-start | bytes 884744 | tf_op jit(solution)/shard_map/ppermute | solution.py:37
  8.4 0.0 copy-start.3
  8.4 0.7 %copy-done.3 = s32[16,8]{0,1:T(8,128)S(1)} copy-done((s32[16,8]{0,1:T(8,128)S(1)}, s32[16,8]{0,1:T(8,128)}, u32[]{:S(2)}) %copy-start.3) | copy-done | bytes 536
  9.1 1.8 %stage.1 = (f32[64,192]{1,0:T(8,128)S(1)}, bf16[2,4,16,1152]{3,2,1,0:T(8,128)(2,1)S(1)}, bf16[2,4,16,1152]{3,2,1,0:T(8,128)(2,1)S(1)}, bf16[2,4,16,1152]{3,2,1,0:T(8,128)(2,1)S(1)}) custom-call(s32[1]{0:T(128)} %bitcast.index_ref, s32[8,16]{1,0:T(8,128)S(1)} %bitcast.2, bf16[2,4,16,1152]{3,2,1,0:T(8,128)(2,1)} %refs_0_.3, bf16[2,4,16,1152]{3,2,1,0:T(8,128)(2,1)} %refs_1_.1, ...), custom_call_target="tpu_custom_call" | custom-call | flops 1 | bytes 1 | tf_op jit(solution)/shard_map/stage/pallas_call | solution.py:160
  10.9 0.0 collective-permute-done.2.refs_3_.refs_1_
  10.9 1.7 %collective-permute-start.6 = (bf16[2,4,16,1152]{3,2,1,0:T(8,128)(2,1)S(1)}, bf16[2,4,16,1152]{3,2,1,0:T(8,128)(2,1)S(1)}, u32[]{:S(2)}, u32[]{:S(2)}) collective-permute-start(bf16[2,4,16,1152]{3,2,1,0:T(8,128)(2,1)S(1)} %get-tuple-element.17.refs_0_), channel_id=1, source_target_pairs={{0,2},{1,3},{2,0},{3,1},{4,6},{5,7},{6,4},{7,5},{8,10},{9,11},{10,... | collective-permute-start | bytes 884744 | tf_op jit(solution)/shard_map/ppermute | solution.py:41
  12.6 1.2 %collective-permute-done.1.refs_2_ = bf16[2,4,16,1152]{3,2,1,0:T(8,128)(2,1)S(1)} collective-permute-done((bf16[2,4,16,1152]{3,2,1,0:T(8,128)(2,1)}, bf16[2,4,16,1152]{3,2,1,0:T(8,128)(2,1)S(1)}, u32[]{:S(2)}, u32[]{:S(2)}) %collective-permute-start.1) | collective-permute-done | bytes 294944 | tf_op jit(solution)/shard_map/ppermute | solution.py:37
  13.8 0.0 collective-permute-done.refs_1_
  13.8 0.0 copy-start
  13.8 1.0 %spatial_weigh.1 = (bf16[2,16,64,192]{3,2,1,0:T(8,128)(2,1)S(1)}, f32[2,64,1152]{2,1,0:T(8,128)S(1)}) custom-call(f32[64,192]{1,0:T(8,128)S(1)} %get-tuple-element.10.bias_ref, bf16[2,4,16,1152]{3,2,1,0:T(8,128)(2,1)S(1)} %get-tuple-element.11.q_ref, bf16[2,4,16,1152]{3,2,1,0:T(8,128)(2,1)S(1)} %get-tuple-element.12.refs_0_, ...), custom_call_target="tpu_custom_call" | custom-call | flops 1 | bytes 1 | tf_op jit(solution)/shard_map/spatial_weigh/pallas_call | solution.py:283
  14.8 0.0 copy-done
  14.8 0.0 copy-start.1
  14.9 0.1 collective-permute-start.5
  14.9 0.0 collective-permute-done.3.refs_1_.refs_3_
  14.9 3.7 %collective-permute-done.4.refs_2_.refs_4_ = bf16[2,4,16,1152]{3,2,1,0:T(8,128)(2,1)S(1)} collective-permute-done((bf16[2,4,16,1152]{3,2,1,0:T(8,128)(2,1)}, bf16[2,4,16,1152]{3,2,1,0:T(8,128)(2,1)S(1)}, u32[]{:S(2)}, u32[]{:S(2)}) %collective-permute-start.4) | collective-permute-done | bytes 294944 | tf_op jit(solution)/shard_map/ppermute | solution.py:37
  18.6 0.4 %collective-permute-done.6.refs_1_ = bf16[2,4,16,1152]{3,2,1,0:T(8,128)(2,1)S(1)} collective-permute-done((bf16[2,4,16,1152]{3,2,1,0:T(8,128)(2,1)S(1)}, bf16[2,4,16,1152]{3,2,1,0:T(8,128)(2,1)S(1)}, u32[]{:S(2)}, u32[]{:S(2)}) %collective-permute-start.6) | collective-permute-done | bytes 294944 | tf_op jit(solution)/shard_map/ppermute | solution.py:41
  19.1 0.1 collective-permute-start.7
  19.2 0.0 copy-done.1
  19.2 0.0 copy-start.2
  19.2 1.1 %spatial_blend.1 = bf16[2,4,16,1152]{3,2,1,0:T(8,128)(2,1)} custom-call(bf16[2,16,64,192]{3,2,1,0:T(8,128)(2,1)S(1)} %get-tuple-element.13.weights_ref.refs_2_, f32[2,64,1152]{2,1,0:T(8,128)S(1)} %get-tuple-element.14.inverse_ref, bf16[2,4,16,1152]{3,2,1,0:T(8,128)(2,1)S(1)} %copy-done.1, ...), custom_call_target="tpu_custom_call" | custom-call | flops 1 | bytes 1 | tf_op jit(solution)/shard_map/spatial_blend/pallas_call | solution.py:283
  20.3 0.0 collective-permute-done.5.refs_1_
  20.3 0.0 copy-done.2
  20.3 0.8 %temporal_weigh.1 = (bf16[4,16,32,128]{3,2,1,0:T(8,128)(2,1)S(1)}, f32[4,32,1152]{2,1,0:T(8,128)S(1)}) custom-call(bf16[2,4,16,1152]{3,2,1,0:T(8,128)(2,1)S(1)} %copy-done.2, bf16[4,4,16,1152]{3,2,1,0:T(8,128)(2,1)S(1)} %join.2.refs_0_, bf16[4,4,16,1152]{3,2,1,0:T(8,128)(2,1)S(1)} %collective-permute-done.5.refs_1_), custom_call_target="tpu_custom_call" | custom-call | flops 1 | bytes 1 | tf_op jit(solution)/shard_map/temporal_weigh/pallas_call | solution.py:283
  21.2 0.0 collective-permute-done.7.refs_1_
  21.2 1.1 %temporal_blend.1 = bf16[2,4,16,1152]{3,2,1,0:T(8,128)(2,1)} custom-call(bf16[4,16,32,128]{3,2,1,0:T(8,128)(2,1)S(1)} %get-tuple-element.15.weights_ref, f32[4,32,1152]{2,1,0:T(8,128)S(1)} %get-tuple-element.16.inverse_ref, bf16[4,4,16,1152]{3,2,1,0:T(8,128)(2,1)S(1)} %join.3.refs_0_, bf16[4,4,16,1152]{3,2,1,0:T(8,128)(2,1)S(1)} %collective-permute-done.7.refs_1_), custom_call_target="tpu_custom_call" | custom-call | flops 1 | bytes 1 | tf_op jit(solution)/shard_map/temporal_blend/pallas_call | solution.py:283
  (2 shorter events, 0.1 us)
Async XLA Ops:
  0.6 10.2 %collective-permute-start.2 = (bf16[2,4,16,1152]{3,2,1,0:T(8,128)(2,1)}, bf16[2,4,16,1152]{3,2,1,0:T(8,128)(2,1)S(1)}, u32[]{:S(2)}, u32[]{:S(2)}) collective-permute-start(bf16[2,4,16,1152]{3,2,1,0:T(8,128)(2,1)} %refs_0_.5), channel_id=1, source_target_pairs={{0,2},{1,3},{2,0},{3,1},{4,6},{5,7},{6,4},{7,5},{8,10},{9,11},{10,... | collective-permute-start | bytes 884744 | tf_op jit(solution)/shard_map/ppermute | solution.py:41
  3.6 10.1 %collective-permute-start.1 = (bf16[2,4,16,1152]{3,2,1,0:T(8,128)(2,1)}, bf16[2,4,16,1152]{3,2,1,0:T(8,128)(2,1)S(1)}, u32[]{:S(2)}, u32[]{:S(2)}) collective-permute-start(bf16[2,4,16,1152]{3,2,1,0:T(8,128)(2,1)} %refs_1_.1), channel_id=1, source_target_pairs={{0,4},{1,5},{2,6},{3,7},{4,0},{5,1},{6,2},{7,3},{8,12},{9,13},{10,... | collective-permute-start | bytes 884744 | tf_op jit(solution)/shard_map/ppermute | solution.py:37
  5.2 8.6 %collective-permute-start = (bf16[2,4,16,1152]{3,2,1,0:T(8,128)(2,1)}, bf16[2,4,16,1152]{3,2,1,0:T(8,128)(2,1)S(1)}, u32[]{:S(2)}, u32[]{:S(2)}) collective-permute-start(bf16[2,4,16,1152]{3,2,1,0:T(8,128)(2,1)} %refs_1_.1), channel_id=1, source_target_pairs={{0,1},{1,0},{2,3},{3,2},{4,8},{5,9},{6,10},{7,11},{8,4},{9,5},{10,... | collective-permute-start | bytes 884744 | tf_op jit(solution)/shard_map/ppermute | solution.py:37
  5.2 9.7 %collective-permute-start.3 = (bf16[2,4,16,1152]{3,2,1,0:T(8,128)(2,1)}, bf16[2,4,16,1152]{3,2,1,0:T(8,128)(2,1)S(1)}, u32[]{:S(2)}, u32[]{:S(2)}) collective-permute-start(bf16[2,4,16,1152]{3,2,1,0:T(8,128)(2,1)} %refs_0_.4), channel_id=1, source_target_pairs={{0,1},{1,0},{2,3},{3,2},{4,8},{5,9},{6,10},{7,11},{8,4},{9,5},{10,... | collective-permute-start | bytes 884744 | tf_op jit(solution)/shard_map/ppermute | solution.py:37
  5.7 12.9 %collective-permute-start.4 = (bf16[2,4,16,1152]{3,2,1,0:T(8,128)(2,1)}, bf16[2,4,16,1152]{3,2,1,0:T(8,128)(2,1)S(1)}, u32[]{:S(2)}, u32[]{:S(2)}) collective-permute-start(bf16[2,4,16,1152]{3,2,1,0:T(8,128)(2,1)} %refs_0_.4), channel_id=1, source_target_pairs={{0,4},{1,5},{2,6},{3,7},{4,0},{5,1},{6,2},{7,3},{8,12},{9,13},{10,... | collective-permute-start | bytes 884744 | tf_op jit(solution)/shard_map/ppermute | solution.py:37
  8.4 0.7 %copy-start.3 = (s32[16,8]{0,1:T(8,128)S(1)}, s32[16,8]{0,1:T(8,128)}, u32[]{:S(2)}) copy-start(s32[16,8]{0,1:T(8,128)} %param.13) | copy-start | bytes 1540
  10.9 8.2 %collective-permute-start.6 = (bf16[2,4,16,1152]{3,2,1,0:T(8,128)(2,1)S(1)}, bf16[2,4,16,1152]{3,2,1,0:T(8,128)(2,1)S(1)}, u32[]{:S(2)}, u32[]{:S(2)}) collective-permute-start(bf16[2,4,16,1152]{3,2,1,0:T(8,128)(2,1)S(1)} %get-tuple-element.17.refs_0_), channel_id=1, source_target_pairs={{0,2},{1,3},{2,0},{3,1},{4,6},{5,7},{6,4},{7,5},{8,10},{9,11},{10,... | collective-permute-start | bytes 884744 | tf_op jit(solution)/shard_map/ppermute | solution.py:41
  13.8 1.0 %copy-start = (bf16[2,4,16,1152]{3,2,1,0:T(8,128)(2,1)S(1)}, bf16[2,4,16,1152]{3,2,1,0:T(8,128)(2,1)}, u32[]{:S(2)}) copy-start(bf16[2,4,16,1152]{3,2,1,0:T(8,128)(2,1)} %refs_0_.5) | copy-start | bytes 884740
  14.8 4.3 %copy-start.1 = (bf16[2,4,16,1152]{3,2,1,0:T(8,128)(2,1)S(1)}, bf16[2,4,16,1152]{3,2,1,0:T(8,128)(2,1)}, u32[]{:S(2)}) copy-start(bf16[2,4,16,1152]{3,2,1,0:T(8,128)(2,1)} %refs_0_.4) | copy-start | bytes 884740
  14.9 5.5 %collective-permute-start.5 = (bf16[4,4,16,1152]{3,2,1,0:T(8,128)(2,1)S(1)}, bf16[4,4,16,1152]{3,2,1,0:T(8,128)(2,1)S(1)}, u32[]{:S(2)}, u32[]{:S(2)}) collective-permute-start(bf16[4,4,16,1152]{3,2,1,0:T(8,128)(2,1)S(1)} %join.2.refs_0_), channel_id=1, source_target_pairs={{0,1},{1,0},{2,3},{3,2},{4,5},{5,4},{6,7},{7,6},{8,9},{9,8},{10,11... | collective-permute-start | bytes 1769480 | tf_op jit(solution)/shard_map/ppermute | solution.py:41
  19.1 2.1 %collective-permute-start.7 = (bf16[4,4,16,1152]{3,2,1,0:T(8,128)(2,1)S(1)}, bf16[4,4,16,1152]{3,2,1,0:T(8,128)(2,1)S(1)}, u32[]{:S(2)}, u32[]{:S(2)}) collective-permute-start(bf16[4,4,16,1152]{3,2,1,0:T(8,128)(2,1)S(1)} %join.3.refs_0_), channel_id=1, source_target_pairs={{0,1},{1,0},{2,3},{3,2},{4,5},{5,4},{6,7},{7,6},{8,9},{9,8},{10,11... | collective-permute-start | bytes 1769480 | tf_op jit(solution)/shard_map/ppermute | solution.py:41
  19.2 1.1 %copy-start.2 = (bf16[2,4,16,1152]{3,2,1,0:T(8,128)(2,1)S(1)}, bf16[2,4,16,1152]{3,2,1,0:T(8,128)(2,1)}, u32[]{:S(2)}) copy-start(bf16[2,4,16,1152]{3,2,1,0:T(8,128)(2,1)} %q_ref.1) | copy-start | bytes 884740

commit v13 on v12

--- a/solution.py
+++ b/solution.py
@@ -136,7 +136,7 @@
     index = index_ref[0]
     key_rows = []
     for distance in range(blocks // 2 + 1):
-        for parity in (1, 0) if distance else (0,):
+        for parity in (0, 1) if distance else (0,):
             owner = partner_of(index, distance, parity) if distance else index
             first = jnp.where((owner >= 0) & (owner < space), owner * rows, -(2**20))
             row = lax.broadcasted_iota(jnp.int32, (columns, rows * columns), 1) // columns
@@ -197,22 +197,12 @@
 
 
 def spatial_blend_kernel(blocks, weights_ref, inverse_ref, *refs):
-    v_refs, (out_ref, held, sems) = refs[:blocks], refs[-3:]
-    frames, rows, columns, channels = held.shape
-    moves = []
+    v_refs, out_ref = refs[:blocks], refs[-1]
+    frames, rows, columns, channels = out_ref.shape
     for frame in range(frames):
-        sent = 0
 
         def write(lanes, value):
-            nonlocal sent
-            held[frame, :, :, lanes] = value.reshape(rows, columns, LANES)
-            if lanes.stop in (channels // 2 // WINDOW * WINDOW, channels):
-                part = (frame, slice(None), slice(None), slice(sent, lanes.stop))
-                moves.append(
-                    pltpu.make_async_copy(held.at[part], out_ref.at[part], sems.at[len(moves)])
-                )
-                moves[-1].start()
-                sent = lanes.stop
+            out_ref[frame, :, :, lanes] = value.reshape(rows, columns, LANES)
 
         blend(
             channels,
@@ -222,8 +212,6 @@
             lambda lanes: read_tokens(v_refs, frame, lanes),
             write,
         )
-    for move in moves:
-        move.wait()
 
 
 def temporal_weigh_kernel(blocks, q_ref, *refs):
@@ -251,10 +239,11 @@
         )
 
 
-def temporal_blend_kernel(blocks, weights_ref, inverse_ref, *refs):
-    v_refs, (out_ref, held, sems) = refs[:blocks], refs[-3:]
+def last_kernel(blocks, spatial_ref, weights_ref, inverse_ref, *refs):
+    v_refs, (spatial_out_ref, out_ref, held, sems) = refs[:blocks], refs[-4:]
     frames, rows, columns, channels = held.shape
-    moves = []
+    moves = [pltpu.make_async_copy(spatial_ref, spatial_out_ref, sems.at[rows])]
+    moves[-1].start()
     for row in range(rows):
 
         def write(lanes, value):
@@ -276,7 +265,7 @@
         move.wait()
 
 
-def call(kernel, name, out_shape, scalars, arrays, flops, others=(), parts=0):
+def call(kernel, name, out_shape, scalars, arrays, flops, others=(), held=(), sems=0):
     in_vmem = pl.BlockSpec(memory_space=pltpu.VMEM)
     in_smem = pl.BlockSpec(memory_space=pltpu.SMEM)
     anywhere = pl.BlockSpec(memory_space=pl.ANY)
@@ -284,13 +273,8 @@
         kernel,
         out_shape=out_shape,
         in_specs=[in_smem] * len(scalars) + [in_vmem] * len(arrays) + [anywhere] * len(others),
-        out_specs=jax.tree.map(lambda _: anywhere if parts else in_vmem, out_shape),
-        scratch_shapes=[
-            pltpu.VMEM(out_shape.shape, out_shape.dtype),
-            pltpu.SemaphoreType.DMA((parts,)),
-        ]
-        if parts
-        else [],
+        out_specs=jax.tree.map(lambda _: anywhere if sems else in_vmem, out_shape),
+        scratch_shapes=[*held, pltpu.SemaphoreType.DMA((sems,))] if sems else [],
         compiler_params=pltpu.CompilerParams(vmem_limit_bytes=40 * 1024 * 1024),
         cost_estimate=pl.CostEstimate(
             flops=flops, bytes_accessed=1, transcendentals=0
@@ -337,7 +321,7 @@
     tokens = frames * rows * columns
     first_step = lax.axis_size("tm") // 2
 
-    exchanges = [(d, parity) for d in range(1, reach + 1) for parity in (1, 0)]
+    exchanges = [(d, parity) for d in range(1, reach + 1) for parity in (0, 1)]
     blocks = 1 + len(exchanges)
     bias, own_q, own_k, own_tv = staged(
         [spatial_q, spatial_k, temporal_v], index, key_lists.T, blocks, space
@@ -380,25 +364,24 @@
         1,
     )
     temporal_values = gathered(own_tv, received_values, [spatial_weights, *spatial_values[1:]])
-    spatial_out = call(
+    spatial_result = call(
         functools.partial(spatial_blend_kernel, len(spatial_values)),
         "spatial_blend",
         out_shape,
         [],
         [spatial_weights, spatial_inverse, *spatial_values],
         1,
-        parts=2 * frames,
-    )
-    temporal_out = call(
-        functools.partial(temporal_blend_kernel, blocks),
-        "temporal_blend",
-        out_shape,
-        [],
-        [temporal_weights, temporal_inverse, *temporal_values],
-        1,
-        parts=rows,
-    )
-    return (spatial_out, temporal_out)
+    )
+    return call(
+        functools.partial(last_kernel, len(temporal_values)),
+        "last",
+        (out_shape, out_shape),
+        [],
+        [spatial_result, temporal_weights, temporal_inverse, *temporal_values],
+        1,
+        held=[pltpu.VMEM(out_shape.shape, out_shape.dtype)],
+        sems=rows + 1,
+    )
 
 
 def solution(mesh):

time: 22.6 us -> 23.8 us (1.053)
  waiting for transfers between devices: 5.3 us -> 6.78 us
  Pallas kernels: 5.9 us -> 5.22 us
  local copies, waits for them, and re-layouts: 0.7 us -> 1.2 us
    ppermute x4, waiting for transfers between devices: 0.42 us -> 1.89 us  [swapped(): lax.ppermute(value, axis, [(i, i ^ step) for i in range(lax.axis_size(axi...]
    pallas_call x6, Pallas kernels: 4.12 us -> 3.45 us  [call(): pl.pallas_call(kernel, out_shape=out_shape, in_specs=[in_smem] * len(scal...]
    unnamed x8, local copies, waits for them, and re-layouts: 0.7 us -> 1.2 us
  transfers between devices with their start and end apart: 8 -> 8, of which waited for: 3 -> 4; matrix products, arithmetic and copies ran while one was open for 0% -> 0% of each run, Pallas kernels for 21% -> 17%
where the time goes in v13:
time: 23.8 us; the launch traced here: 23.6 us
  starting transfers between devices  9.62 us (40%)
  waiting for transfers between devices  6.78 us (28%)
  Pallas kernels  5.22 us (22%)
  local copies, waits for them, and re-layouts  1.2 us (5%)
  between operations  0.74 us (3%)
    ppermute x4, waiting for transfers between devices, exchanged(): return lax.ppermute(value, AXES, pairs)  4.89 us
    ppermute x4, starting transfers between devices, swapped(): lax.ppermute(value, axis, [(i, i ^ step) for i in range(lax.axis_size(axi...  4.88 us
    ppermute x4, starting transfers between devices, exchanged(): return lax.ppermute(value, AXES, pairs)  4.73 us
    pallas_call x6, Pallas kernels, call(): pl.pallas_call(kernel, out_shape=out_shape, in_specs=[in_smem] * len(scal...  3.45 us
    ppermute x4, waiting for transfers between devices, swapped(): lax.ppermute(value, axis, [(i, i ^ step) for i in range(lax.axis_size(axi...  1.89 us
    pallas_call x1, Pallas kernels, staged(): pl.pallas_call(functools.partial(stage_kernel, blocks, space), out_shape=...  1.77 us
    unnamed x8, local copies, waits for them, and re-layouts  1.2 us
  transfers between devices with their start and end apart: 8, of which 4 were waited for; matrix products, arithmetic and copies ran while one was open for 0% of the time, Pallas kernels for 17%

profile of v13, /device:TPU:0, one launch (start us, length us, event | category | flops | bytes accessed | tf_op | source)
XLA Modules:
  0.0 23.6 jit_solution(12487388648110484134)
XLA Ops:
  0.6 3.0 %collective-permute-start.2 = (bf16[2,4,16,1152]{3,2,1,0:T(8,128)(2,1)}, bf16[2,4,16,1152]{3,2,1,0:T(8,128)(2,1)S(1)}, u32[]{:S(2)}, u32[]{:S(2)}) collective-permute-start(bf16[2,4,16,1152]{3,2,1,0:T(8,128)(2,1)} %refs_0_.5), channel_id=1, source_target_pairs={{0,2},{1,3},{2,0},{3,1},{4,6},{5,7},{6,4},{7,5},{8,10},{9,11},{10,... | collective-permute-start | bytes 884744 | tf_op jit(solution)/shard_map/ppermute | solution.py:41
  3.6 1.6 %collective-permute-start = (bf16[2,4,16,1152]{3,2,1,0:T(8,128)(2,1)}, bf16[2,4,16,1152]{3,2,1,0:T(8,128)(2,1)S(1)}, u32[]{:S(2)}, u32[]{:S(2)}) collective-permute-start(bf16[2,4,16,1152]{3,2,1,0:T(8,128)(2,1)} %refs_1_.1), channel_id=1, source_target_pairs={{0,4},{1,5},{2,6},{3,7},{4,0},{5,1},{6,2},{7,3},{8,12},{9,13},{10,... | collective-permute-start | bytes 884744 | tf_op jit(solution)/shard_map/ppermute | solution.py:37
  5.2 0.0 collective-permute-start.1
  5.2 3.1 %collective-permute-start.3 = (bf16[2,4,16,1152]{3,2,1,0:T(8,128)(2,1)}, bf16[2,4,16,1152]{3,2,1,0:T(8,128)(2,1)S(1)}, u32[]{:S(2)}, u32[]{:S(2)}) collective-permute-start(bf16[2,4,16,1152]{3,2,1,0:T(8,128)(2,1)} %refs_0_.4), channel_id=1, source_target_pairs={{0,4},{1,5},{2,6},{3,7},{4,0},{5,1},{6,2},{7,3},{8,12},{9,13},{10,... | collective-permute-start | bytes 884744 | tf_op jit(solution)/shard_map/ppermute | solution.py:37
  8.4 0.0 collective-permute-start.4
  8.4 0.0 copy-start.3
  8.4 0.7 %copy-done.3 = s32[16,8]{0,1:T(8,128)S(1)} copy-done((s32[16,8]{0,1:T(8,128)S(1)}, s32[16,8]{0,1:T(8,128)}, u32[]{:S(2)}) %copy-start.3) | copy-done | bytes 536
  9.1 1.8 %stage.1 = (f32[64,192]{1,0:T(8,128)S(1)}, bf16[2,4,16,1152]{3,2,1,0:T(8,128)(2,1)S(1)}, bf16[2,4,16,1152]{3,2,1,0:T(8,128)(2,1)S(1)}, bf16[2,4,16,1152]{3,2,1,0:T(8,128)(2,1)S(1)}) custom-call(s32[1]{0:T(128)} %bitcast.index_ref, s32[8,16]{1,0:T(8,128)S(1)} %bitcast.2, bf16[2,4,16,1152]{3,2,1,0:T(8,128)(2,1)} %refs_0_.3, bf16[2,4,16,1152]{3,2,1,0:T(8,128)(2,1)} %refs_1_.1, ...), custom_call_target="tpu_custom_call" | custom-call | flops 1 | bytes 1 | tf_op jit(solution)/shard_map/stage/pallas_call | solution.py:160
  10.8 0.0 collective-permute-done.2.refs_3_.refs_1_
  10.9 1.7 %collective-permute-start.6 = (bf16[2,4,16,1152]{3,2,1,0:T(8,128)(2,1)S(1)}, bf16[2,4,16,1152]{3,2,1,0:T(8,128)(2,1)S(1)}, u32[]{:S(2)}, u32[]{:S(2)}) collective-permute-start(bf16[2,4,16,1152]{3,2,1,0:T(8,128)(2,1)S(1)} %get-tuple-element.17.refs_0_), channel_id=1, source_target_pairs={{0,2},{1,3},{2,0},{3,1},{4,6},{5,7},{6,4},{7,5},{8,10},{9,11},{10,... | collective-permute-start | bytes 884744 | tf_op jit(solution)/shard_map/ppermute | solution.py:41
  12.6 1.2 %collective-permute-done.refs_1_ = bf16[2,4,16,1152]{3,2,1,0:T(8,128)(2,1)S(1)} collective-permute-done((bf16[2,4,16,1152]{3,2,1,0:T(8,128)(2,1)}, bf16[2,4,16,1152]{3,2,1,0:T(8,128)(2,1)S(1)}, u32[]{:S(2)}, u32[]{:S(2)}) %collective-permute-start) | collective-permute-done | bytes 294944 | tf_op jit(solution)/shard_map/ppermute | solution.py:37
  13.8 0.0 collective-permute-done.1.refs_2_
  13.8 0.0 copy-start
  13.8 1.0 %spatial_weigh.1 = (bf16[2,16,64,192]{3,2,1,0:T(8,128)(2,1)S(1)}, f32[2,64,1152]{2,1,0:T(8,128)S(1)}) custom-call(f32[64,192]{1,0:T(8,128)S(1)} %get-tuple-element.10.bias_ref, bf16[2,4,16,1152]{3,2,1,0:T(8,128)(2,1)S(1)} %get-tuple-element.11.q_ref, bf16[2,4,16,1152]{3,2,1,0:T(8,128)(2,1)S(1)} %get-tuple-element.12.refs_0_, ...), custom_call_target="tpu_custom_call" | custom-call | flops 1 | bytes 1 | tf_op jit(solution)/shard_map/spatial_weigh/pallas_call | solution.py:272
  14.8 0.0 copy-done
  14.8 0.0 copy-start.1
  14.9 0.1 collective-permute-start.5
  14.9 3.7 %collective-permute-done.3.refs_1_.refs_3_ = bf16[2,4,16,1152]{3,2,1,0:T(8,128)(2,1)S(1)} collective-permute-done((bf16[2,4,16,1152]{3,2,1,0:T(8,128)(2,1)}, bf16[2,4,16,1152]{3,2,1,0:T(8,128)(2,1)S(1)}, u32[]{:S(2)}, u32[]{:S(2)}) %collective-permute-start.3) | collective-permute-done | bytes 294944 | tf_op jit(solution)/shard_map/ppermute | solution.py:37
  18.6 0.0 collective-permute-done.4.refs_2_.refs_4_
  18.6 1.7 %collective-permute-done.6.refs_1_ = bf16[2,4,16,1152]{3,2,1,0:T(8,128)(2,1)S(1)} collective-permute-done((bf16[2,4,16,1152]{3,2,1,0:T(8,128)(2,1)S(1)}, bf16[2,4,16,1152]{3,2,1,0:T(8,128)(2,1)S(1)}, u32[]{:S(2)}, u32[]{:S(2)}) %collective-permute-start.6) | collective-permute-done | bytes 294944 | tf_op jit(solution)/shard_map/ppermute | solution.py:41
  20.4 0.1 collective-permute-start.7
  20.5 0.0 copy-done.1
  20.5 0.0 copy-start.2
  20.5 0.4 %spatial_blend.1.spatial_ref = bf16[2,4,16,1152]{3,2,1,0:T(8,128)(2,1)S(1)} custom-call(bf16[2,16,64,192]{3,2,1,0:T(8,128)(2,1)S(1)} %get-tuple-element.13.weights_ref.refs_2_, f32[2,64,1152]{2,1,0:T(8,128)S(1)} %get-tuple-element.14.inverse_ref, bf16[2,4,16,1152]{3,2,1,0:T(8,128)(2,1)S(1)} %copy-done.1, ...), custom_call_target="tpu_custom_call" | custom-call | flops 1 | bytes 1 | tf_op jit(solution)/shard_map/spatial_blend/pallas_call | solution.py:272
  20.9 0.0 collective-permute-done.5.refs_1_
  20.9 0.5 %copy-done.2 = bf16[2,4,16,1152]{3,2,1,0:T(8,128)(2,1)S(1)} copy-done((bf16[2,4,16,1152]{3,2,1,0:T(8,128)(2,1)S(1)}, bf16[2,4,16,1152]{3,2,1,0:T(8,128)(2,1)}, u32[]{:S(2)}) %copy-start.2) | copy-done | bytes 294936
  21.4 0.8 %temporal_weigh.1 = (bf16[4,16,32,128]{3,2,1,0:T(8,128)(2,1)S(1)}, f32[4,32,1152]{2,1,0:T(8,128)S(1)}) custom-call(bf16[2,4,16,1152]{3,2,1,0:T(8,128)(2,1)S(1)} %copy-done.2, bf16[4,4,16,1152]{3,2,1,0:T(8,128)(2,1)S(1)} %join.2.refs_0_, bf16[4,4,16,1152]{3,2,1,0:T(8,128)(2,1)S(1)} %collective-permute-done.5.refs_1_), custom_call_target="tpu_custom_call" | custom-call | flops 1 | bytes 1 | tf_op jit(solution)/shard_map/temporal_weigh/pallas_call | solution.py:272
  22.3 0.2 collective-permute-done.7.refs_1_
  22.4 1.1 %last.1 = (bf16[2,4,16,1152]{3,2,1,0:T(8,128)(2,1)}, bf16[2,4,16,1152]{3,2,1,0:T(8,128)(2,1)}) custom-call(bf16[2,4,16,1152]{3,2,1,0:T(8,128)(2,1)S(1)} %spatial_blend.1.spatial_ref, bf16[4,16,32,128]{3,2,1,0:T(8,128)(2,1)S(1)} %get-tuple-element.15.weights_ref, f32[4,32,1152]{2,1,0:T(8,128)S(1)} %get-tuple-element.16.inverse_ref, ...), custom_call_target="tpu_custom_call" | custom-call | flops 1 | bytes 1 | tf_op jit(solution)/shard_map/last/pallas_call | solution.py:272
  (2 shorter events, 0.1 us)
Async XLA Ops:
  0.6 10.2 %collective-permute-start.2 = (bf16[2,4,16,1152]{3,2,1,0:T(8,128)(2,1)}, bf16[2,4,16,1152]{3,2,1,0:T(8,128)(2,1)S(1)}, u32[]{:S(2)}, u32[]{:S(2)}) collective-permute-start(bf16[2,4,16,1152]{3,2,1,0:T(8,128)(2,1)} %refs_0_.5), channel_id=1, source_target_pairs={{0,2},{1,3},{2,0},{3,1},{4,6},{5,7},{6,4},{7,5},{8,10},{9,11},{10,... | collective-permute-start | bytes 884744 | tf_op jit(solution)/shard_map/ppermute | solution.py:41
  3.6 10.1 %collective-permute-start = (bf16[2,4,16,1152]{3,2,1,0:T(8,128)(2,1)}, bf16[2,4,16,1152]{3,2,1,0:T(8,128)(2,1)S(1)}, u32[]{:S(2)}, u32[]{:S(2)}) collective-permute-start(bf16[2,4,16,1152]{3,2,1,0:T(8,128)(2,1)} %refs_1_.1), channel_id=1, source_target_pairs={{0,4},{1,5},{2,6},{3,7},{4,0},{5,1},{6,2},{7,3},{8,12},{9,13},{10,... | collective-permute-start | bytes 884744 | tf_op jit(solution)/shard_map/ppermute | solution.py:37
  5.2 8.6 %collective-permute-start.1 = (bf16[2,4,16,1152]{3,2,1,0:T(8,128)(2,1)}, bf16[2,4,16,1152]{3,2,1,0:T(8,128)(2,1)S(1)}, u32[]{:S(2)}, u32[]{:S(2)}) collective-permute-start(bf16[2,4,16,1152]{3,2,1,0:T(8,128)(2,1)} %refs_1_.1), channel_id=1, source_target_pairs={{0,1},{1,0},{2,3},{3,2},{4,8},{5,9},{6,10},{7,11},{8,4},{9,5},{10,... | collective-permute-start | bytes 884744 | tf_op jit(solution)/shard_map/ppermute | solution.py:37
  5.2 13.4 %collective-permute-start.3 = (bf16[2,4,16,1152]{3,2,1,0:T(8,128)(2,1)}, bf16[2,4,16,1152]{3,2,1,0:T(8,128)(2,1)S(1)}, u32[]{:S(2)}, u32[]{:S(2)}) collective-permute-start(bf16[2,4,16,1152]{3,2,1,0:T(8,128)(2,1)} %refs_0_.4), channel_id=1, source_target_pairs={{0,4},{1,5},{2,6},{3,7},{4,0},{5,1},{6,2},{7,3},{8,12},{9,13},{10,... | collective-permute-start | bytes 884744 | tf_op jit(solution)/shard_map/ppermute | solution.py:37
  8.4 10.3 %collective-permute-start.4 = (bf16[2,4,16,1152]{3,2,1,0:T(8,128)(2,1)}, bf16[2,4,16,1152]{3,2,1,0:T(8,128)(2,1)S(1)}, u32[]{:S(2)}, u32[]{:S(2)}) collective-permute-start(bf16[2,4,16,1152]{3,2,1,0:T(8,128)(2,1)} %refs_0_.4), channel_id=1, source_target_pairs={{0,1},{1,0},{2,3},{3,2},{4,8},{5,9},{6,10},{7,11},{8,4},{9,5},{10,... | collective-permute-start | bytes 884744 | tf_op jit(solution)/shard_map/ppermute | solution.py:37
  8.4 0.7 %copy-start.3 = (s32[16,8]{0,1:T(8,128)S(1)}, s32[16,8]{0,1:T(8,128)}, u32[]{:S(2)}) copy-start(s32[16,8]{0,1:T(8,128)} %param.13) | copy-start | bytes 1540
  10.9 9.5 %collective-permute-start.6 = (bf16[2,4,16,1152]{3,2,1,0:T(8,128)(2,1)S(1)}, bf16[2,4,16,1152]{3,2,1,0:T(8,128)(2,1)S(1)}, u32[]{:S(2)}, u32[]{:S(2)}) collective-permute-start(bf16[2,4,16,1152]{3,2,1,0:T(8,128)(2,1)S(1)} %get-tuple-element.17.refs_0_), channel_id=1, source_target_pairs={{0,2},{1,3},{2,0},{3,1},{4,6},{5,7},{6,4},{7,5},{8,10},{9,11},{10,... | collective-permute-start | bytes 884744 | tf_op jit(solution)/shard_map/ppermute | solution.py:41
  13.8 1.0 %copy-start = (bf16[2,4,16,1152]{3,2,1,0:T(8,128)(2,1)S(1)}, bf16[2,4,16,1152]{3,2,1,0:T(8,128)(2,1)}, u32[]{:S(2)}) copy-start(bf16[2,4,16,1152]{3,2,1,0:T(8,128)(2,1)} %refs_0_.5) | copy-start | bytes 884740
  14.8 5.6 %copy-start.1 = (bf16[2,4,16,1152]{3,2,1,0:T(8,128)(2,1)S(1)}, bf16[2,4,16,1152]{3,2,1,0:T(8,128)(2,1)}, u32[]{:S(2)}) copy-start(bf16[2,4,16,1152]{3,2,1,0:T(8,128)(2,1)} %refs_0_.4) | copy-start | bytes 884740
  14.9 6.1 %collective-permute-start.5 = (bf16[4,4,16,1152]{3,2,1,0:T(8,128)(2,1)S(1)}, bf16[4,4,16,1152]{3,2,1,0:T(8,128)(2,1)S(1)}, u32[]{:S(2)}, u32[]{:S(2)}) collective-permute-start(bf16[4,4,16,1152]{3,2,1,0:T(8,128)(2,1)S(1)} %join.2.refs_0_), channel_id=1, source_target_pairs={{0,1},{1,0},{2,3},{3,2},{4,5},{5,4},{6,7},{7,6},{8,9},{9,8},{10,11... | collective-permute-start | bytes 1769480 | tf_op jit(solution)/shard_map/ppermute | solution.py:41
  20.4 2.1 %collective-permute-start.7 = (bf16[4,4,16,1152]{3,2,1,0:T(8,128)(2,1)S(1)}, bf16[4,4,16,1152]{3,2,1,0:T(8,128)(2,1)S(1)}, u32[]{:S(2)}, u32[]{:S(2)}) collective-permute-start(bf16[4,4,16,1152]{3,2,1,0:T(8,128)(2,1)S(1)} %join.3.refs_0_), channel_id=1, source_target_pairs={{0,1},{1,0},{2,3},{3,2},{4,5},{5,4},{6,7},{7,6},{8,9},{9,8},{10,11... | collective-permute-start | bytes 1769480 | tf_op jit(solution)/shard_map/ppermute | solution.py:41
  20.5 1.0 %copy-start.2 = (bf16[2,4,16,1152]{3,2,1,0:T(8,128)(2,1)S(1)}, bf16[2,4,16,1152]{3,2,1,0:T(8,128)(2,1)}, u32[]{:S(2)}) copy-start(bf16[2,4,16,1152]{3,2,1,0:T(8,128)(2,1)} %q_ref.1) | copy-start | bytes 884740

commit v14 on v13

--- a/solution.py
+++ b/solution.py
@@ -164,7 +164,7 @@
         + [pl.BlockSpec(memory_space=pl.ANY)] * len(arrays),
         out_specs=(in_vmem,) * (1 + len(arrays)),
         scratch_shapes=[pltpu.SemaphoreType.DMA((len(arrays),))],
-        compiler_params=pltpu.CompilerParams(vmem_limit_bytes=53 * 1024 * 1024),
+        compiler_params=pltpu.CompilerParams(vmem_limit_bytes=53*1024*1024),
         cost_estimate=pl.CostEstimate(flops=1, bytes_accessed=1, transcendentals=0),
         name="stage",
     )(index, lists, *arrays)
@@ -323,8 +323,8 @@
 
     exchanges = [(d, parity) for d in range(1, reach + 1) for parity in (0, 1)]
     blocks = 1 + len(exchanges)
-    bias, own_q, own_k, own_tv = staged(
-        [spatial_q, spatial_k, temporal_v], index, key_lists.T, blocks, space
+    bias, own_q, own_k, own_v = staged(
+        [spatial_q, spatial_k, spatial_v], index, key_lists.T, blocks, space
     )
 
     def gathered(own, received, others):
@@ -336,10 +336,10 @@
         return held
 
     received_keys = swapped(temporal_k, "tm", first_step)
-    received_values = swapped(own_tv, "tm", first_step)
+    received_values = swapped(temporal_v, "tm", first_step)
     spatial_keys = [own_k] + [exchanged(spatial_k, *which) for which in exchanges]
-    spatial_values = [spatial_v] + [
-        exchanged(spatial_v, *which) for which in exchanges
+    spatial_values = [own_v] + [
+        exchanged(own_v if which[1] == 0 else spatial_v, *which) for which in exchanges
     ]
 
     keys = blocks * rows * columns
@@ -363,14 +363,14 @@
         [temporal_q, *temporal_keys],
         1,
     )
-    temporal_values = gathered(own_tv, received_values, [spatial_weights, *spatial_values[1:]])
+    temporal_values = gathered(temporal_v, received_values, [spatial_weights])
     spatial_result = call(
         functools.partial(spatial_blend_kernel, len(spatial_values)),
         "spatial_blend",
         out_shape,
         [],
         [spatial_weights, spatial_inverse, *spatial_values],
-        1,
+        10**11,
     )
     return call(
         functools.partial(last_kernel, len(temporal_values)),

time: 23.8 us -> 21.8 us (0.916)
  starting transfers between devices: 9.62 us -> 8.48 us
  waiting for transfers between devices: 6.78 us -> 5.91 us
    ppermute x4, waiting for transfers between devices: 4.89 us -> 3.1 us  [exchanged(): return lax.ppermute(value, AXES, pairs)]
    ppermute x4, starting transfers between devices: 4.88 us -> 3.68 us  [swapped(): lax.ppermute(value, axis, [(i, i ^ step) for i in range(lax.axis_size(axi...]
    ppermute x4, waiting for transfers between devices: 1.89 us -> 2.82 us  [swapped(): lax.ppermute(value, axis, [(i, i ^ step) for i in range(lax.axis_size(axi...]
    unnamed x8 -> x10, local copies, waits for them, and re-layouts: 1.2 us -> 1.2 us
  transfers between devices with their start and end apart: 8 -> 8, of which waited for: 4 -> 4; matrix products, arithmetic and copies ran while one was open for 0% -> 0% of each run, Pallas kernels for 17% -> 19%
where the time goes in v14:
time: 21.8 us; the launch traced here: 21.6 us
  starting transfers between devices  8.48 us (39%)
  waiting for transfers between devices  5.91 us (27%)
  Pallas kernels  5.24 us (24%)
  local copies, waits for them, and re-layouts  1.2 us (6%)
  between operations  0.73 us (3%)
    ppermute x4, starting transfers between devices, exchanged(): return lax.ppermute(value, AXES, pairs)  4.8 us
    ppermute x4, starting transfers between devices, swapped(): lax.ppermute(value, axis, [(i, i ^ step) for i in range(lax.axis_size(axi...  3.68 us
    pallas_call x6, Pallas kernels, call(): pl.pallas_call(kernel, out_shape=out_shape, in_specs=[in_smem] * len(scal...  3.47 us
    ppermute x4, waiting for transfers between devices, exchanged(): return lax.ppermute(value, AXES, pairs)  3.1 us
    ppermute x4, waiting for transfers between devices, swapped(): lax.ppermute(value, axis, [(i, i ^ step) for i in range(lax.axis_size(axi...  2.82 us
    pallas_call x1, Pallas kernels, staged(): pl.pallas_call(functools.partial(stage_kernel, blocks, space), out_shape=...  1.77 us
    unnamed x10, local copies, waits for them, and re-layouts  1.2 us
  transfers between devices with their start and end apart: 8, of which 4 were waited for; matrix products, arithmetic and copies ran while one was open for 0% of the time, Pallas kernels for 19%

profile of v14, /device:TPU:0, one launch (start us, length us, event | category | flops | bytes accessed | tf_op | source)
XLA Modules:
  0.0 21.6 jit_solution(10593902981806654767)
XLA Ops:
  0.6 3.0 %collective-permute-start.2 = (bf16[2,4,16,1152]{3,2,1,0:T(8,128)(2,1)}, bf16[2,4,16,1152]{3,2,1,0:T(8,128)(2,1)S(1)}, u32[]{:S(2)}, u32[]{:S(2)}) collective-permute-start(bf16[2,4,16,1152]{3,2,1,0:T(8,128)(2,1)} %refs_0_.4), channel_id=1, source_target_pairs={{0,2},{1,3},{2,0},{3,1},{4,6},{5,7},{6,4},{7,5},{8,10},{9,11},{10,... | collective-permute-start | bytes 884744 | tf_op jit(solution)/shard_map/ppermute | solution.py:41
  3.6 1.6 %collective-permute-start = (bf16[2,4,16,1152]{3,2,1,0:T(8,128)(2,1)}, bf16[2,4,16,1152]{3,2,1,0:T(8,128)(2,1)S(1)}, u32[]{:S(2)}, u32[]{:S(2)}) collective-permute-start(bf16[2,4,16,1152]{3,2,1,0:T(8,128)(2,1)} %refs_1_.1), channel_id=1, source_target_pairs={{0,4},{1,5},{2,6},{3,7},{4,0},{5,1},{6,2},{7,3},{8,12},{9,13},{10,... | collective-permute-start | bytes 884744 | tf_op jit(solution)/shard_map/ppermute | solution.py:37
  5.2 0.0 collective-permute-start.1
  5.2 0.5 %collective-permute-start.6 = (bf16[2,4,16,1152]{3,2,1,0:T(8,128)(2,1)}, bf16[2,4,16,1152]{3,2,1,0:T(8,128)(2,1)S(1)}, u32[]{:S(2)}, u32[]{:S(2)}) collective-permute-start(bf16[2,4,16,1152]{3,2,1,0:T(8,128)(2,1)} %refs_0_.5), channel_id=1, source_target_pairs={{0,2},{1,3},{2,0},{3,1},{4,6},{5,7},{6,4},{7,5},{8,10},{9,11},{10,... | collective-permute-start | bytes 884744 | tf_op jit(solution)/shard_map/ppermute | solution.py:41
  5.7 0.0 copy-start.3
  5.8 0.7 %copy-done.3 = s32[16,8]{0,1:T(8,128)S(1)} copy-done((s32[16,8]{0,1:T(8,128)S(1)}, s32[16,8]{0,1:T(8,128)}, u32[]{:S(2)}) %copy-start.3) | copy-done | bytes 536
  6.4 0.0 copy-start.4
  6.4 1.8 %stage.1 = (f32[64,192]{1,0:T(8,128)S(1)}, bf16[2,4,16,1152]{3,2,1,0:T(8,128)(2,1)S(1)}, bf16[2,4,16,1152]{3,2,1,0:T(8,128)(2,1)S(1)}, bf16[2,4,16,1152]{3,2,1,0:T(8,128)(2,1)S(1)}) custom-call(s32[1]{0:T(128)} %bitcast.index_ref, s32[8,16]{1,0:T(8,128)S(1)} %bitcast.2, bf16[2,4,16,1152]{3,2,1,0:T(8,128)(2,1)} %refs_0_.3, bf16[2,4,16,1152]{3,2,1,0:T(8,128)(2,1)} %refs_1_.1, ...), custom_call_target="tpu_custom_call" | custom-call | flops 1 | bytes 1 | tf_op jit(solution)/shard_map/stage/pallas_call | solution.py:160
  8.2 3.2 %collective-permute-start.3 = (bf16[2,4,16,1152]{3,2,1,0:T(8,128)(2,1)S(1)}, bf16[2,4,16,1152]{3,2,1,0:T(8,128)(2,1)S(1)}, u32[]{:S(2)}, u32[]{:S(2)}) collective-permute-start(bf16[2,4,16,1152]{3,2,1,0:T(8,128)(2,1)S(1)} %get-tuple-element.15.refs_0_), channel_id=1, source_target_pairs={{0,4},{1,5},{2,6},{3,7},{4,0},{5,1},{6,2},{7,3},{8,12},{9,13},{10,... | collective-permute-start | bytes 884744 | tf_op jit(solution)/shard_map/ppermute | solution.py:37
  11.4 0.2 %collective-permute-done.2.refs_3_.refs_1_ = bf16[2,4,16,1152]{3,2,1,0:T(8,128)(2,1)S(1)} collective-permute-done((bf16[2,4,16,1152]{3,2,1,0:T(8,128)(2,1)}, bf16[2,4,16,1152]{3,2,1,0:T(8,128)(2,1)S(1)}, u32[]{:S(2)}, u32[]{:S(2)}) %collective-permute-start.2) | collective-permute-done | bytes 294944 | tf_op jit(solution)/shard_map/ppermute | solution.py:41
  11.7 0.0 copy-done.4
  11.7 0.0 collective-permute-start.4
  11.7 1.8 %collective-permute-done.refs_1_ = bf16[2,4,16,1152]{3,2,1,0:T(8,128)(2,1)S(1)} collective-permute-done((bf16[2,4,16,1152]{3,2,1,0:T(8,128)(2,1)}, bf16[2,4,16,1152]{3,2,1,0:T(8,128)(2,1)S(1)}, u32[]{:S(2)}, u32[]{:S(2)}) %collective-permute-start) | collective-permute-done | bytes 294944 | tf_op jit(solution)/shard_map/ppermute | solution.py:37
  13.5 0.0 collective-permute-done.1.refs_2_
  13.5 0.0 copy-start
  13.5 1.0 %spatial_weigh.1 = (bf16[2,16,64,192]{3,2,1,0:T(8,128)(2,1)S(1)}, f32[2,64,1152]{2,1,0:T(8,128)S(1)}) custom-call(f32[64,192]{1,0:T(8,128)S(1)} %get-tuple-element.10.bias_ref, bf16[2,4,16,1152]{3,2,1,0:T(8,128)(2,1)S(1)} %get-tuple-element.11.q_ref, bf16[2,4,16,1152]{3,2,1,0:T(8,128)(2,1)S(1)} %get-tuple-element.12.refs_0_, ...), custom_call_target="tpu_custom_call" | custom-call | flops 1 | bytes 1 | tf_op jit(solution)/shard_map/spatial_weigh/pallas_call | solution.py:272
  14.5 0.0 copy-done
  14.5 0.0 copy-start.1
  14.5 0.1 collective-permute-start.5
  14.6 2.6 %collective-permute-done.6.refs_1_ = bf16[2,4,16,1152]{3,2,1,0:T(8,128)(2,1)S(1)} collective-permute-done((bf16[2,4,16,1152]{3,2,1,0:T(8,128)(2,1)}, bf16[2,4,16,1152]{3,2,1,0:T(8,128)(2,1)S(1)}, u32[]{:S(2)}, u32[]{:S(2)}) %collective-permute-start.6) | collective-permute-done | bytes 294944 | tf_op jit(solution)/shard_map/ppermute | solution.py:41
  17.2 0.0 copy-done.1
  17.2 0.1 collective-permute-start.7
  17.3 1.3 %collective-permute-done.3.refs_1_ = bf16[2,4,16,1152]{3,2,1,0:T(8,128)(2,1)S(1)} collective-permute-done((bf16[2,4,16,1152]{3,2,1,0:T(8,128)(2,1)S(1)}, bf16[2,4,16,1152]{3,2,1,0:T(8,128)(2,1)S(1)}, u32[]{:S(2)}, u32[]{:S(2)}) %collective-permute-start.3) | collective-permute-done | bytes 294944 | tf_op jit(solution)/shard_map/ppermute | solution.py:37
  18.6 0.0 collective-permute-done.4.refs_2_
  18.6 0.0 copy-start.2
  18.6 0.4 %spatial_blend.1.spatial_ref = bf16[2,4,16,1152]{3,2,1,0:T(8,128)(2,1)S(1)} custom-call(bf16[2,16,64,192]{3,2,1,0:T(8,128)(2,1)S(1)} %get-tuple-element.13.weights_ref.refs_2_, f32[2,64,1152]{2,1,0:T(8,128)S(1)} %get-tuple-element.14.inverse_ref, bf16[2,4,16,1152]{3,2,1,0:T(8,128)(2,1)S(1)} %get-tuple-element.15.refs_0_, ...), custom_call_target="tpu_custom_call" | custom-call | flops 99999997952 | bytes 1 | tf_op jit(solution)/shard_map/spatial_blend/pallas_call | solution.py:272
  19.1 0.0 collective-permute-done.5.refs_1_
  19.1 0.5 %copy-done.2 = bf16[2,4,16,1152]{3,2,1,0:T(8,128)(2,1)S(1)} copy-done((bf16[2,4,16,1152]{3,2,1,0:T(8,128)(2,1)S(1)}, bf16[2,4,16,1152]{3,2,1,0:T(8,128)(2,1)}, u32[]{:S(2)}) %copy-start.2) | copy-done | bytes 294936
  19.6 0.8 %temporal_weigh.1 = (bf16[4,16,32,128]{3,2,1,0:T(8,128)(2,1)S(1)}, f32[4,32,1152]{2,1,0:T(8,128)S(1)}) custom-call(bf16[2,4,16,1152]{3,2,1,0:T(8,128)(2,1)S(1)} %copy-done.2, bf16[4,4,16,1152]{3,2,1,0:T(8,128)(2,1)S(1)} %join.2.refs_0_, bf16[4,4,16,1152]{3,2,1,0:T(8,128)(2,1)S(1)} %collective-permute-done.5.refs_1_), custom_call_target="tpu_custom_call" | custom-call | flops 1 | bytes 1 | tf_op jit(solution)/shard_map/temporal_weigh/pallas_call | solution.py:272
  20.4 0.0 collective-permute-done.7.refs_1_
  20.5 1.1 %last.1 = (bf16[2,4,16,1152]{3,2,1,0:T(8,128)(2,1)}, bf16[2,4,16,1152]{3,2,1,0:T(8,128)(2,1)}) custom-call(bf16[2,4,16,1152]{3,2,1,0:T(8,128)(2,1)S(1)} %spatial_blend.1.spatial_ref, bf16[4,16,32,128]{3,2,1,0:T(8,128)(2,1)S(1)} %get-tuple-element.16.weights_ref, f32[4,32,1152]{2,1,0:T(8,128)S(1)} %get-tuple-element.17.inverse_ref, ...), custom_call_target="tpu_custom_call" | custom-call | flops 1 | bytes 1 | tf_op jit(solution)/shard_map/last/pallas_call | solution.py:272
  (2 shorter events, 0.1 us)
Async XLA Ops:
  0.6 11.1 %collective-permute-start.2 = (bf16[2,4,16,1152]{3,2,1,0:T(8,128)(2,1)}, bf16[2,4,16,1152]{3,2,1,0:T(8,128)(2,1)S(1)}, u32[]{:S(2)}, u32[]{:S(2)}) collective-permute-start(bf16[2,4,16,1152]{3,2,1,0:T(8,128)(2,1)} %refs_0_.4), channel_id=1, source_target_pairs={{0,2},{1,3},{2,0},{3,1},{4,6},{5,7},{6,4},{7,5},{8,10},{9,11},{10,... | collective-permute-start | bytes 884744 | tf_op jit(solution)/shard_map/ppermute | solution.py:41
  3.6 9.8 %collective-permute-start = (bf16[2,4,16,1152]{3,2,1,0:T(8,128)(2,1)}, bf16[2,4,16,1152]{3,2,1,0:T(8,128)(2,1)S(1)}, u32[]{:S(2)}, u32[]{:S(2)}) collective-permute-start(bf16[2,4,16,1152]{3,2,1,0:T(8,128)(2,1)} %refs_1_.1), channel_id=1, source_target_pairs={{0,4},{1,5},{2,6},{3,7},{4,0},{5,1},{6,2},{7,3},{8,12},{9,13},{10,... | collective-permute-start | bytes 884744 | tf_op jit(solution)/shard_map/ppermute | solution.py:37
  5.2 8.2 %collective-permute-start.1 = (bf16[2,4,16,1152]{3,2,1,0:T(8,128)(2,1)}, bf16[2,4,16,1152]{3,2,1,0:T(8,128)(2,1)S(1)}, u32[]{:S(2)}, u32[]{:S(2)}) collective-permute-start(bf16[2,4,16,1152]{3,2,1,0:T(8,128)(2,1)} %refs_1_.1), channel_id=1, source_target_pairs={{0,1},{1,0},{2,3},{3,2},{4,8},{5,9},{6,10},{7,11},{8,4},{9,5},{10,... | collective-permute-start | bytes 884744 | tf_op jit(solution)/shard_map/ppermute | solution.py:37
  5.2 12.0 %collective-permute-start.6 = (bf16[2,4,16,1152]{3,2,1,0:T(8,128)(2,1)}, bf16[2,4,16,1152]{3,2,1,0:T(8,128)(2,1)S(1)}, u32[]{:S(2)}, u32[]{:S(2)}) collective-permute-start(bf16[2,4,16,1152]{3,2,1,0:T(8,128)(2,1)} %refs_0_.5), channel_id=1, source_target_pairs={{0,2},{1,3},{2,0},{3,1},{4,6},{5,7},{6,4},{7,5},{8,10},{9,11},{10,... | collective-permute-start | bytes 884744 | tf_op jit(solution)/shard_map/ppermute | solution.py:41
  5.7 0.7 %copy-start.3 = (s32[16,8]{0,1:T(8,128)S(1)}, s32[16,8]{0,1:T(8,128)}, u32[]{:S(2)}) copy-start(s32[16,8]{0,1:T(8,128)} %param.13) | copy-start | bytes 1540
  6.4 5.2 %copy-start.4 = (bf16[2,4,16,1152]{3,2,1,0:T(8,128)(2,1)S(1)}, bf16[2,4,16,1152]{3,2,1,0:T(8,128)(2,1)}, u32[]{:S(2)}) copy-start(bf16[2,4,16,1152]{3,2,1,0:T(8,128)(2,1)} %refs_2_.1) | copy-start | bytes 884740
  8.2 10.4 %collective-permute-start.3 = (bf16[2,4,16,1152]{3,2,1,0:T(8,128)(2,1)S(1)}, bf16[2,4,16,1152]{3,2,1,0:T(8,128)(2,1)S(1)}, u32[]{:S(2)}, u32[]{:S(2)}) collective-permute-start(bf16[2,4,16,1152]{3,2,1,0:T(8,128)(2,1)S(1)} %get-tuple-element.15.refs_0_), channel_id=1, source_target_pairs={{0,4},{1,5},{2,6},{3,7},{4,0},{5,1},{6,2},{7,3},{8,12},{9,13},{10,... | collective-permute-start | bytes 884744 | tf_op jit(solution)/shard_map/ppermute | solution.py:37
  11.7 7.0 %collective-permute-start.4 = (bf16[2,4,16,1152]{3,2,1,0:T(8,128)(2,1)S(1)}, bf16[2,4,16,1152]{3,2,1,0:T(8,128)(2,1)S(1)}, u32[]{:S(2)}, u32[]{:S(2)}) collective-permute-start(bf16[2,4,16,1152]{3,2,1,0:T(8,128)(2,1)S(1)} %copy-done.4), channel_id=1, source_target_pairs={{0,1},{1,0},{2,3},{3,2},{4,8},{5,9},{6,10},{7,11},{8,4},{9,5},{10,... | collective-permute-start | bytes 884744 | tf_op jit(solution)/shard_map/ppermute | solution.py:37
  13.5 1.0 %copy-start = (bf16[2,4,16,1152]{3,2,1,0:T(8,128)(2,1)S(1)}, bf16[2,4,16,1152]{3,2,1,0:T(8,128)(2,1)}, u32[]{:S(2)}) copy-start(bf16[2,4,16,1152]{3,2,1,0:T(8,128)(2,1)} %refs_0_.4) | copy-start | bytes 884740
  14.5 2.7 %copy-start.1 = (bf16[2,4,16,1152]{3,2,1,0:T(8,128)(2,1)S(1)}, bf16[2,4,16,1152]{3,2,1,0:T(8,128)(2,1)}, u32[]{:S(2)}) copy-start(bf16[2,4,16,1152]{3,2,1,0:T(8,128)(2,1)} %refs_0_.5) | copy-start | bytes 884740
  14.5 4.6 %collective-permute-start.5 = (bf16[4,4,16,1152]{3,2,1,0:T(8,128)(2,1)S(1)}, bf16[4,4,16,1152]{3,2,1,0:T(8,128)(2,1)S(1)}, u32[]{:S(2)}, u32[]{:S(2)}) collective-permute-start(bf16[4,4,16,1152]{3,2,1,0:T(8,128)(2,1)S(1)} %join.2.refs_0_), channel_id=1, source_target_pairs={{0,1},{1,0},{2,3},{3,2},{4,5},{5,4},{6,7},{7,6},{8,9},{9,8},{10,11... | collective-permute-start | bytes 1769480 | tf_op jit(solution)/shard_map/ppermute | solution.py:41
  17.2 3.2 %collective-permute-start.7 = (bf16[4,4,16,1152]{3,2,1,0:T(8,128)(2,1)S(1)}, bf16[4,4,16,1152]{3,2,1,0:T(8,128)(2,1)S(1)}, u32[]{:S(2)}, u32[]{:S(2)}) collective-permute-start(bf16[4,4,16,1152]{3,2,1,0:T(8,128)(2,1)S(1)} %join.3.refs_0_), channel_id=1, source_target_pairs={{0,1},{1,0},{2,3},{3,2},{4,5},{5,4},{6,7},{7,6},{8,9},{9,8},{10,11... | collective-permute-start | bytes 1769480 | tf_op jit(solution)/shard_map/ppermute | solution.py:41
  18.6 1.0 %copy-start.2 = (bf16[2,4,16,1152]{3,2,1,0:T(8,128)(2,1)S(1)}, bf16[2,4,16,1152]{3,2,1,0:T(8,128)(2,1)}, u32[]{:S(2)}) copy-start(bf16[2,4,16,1152]{3,2,1,0:T(8,128)(2,1)} %q_ref.1) | copy-start | bytes 884740
